TPU v7x, 32 devices: a whole 2x2x4 slice. The times are simulated.
32 devices in a mesh: section: 2 (over x), expert: 8 (over z, core), dp: 2 (over y).
Axes of the slice: x: 2, y: 2, z: 4, core: 2. Of those that a mesh axis runs over, the one named last changes fastest.
Arguments:
- tokens: bfloat16 [2, 2048, 3584], P('section', ('expert', 'dp')), may hold values from -6 to 6
- grad_out: bfloat16 [2, 2048, 3584], P('section', ('expert', 'dp')), may hold values from -6 to 6
- expert_ids: int32 [2, 2048, 2], P('section', ('expert', 'dp')), may hold values from 0 to 3, all different within a row; in each aligned block of 128 rows (0 to 127, 128 to 255, ..., all dimensions but the last counted through in order) at most 65 rows name the same one
- gate_values: float32 [2, 2048, 2], P('section', ('expert', 'dp')), may hold values from 0.1 to 1
- w_in: bfloat16 [2, 8, 1792, 1024], P('section', 'expert', None, 'dp'), may hold values from -0.09375 to 0.09375
- w_out_t: bfloat16 [2, 8, 1792, 1024], P('section', 'expert', None, 'dp'), may hold values from -0.1875 to 0.1875
Outputs:
- handed_grad: bfloat16 [2, 2048, 3584], P('section', ('expert', 'dp'))
Inputs may be any that keep to these rules, and one draw needn't show every extreme that they name: `expert_ids`: each token names 2 different experts; in each aligned block of 128 tokens (the tokens of one device) no expert is named more than 65 times, a bound that some block reaches.
All inputs are finite; a program needn't handle non-finite values.
Results may differ from a plain program's by a relative error of at most 0.0051.
Values may be sent and summed in bfloat16 or wider, within the bound.
No kernel may reach another device: no remote copies, remote signals or barrier semaphores. Data moves between devices by JAX's collectives and lax.ppermute only.
A program may use at most 128 MiB of HBM per device.

v0:
```python
import jax
import jax.numpy as jnp
from jax import lax
from jax.sharding import PartitionSpec as P


def partner(value, axis, apart):
    mask = 2**apart
    pairs = [(source, source ^ mask) for source in range(lax.axis_size(axis))]
    return lax.ppermute(value, axis, pairs)


def slot_layout(ids, experts):
    flat_ids = ids.reshape(-1)
    onehot = (flat_ids[:, None] == jnp.arange(experts, dtype=jnp.int32)[None, :]).astype(jnp.int32)
    before = jnp.cumsum(onehot, axis=0) - onehot
    rank = jnp.sum(before * onehot, axis=1)
    return (flat_ids, rank)


def silu_slope(pre):
    sig = jax.nn.sigmoid(pre)
    return sig * (1.0 + pre * (1.0 - sig))


def body(tokens, grad_out, expert_ids, gate_values, w_in, w_out_t):
    tok_rows = tokens[0]
    grad_rows = grad_out[0]
    ids = expert_ids[0]
    gates = gate_values[0]
    tok_dev, width = tok_rows.shape
    top = ids.shape[1]
    half = width // 2
    n_expert = lax.axis_size("expert")
    experts = n_expert // 2
    capacity = min(tok_dev, max(2, tok_dev * top // experts + 1))
    w_in_full, w_out_full = (
        lax.all_gather(w_in[0, 0], "dp", axis=1, tiled=True),
        lax.all_gather(w_out_t[0, 0], "dp", axis=1, tiled=True),
    )
    flat_ids, rank = slot_layout(ids, experts)
    source = jnp.arange(tok_dev * top, dtype=jnp.int32) // top
    scaled = (gates.reshape(-1)[:, None] * grad_rows[source].astype(jnp.float32)).astype(
        jnp.bfloat16
    )
    empty = jnp.zeros((experts, 2, capacity, half), jnp.bfloat16)
    tok_send = empty.at[flat_ids, :, rank].set(tok_rows[source].reshape(-1, 2, half))
    grad_send = empty.at[flat_ids, :, rank].set(scaled.reshape(-1, 2, half))
    tok_send = tok_send.reshape(n_expert, capacity, half)
    grad_send = grad_send.reshape(n_expert, capacity, half)
    tok_in = lax.all_to_all(tok_send, "expert", split_axis=0, concat_axis=0, tiled=True)
    grad_in = lax.all_to_all(grad_send, "expert", split_axis=0, concat_axis=0, tiled=True)
    sources, slots, _ = tok_in.shape
    tok_flat = tok_in.reshape(sources * slots, half)
    grad_flat = grad_in.reshape(sources * slots, half)
    pre_part = jnp.dot(tok_flat, w_in_full, preferred_element_type=jnp.float32).astype(jnp.bfloat16)
    hid_part = jnp.dot(grad_flat, w_out_full, preferred_element_type=jnp.float32).astype(
        jnp.bfloat16
    )
    pre_other, hid_other = partner((pre_part, hid_part), "expert", 0)
    pre = pre_part.astype(jnp.float32) + pre_other.astype(jnp.float32)
    hidden = hid_part.astype(jnp.float32) + hid_other.astype(jnp.float32)
    act_grad = (hidden * silu_slope(pre)).astype(jnp.bfloat16)
    back = lax.dot_general(
        act_grad, w_in_full, (((1,), (1,)), ((), ())), preferred_element_type=jnp.float32
    )
    back = back.astype(jnp.bfloat16).reshape(sources, slots, half)
    returned = lax.all_to_all(back, "expert", split_axis=0, concat_axis=0, tiled=True)
    returned = returned.reshape(experts, 2, capacity, half)
    rows_back = returned[flat_ids, :, rank].reshape(tok_dev, top, width).astype(jnp.float32)
    expert_sum = jnp.sum(rows_back, axis=1)
    own_grad = (grad_rows.astype(jnp.float32) + expert_sum).astype(jnp.bfloat16)
    handed = partner(own_grad, "section", 0)
    return handed[None]


def solution(mesh):
    return jax.shard_map(
        body,
        mesh=mesh,
        in_specs=(
            P("section", ("expert", "dp"), None),
            P("section", ("expert", "dp"), None),
            P("section", ("expert", "dp"), None),
            P("section", ("expert", "dp"), None),
            P("section", "expert", None, "dp"),
            P("section", "expert", None, "dp"),
        ),
        out_specs=P("section", ("expert", "dp"), None),
        check_vma=False,
    )
```

profile of v0, /device:TPU:0, one launch (start us, length us, event | category | flops | bytes accessed | tf_op | source)
XLA Modules:
  0.0 299.8 jit_solution(8298143375998179354)
XLA Ops:
  6.5 0.0 copy-start
  6.5 0.0 all-gather.7.cloned.1.call-start
  6.5 0.7 all-gather.7.cloned.1.call-update
  7.3 0.8 copy.31
  8.0 0.1 eq.29
  8.2 0.1 eq.25
  8.4 1.2 reduce-window.6
  9.6 0.1 slice.18
  9.7 0.1 copy.34
  9.8 0.1 copy.35
  9.9 0.1 add_bitcast_fusion
  10.0 0.1 reshape_squeeze.3
  10.1 0.0 copy-done
  10.2 1.7 gather_fusion.1
  11.9 1.5 reshape.175
  13.4 2.2 broadcast_in_dim.4.clone
  15.6 35.4 %scatter_fusion.1 = bf16[4,2,65,1792]{3,1,2,0:T(2,128)(2,1)} fusion(bf16[4,2,65,1792]{3,1,2,0:T(2,128)(2,1)} %broadcast_in_dim.4.clone, s32[256]{0:T(256)S(1)} %bitcast.48, bf16[256,2,1792]{2,1,0:T(2,128)(2,1)} %reshape.175), kind=kCustom, calls=%fused_computation.4 | custom fusion | bytes 5507072 | tf_op jit(solution)/shard_map/scatter | solution.py:47
  51.0 3.0 %copy.44 = bf16[4,2,65,1792]{3,2,1,0:T(8,128)(2,1)} copy(bf16[4,2,65,1792]{3,1,2,0:T(2,128)(2,1)} %scatter_fusion.1) | data formatting | bytes 3727360 | tf_op jit(solution)/shard_map/reshape | solution.py:49
  54.0 0.0 copy-start.1
  54.0 6.4 %all-to-all-start.1 = ((bf16[8,65,1792]{2,1,0:T(8,128)(2,1)}), bf16[8,65,1792]{2,1,0:T(8,128)(2,1)}, u32[]{:S(2)}, u32[]{:S(2)}) async-start(bf16[8,65,1792]{2,1,0:T(8,128)(2,1)} %bitcast.51), calls=%async_computation.1 | async-start | bytes 4128768 | tf_op jit(solution)/shard_map/all_to_all | solution.py:51
  60.4 0.0 copy-done.1
  60.4 3.0 %gather_fusion = bf16[256,3584]{1,0:T(8,128)(2,1)} fusion(bf16[128,3584]{1,0:T(8,128)(2,1)S(1)} %bitcast.47, s32[1024]{0:T(1024)S(1)} %pad_clamp_fusion), kind=kCustom, calls=%fused_computation | custom fusion | bytes 3671040 | tf_op jit(solution)/shard_map/gather | solution.py:43
  63.5 0.0 copy-start.2
  63.5 5.4 %reshape.143 = f32[256,2,1792]{2,1,0:T(2,128)} reshape(bf16[256,3584]{1,0:T(8,128)(2,1)} %gather_fusion) | data formatting | bytes 5505024 | tf_op jit(solution)/shard_map/convert_element_type | solution.py:43
  68.8 0.0 copy-done.2
  68.8 0.1 copy.36
  69.0 0.1 mul.24
  69.1 4.7 %multiply_convert_fusion = bf16[256,2,1792]{2,1,0:T(2,128)(2,1)} fusion(f32[256,2,1792]{2,1,0:T(2,128)} %reshape.143, f32[256]{0:T(256)S(1)} %mul.24), kind=kLoop, calls=%fused_computation.11 | loop fusion | flops 1835008 | bytes 5506048 | tf_op jit(solution)/shard_map/convert_element_type | solution.py:43
  73.8 2.2 broadcast_in_dim.4.clone.1
  76.0 35.2 %scatter_fusion = bf16[4,2,65,1792]{3,1,2,0:T(2,128)(2,1)} fusion(bf16[4,2,65,1792]{3,1,2,0:T(2,128)(2,1)} %broadcast_in_dim.4.clone.1, s32[256]{0:T(256)S(1)} %bitcast.49, bf16[256,2,1792]{2,1,0:T(2,128)(2,1)} %multiply_convert_fusion), kind=kCustom, calls=%fused_computation.3 | custom fusion | bytes 5507072 | tf_op jit(solution)/shard_map/scatter | solution.py:48
  111.2 3.1 %copy.43 = bf16[4,2,65,1792]{3,2,1,0:T(8,128)(2,1)} copy(bf16[4,2,65,1792]{3,1,2,0:T(2,128)(2,1)} %scatter_fusion) | data formatting | bytes 3727360 | tf_op jit(solution)/shard_map/reshape | solution.py:50
  114.3 0.0 all-to-all-done.1
  114.3 5.1 %all-to-all-start = ((bf16[8,65,1792]{2,1,0:T(8,128)(2,1)}), bf16[8,65,1792]{2,1,0:T(8,128)(2,1)}, u32[]{:S(2)}, u32[]{:S(2)}) async-start(bf16[8,65,1792]{2,1,0:T(8,128)(2,1)} %bitcast.52), calls=%async_computation | async-start | bytes 4128768 | tf_op jit(solution)/shard_map/all_to_all | solution.py:52
  119.4 0.2 all-gather.5.cloned.1.call-start
  119.6 0.5 all-gather.5.cloned.1.call-update
  120.1 3.4 %reshape.140 = bf16[520,1792]{1,0:T(8,128)(2,1)} reshape(bf16[8,65,1792]{2,1,0:T(8,128)(2,1)} %all-to-all-done.1) | data formatting | bytes 3727360 | tf_op jit(solution)/shard_map/reshape | solution.py:54
  123.5 44.3 %all-to-all-done = bf16[8,65,1792]{2,1,0:T(8,128)(2,1)} async-done(((bf16[8,65,1792]{2,1,0:T(8,128)(2,1)}), bf16[8,65,1792]{2,1,0:T(8,128)(2,1)}, u32[]{:S(2)}, u32[]{:S(2)}) %all-to-all-start) | async-done | bytes 1863712 | tf_op jit(solution)/shard_map/all_to_all | solution.py:52
  167.8 3.5 %reshape.137 = bf16[520,1792]{1,0:T(8,128)(2,1)} reshape(bf16[8,65,1792]{2,1,0:T(8,128)(2,1)} %all-to-all-done) | data formatting | bytes 3727360 | tf_op jit(solution)/shard_map/reshape | solution.py:55
  171.3 0.0 all-gather.7.cloned.1.call-done
  171.3 4.7 %fusion.12 = bf16[520,1024]{1,0:T(8,128)(2,1)S(1)} fusion(bf16[520,1792]{1,0:T(8,128)(2,1)} %reshape.140, bf16[1,1,1792,1024]{3,2,1,0:T(8,128)(2,1)} %all-gather.7.cloned.1.call-done), kind=kOutput, calls=%fused_computation.16 | convolution fusion | flops 1908940800 | bytes 6598656 | tf_op jit(solution)/shard_map/dot_general | solution.py:56
  176.0 0.1 collective-permute-start.1
  176.1 0.0 all-gather.5.cloned.1.call-done
  176.1 0.0 copy-start.3
  176.1 4.8 %fusion.9 = bf16[520,1024]{1,0:T(8,128)(2,1)S(1)} fusion(bf16[520,1792]{1,0:T(8,128)(2,1)} %reshape.137, bf16[1,1,1792,1024]{3,2,1,0:T(8,128)(2,1)} %all-gather.5.cloned.1.call-done), kind=kOutput, calls=%fused_computation.15 | convolution fusion | flops 1908940800 | bytes 6598656 | tf_op jit(solution)/shard_map/dot_general | solution.py:57
  181.0 0.5 collective-permute-start
  181.5 0.0 collective-permute-done.1
  181.5 2.3 collective-permute-done
  183.8 0.0 copy-done.3
  183.8 5.4 %fusion.6 = bf16[520,1792]{1,0:T(8,128)(2,1)} fusion(bf16[1,1,1792,1024]{3,2,1,0:T(8,128)(2,1)S(1)} %copy-done.3, bf16[520,1024]{1,0:T(8,128)(2,1)} %collective-permute-done.1, bf16[520,1024]{1,0:T(8,128)(2,1)S(1)} %fusion.12, bf16[520,1024]{1,0:T(8,128)(2,1)S(1)} %collective-permute-done, bf16[520,1024]{1,0:T(8,128)(2,1)S(1)} %fusion.9), kind=kOutput, calls=%fused_computation.12 | convolution fusion | flops 1917327360 | bytes 9793536 | tf_op jit(solution)/shard_map/dot_general | solution.py:64
  189.3 3.4 %reshape.141 = bf16[8,65,1792]{2,1,0:T(8,128)(2,1)} reshape(bf16[520,1792]{1,0:T(8,128)(2,1)} %fusion.6) | data formatting | bytes 3727360 | tf_op jit(solution)/shard_map/reshape | solution.py:67
  192.7 51.9 %all_to_all.15 = bf16[8,65,1792]{2,1,0:T(8,128)(2,1)S(1)} all-to-all(bf16[8,65,1792]{2,1,0:T(8,128)(2,1)} %reshape.141), channel_id=1, replica_groups=mesh['section'=2,'expert'=8,'dp'=2] {'expert'}, dimensions={0} | all-to-all | bytes 3727360 | tf_op jit(solution)/shard_map/all_to_all | solution.py:68
  244.6 2.7 copy.42
  247.3 7.3 %gather_fusion.2 = bf16[256,2,1792]{2,1,0:T(2,128)(2,1)} fusion(bf16[4,2,65,1792]{3,1,2,0:T(2,128)(2,1)} %copy.42, s32[256]{0:T(256)S(1)} %bitcast.50), kind=kCustom, calls=%fused_computation.2 | custom fusion | bytes 3672064 | tf_op jit(solution)/shard_map/gather | solution.py:70
  254.5 6.3 %reshape.144 = f32[128,2,3584]{2,1,0:T(2,128)} reshape(bf16[256,2,1792]{2,1,0:T(2,128)(2,1)} %gather_fusion.2) | data formatting | bytes 5505024 | tf_op jit(solution)/shard_map/convert_element_type | solution.py:70
  260.9 7.6 %reduce_sum.22 = f32[128,3584]{1,0:T(8,128)} reduce(f32[128,2,3584]{2,1,0:T(2,128)} %reshape.144, f32[]{:T(128)} %constant.33.clone.1), dimensions={1}, to_apply=%region_5.6 | reduce | flops 458752 | bytes 5505028 | tf_op jit(solution)/shard_map/reduce_sum | solution.py:71
  268.5 1.7 add_convert_fusion
  270.2 1.6 collective-permute-start.2
  271.8 20.3 %collective-permute-done.2 = bf16[128,3584]{1,0:T(8,128)(2,1)S(1)} collective-permute-done((bf16[128,3584]{1,0:T(8,128)(2,1)S(1)}, bf16[128,3584]{1,0:T(8,128)(2,1)S(1)}, u32[]{:S(2)}, u32[]{:S(2)}) %collective-permute-start.2) | collective-permute-done | bytes 917536 | tf_op jit(solution)/shard_map/ppermute | solution.py:10
  292.1 0.9 copy.54
  (7 shorter events, 0.1 us)
Async XLA Ops:
  6.5 3.6 %copy-start = (bf16[1,128,3584]{2,1,0:T(8,128)(2,1)S(1)}, bf16[1,128,3584]{2,1,0:T(8,128)(2,1)}, u32[]{:S(2)}) copy-start(bf16[1,128,3584]{2,1,0:T(8,128)(2,1)} %param.6) | copy-start | bytes 2752516
  6.5 164.8 %all-gather.7.cloned.1.call-start = ((), (), s32[]{:S(2)}) async-start(), calls=%async_computation.4 | async-start | bytes 5505024 | tf_op jit(solution)/shard_map/all_gather | solution.py:38
  54.0 6.4 %copy-start.1 = (bf16[1,128,3584]{2,1,0:T(8,128)(2,1)S(1)}, bf16[1,128,3584]{2,1,0:T(8,128)(2,1)}, u32[]{:S(2)}) copy-start(bf16[1,128,3584]{2,1,0:T(8,128)(2,1)} %param.7) | copy-start | bytes 2752516
  54.0 60.3 %all-to-all-start.1 = ((bf16[8,65,1792]{2,1,0:T(8,128)(2,1)}), bf16[8,65,1792]{2,1,0:T(8,128)(2,1)}, u32[]{:S(2)}, u32[]{:S(2)}) async-start(bf16[8,65,1792]{2,1,0:T(8,128)(2,1)} %bitcast.51), calls=%async_computation.1 | async-start | bytes 4128768 | tf_op jit(solution)/shard_map/all_to_all | solution.py:51
  63.5 5.4 %copy-start.2 = (f32[1,128,2]{1,2,0:T(2,128)S(1)}, f32[1,128,2]{1,2,0:T(2,128)}, u32[]{:S(2)}) copy-start(f32[1,128,2]{1,2,0:T(2,128)} %param.9) | copy-start | bytes 3076
  114.3 53.5 %all-to-all-start = ((bf16[8,65,1792]{2,1,0:T(8,128)(2,1)}), bf16[8,65,1792]{2,1,0:T(8,128)(2,1)}, u32[]{:S(2)}, u32[]{:S(2)}) async-start(bf16[8,65,1792]{2,1,0:T(8,128)(2,1)} %bitcast.52), calls=%async_computation | async-start | bytes 4128768 | tf_op jit(solution)/shard_map/all_to_all | solution.py:52
  119.4 56.8 %all-gather.5.cloned.1.call-start = ((), (), s32[]{:S(2)}) async-start(), calls=%async_computation.3 | async-start | bytes 5505024 | tf_op jit(solution)/shard_map/all_gather | solution.py:39
  176.0 5.5 %collective-permute-start.1 = (bf16[520,1024]{1,0:T(8,128)(2,1)S(1)}, bf16[520,1024]{1,0:T(8,128)(2,1)}, u32[]{:S(2)}, u32[]{:S(2)}) collective-permute-start(bf16[520,1024]{1,0:T(8,128)(2,1)S(1)} %fusion.12), channel_id=1, source_target_pairs={{0,2},{2,0},{4,6},{6,4},{8,10},{10,8},{12,14},{14,12},{1,3},{3,1},... | collective-permute-start | bytes 3194888 | tf_op jit(solution)/shard_map/ppermute | solution.py:10
  176.1 7.7 %copy-start.3 = (bf16[1,1,1792,1024]{3,2,1,0:T(8,128)(2,1)S(1)}, bf16[1,1,1792,1024]{3,2,1,0:T(8,128)(2,1)}, u32[]{:S(2)}) copy-start(bf16[1,1,1792,1024]{3,2,1,0:T(8,128)(2,1)} %all-gather.7.cloned.1.call-done) | copy-start | bytes 11010052
  181.0 2.8 collective-permute-start
  270.2 21.8 %collective-permute-start.2 = (bf16[128,3584]{1,0:T(8,128)(2,1)S(1)}, bf16[128,3584]{1,0:T(8,128)(2,1)S(1)}, u32[]{:S(2)}, u32[]{:S(2)}) collective-permute-start(bf16[128,3584]{1,0:T(8,128)(2,1)S(1)} %add_convert_fusion), channel_id=1, source_target_pairs={{0,16},{16,0},{1,17},{17,1},{2,18},{18,2},{3,19},{19,3},{4,20},{20... | collective-permute-start | bytes 2752520 | tf_op jit(solution)/shard_map/ppermute | solution.py:10
Sparse Core Ops, SparseCore 0:
  8.9 53.5 all-gather.6
  121.7 52.3 all-gather.4
where the time goes:
time: 302 us; the launch traced here: 300 us
  local copies, waits for them, and re-layouts  122 us (40%)
  waiting for transfers between devices  68.2 us (23%)
  blocking collectives  51.9 us (17%)
  other arithmetic  15.5 us (5%)
  matrix products  15 us (5%)
  starting transfers between devices  13.8 us (5%)
  between operations  13.5 us (4%)
    all_to_all x1, blocking collectives, body(): lax.all_to_all(back, 'expert', split_axis=0, concat_axis=0, tiled=True)  51.9 us
    all_to_all x1, waiting for transfers between devices, body(): lax.all_to_all(grad_send, 'expert', split_axis=0, concat_axis=0, tiled=True)  44.3 us
    scatter x1, local copies, waits for them, and re-layouts, body(): empty.at[flat_ids, :, rank].set(tok_rows[source].reshape(-1, 2, half))  35.4 us
    scatter x1, local copies, waits for them, and re-layouts, body(): grad_send = empty.at[flat_ids, :, rank].set(scaled.reshape(-1, 2, half))  35.2 us
    ppermute x3, waiting for transfers between devices, partner(): return lax.ppermute(value, axis, pairs)  22.6 us
    reduce_sum x1, other arithmetic, body(): expert_sum = jnp.sum(rows_back, axis=1)  7.65 us
    gather x1, local copies, waits for them, and re-layouts, body(): returned[flat_ids, :, rank].reshape(tok_dev, top, width).astype(jnp.float32)  7.27 us
    all_to_all x1, starting transfers between devices, body(): lax.all_to_all(tok_send, 'expert', split_axis=0, concat_axis=0, tiled=True)  6.4 us
  transfers between devices with their start and end apart: 7, of which 3 were waited for; matrix products, arithmetic and copies ran while one was open for 39% of the time, Pallas kernels for 0%

commit v1 on v0

v1 whole, which is shorter than its diff:
```python
import functools

import jax
import jax.numpy as jnp
from jax import lax
from jax.experimental import pallas as pl
from jax.experimental.pallas import tpu as pltpu
from jax.sharding import PartitionSpec as P

LANES = 128
TILE = 256
F32 = jnp.float32
BF16 = jnp.bfloat16
MIB = 1 << 20


def slots_of(tok_dev, top, experts):
    capacity = min(tok_dev, max(2, tok_dev * top // experts + 1))
    if capacity % 16 == 1 and capacity > 1:
        return capacity - 1, 1
    return -(-capacity // 16) * 16, 0


def fold_columns(pieces, base):
    return -(-pieces // base) * LANES


def fold(ext_ref, row, pieces, first, base):
    for k in range(pieces):
        at = first + k
        column = at // base * LANES
        ext_ref[at % base : at % base + 1, column : column + LANES] = row[:, k * LANES : (k + 1) * LANES]


def unfold(row_ref, at_row, ext, pieces, first, base):
    for k in range(pieces):
        at = first + k
        column = at // base * LANES
        row_ref[at_row : at_row + 1, k * LANES : (k + 1) * LANES] = ext[
            at % base : at % base + 1, column : column + LANES
        ]


def slot_row(ids, expert):
    tokens = ids.shape[1]
    hit = jnp.where(ids == expert, 1.0, 0.0).astype(F32)
    mask = jnp.sum(hit, axis=0, keepdims=True)
    earlier = lax.broadcasted_iota(jnp.int32, (tokens, tokens), 0) < lax.broadcasted_iota(
        jnp.int32, (tokens, tokens), 1
    )
    before = jnp.dot(
        jnp.broadcast_to(mask, (16, tokens)).astype(BF16),
        jnp.where(earlier, 1.0, 0.0).astype(BF16),
        preferred_element_type=F32,
    )[0:1]
    return jnp.where(mask > 0.5, before, -1.0)


def dispatch_kernel(dists, base, extra, ids_ref, gates_ref, tok_ref, grad_ref, *refs):
    outs, ext_ref = refs[: len(dists)], refs[len(dists)]
    here = lax.axis_index("expert") // 2
    ids, gates = ids_ref[...], gates_ref[...]
    tokens, width = tok_ref.shape
    pieces = width // LANES
    rows = base + 16 * extra
    for dist, out in zip(dists, outs):
        expert = here ^ dist
        slot = slot_row(ids, expert)
        gate = jnp.sum(jnp.where(ids == expert, gates, 0.0), axis=0, keepdims=True)
        picks = lax.broadcasted_iota(jnp.int32, (rows, tokens), 0).astype(F32) == slot
        onehot = jnp.where(picks, 1.0, 0.0).astype(BF16)
        scale = jnp.sum(jnp.where(picks, gate, 0.0), axis=1, keepdims=True)
        if extra:
            ext_ref[...] = jnp.zeros_like(ext_ref)
        for at in range(0, width, 512):
            cols = slice(at, at + 512)
            x = jnp.dot(onehot, tok_ref[:, cols], preferred_element_type=F32)
            g = jnp.dot(onehot, grad_ref[:, cols], preferred_element_type=F32) * scale
            out[:, cols] = x[:base].astype(BF16)
            out[:, width + at : width + at + 512] = g[:base].astype(BF16)
            if extra:
                fold(ext_ref, x[base : base + 1], 4, at // LANES, base)
                fold(ext_ref, g[base : base + 1], 4, pieces + at // LANES, base)
        if extra:
            out[:, 2 * width :] = ext_ref[...].astype(BF16)


def dispatch(dists, base, extra, ids_t, gates_t, tok, grad):
    tokens, width = tok.shape
    ext = fold_columns(2 * width // LANES, base)
    cols = 2 * width + extra * ext
    vmem = pl.BlockSpec(memory_space=pltpu.VMEM)
    return pl.pallas_call(
        functools.partial(dispatch_kernel, dists, base, extra),
        out_shape=[jax.ShapeDtypeStruct((base, cols), BF16) for _ in dists],
        in_specs=[vmem] * 4,
        out_specs=[vmem] * len(dists),
        scratch_shapes=[pltpu.VMEM((base, ext), F32)],
        compiler_params=pltpu.CompilerParams(vmem_limit_bytes=24 * MIB),
        cost_estimate=pl.CostEstimate(
            flops=4 * len(dists) * (base + 16) * tokens * width,
            bytes_accessed=4 * tokens * width + 2 * len(dists) * base * cols,
            transcendentals=0,
        ),
        name="dispatch",
    )(ids_t, gates_t, tok, grad)


def silu_slope(pre):
    sig = jax.nn.sigmoid(pre)
    return sig * (1.0 + pre * (1.0 - sig))


def expert_kernel(n, base, extra, shards, *refs):
    msgs, refs = refs[:n], refs[n:]
    w_shards, v_shards, refs = refs[:shards], refs[shards : 2 * shards], refs[2 * shards :]
    outs, refs = refs[:n], refs[n:]
    w, v, x, g, slope, act, ext, row32, ext32, sem_x, sem_g, sem_e, sem_w, sem_v = refs
    width, ff = w.shape
    parts = shards // 2
    half, fh = width // 2, ff // parts
    pieces = width // LANES
    full = n * base
    core = lax.axis_index("expert") % 2

    def start(src, dst, sem):
        copy = pltpu.make_async_copy(src, dst, sem)
        copy.start()
        return copy

    x_in, g_in, e_in = [], [], []
    for i in range(n):
        rows = pl.ds(i * base, base)
        x_in.append(start(msgs[i].at[:, pl.ds(0, width)], x.at[rows, :], sem_x.at[i]))
        if extra:
            e_in.append(start(msgs[i].at[:, pl.ds(2 * width, ext.shape[2])], ext.at[i], sem_e.at[i]))

    def shards_in(given, whole, sems):
        copies = []
        for y in range(parts):
            for c in range(2):
                at = pl.multiple_of((core if c == 0 else 1 - core) * half, half)
                copies.append(
                    start(given[2 * y + c], whole.at[pl.ds(at, half), pl.ds(y * fh, fh)], sems.at[2 * y + c])
                )
        return copies

    w_in = shards_in(w_shards, w, sem_w)
    for i in range(n):
        g_in.append(start(msgs[i].at[:, pl.ds(width, width)], g.at[pl.ds(i * base, base), :], sem_g.at[i]))
    v_in = shards_in(v_shards, v, sem_v)

    def put_extra(rows_ref, first):
        row32[...] = jnp.zeros_like(row32)
        for i in range(n):
            unfold(row32, i, ext[i].astype(F32), pieces, first, base)
        rows_ref[full:, :] = row32[...].astype(BF16)

    for copy in x_in + e_in:
        copy.wait()
    if extra:
        put_extra(x, 0)
    for y in range(parts):
        for copy in w_in[2 * y : 2 * y + 2]:
            copy.wait()
        for at in range(y * fh, (y + 1) * fh, TILE):
            cols = slice(at, at + TILE)
            slope[:, cols] = silu_slope(jnp.dot(x[...], w[:, cols], preferred_element_type=F32))
    for copy in g_in:
        copy.wait()
    if extra:
        put_extra(g, pieces)
    for y in range(parts):
        for copy in v_in[2 * y : 2 * y + 2]:
            copy.wait()
        for at in range(y * fh, (y + 1) * fh, TILE):
            cols = slice(at, at + TILE)
            hid = jnp.dot(g[...], v[:, cols], preferred_element_type=F32)
            act[:, cols] = (hid * slope[:, cols]).astype(BF16)
    if extra:
        ext32[...] = jnp.zeros_like(ext32)
    for at in range(0, width, TILE):
        back = lax.dot_general(
            act[...], w[at : at + TILE, :], (((1,), (1,)), ((), ())), preferred_element_type=F32
        )
        for i in range(n):
            outs[i][:, at : at + TILE] = back[i * base : (i + 1) * base].astype(BF16)
            if extra:
                fold(ext32.at[i], back[full + i : full + i + 1], TILE // LANES, at // LANES, base)
    if extra:
        for i in range(n):
            outs[i][:, width:] = ext32[i].astype(BF16)


def expert(msgs, base, extra, w_shards, v_shards):
    n = len(msgs)
    half, fh = w_shards[0].shape
    shards = len(w_shards)
    width, ff = 2 * half, shards // 2 * fh
    rows = n * base + -(-n * extra // 16) * 16
    ext = fold_columns(2 * width // LANES, base)
    back_ext = fold_columns(width // LANES, base)
    cols = width + extra * back_ext
    anywhere, vmem = pl.BlockSpec(memory_space=pl.ANY), pl.BlockSpec(memory_space=pltpu.VMEM)
    spare = max(16, rows - n * base)
    return pl.pallas_call(
        functools.partial(expert_kernel, n, base, extra, shards),
        out_shape=[jax.ShapeDtypeStruct((base, cols), BF16) for _ in msgs],
        in_specs=[anywhere] * (n + 2 * shards),
        out_specs=[vmem] * n,
        scratch_shapes=[
            pltpu.VMEM((width, ff), BF16),
            pltpu.VMEM((width, ff), BF16),
            pltpu.VMEM((rows, width), BF16),
            pltpu.VMEM((rows, width), BF16),
            pltpu.VMEM((rows, ff), F32),
            pltpu.VMEM((rows, ff), BF16),
            pltpu.VMEM((n, base, ext), BF16),
            pltpu.VMEM((spare, width), F32),
            pltpu.VMEM((n, base, back_ext), F32),
            pltpu.SemaphoreType.DMA((n,)),
            pltpu.SemaphoreType.DMA((n,)),
            pltpu.SemaphoreType.DMA((n,)),
            pltpu.SemaphoreType.DMA((shards,)),
            pltpu.SemaphoreType.DMA((shards,)),
        ],
        compiler_params=pltpu.CompilerParams(vmem_limit_bytes=40 * MIB),
        cost_estimate=pl.CostEstimate(
            flops=6 * rows * width * ff,
            bytes_accessed=4 * width * ff + 6 * rows * width,
            transcendentals=rows * ff,
        ),
        name="expert",
    )(*msgs, *w_shards, *v_shards)


def combine_kernel(dists, base, extra, ids_ref, grad_ref, *refs):
    n = len(dists)
    msgs, (out, rows, ext, row32, sem_b, sem_e) = refs[:n], refs[n:]
    tokens, width = grad_ref.shape
    pieces = width // LANES
    full = n * base
    here = lax.axis_index("expert") // 2
    copies = []
    for i in range(n):
        copies.append(
            pltpu.make_async_copy(msgs[i].at[:, pl.ds(0, width)], rows.at[pl.ds(i * base, base), :], sem_b.at[i])
        )
        if extra:
            copies.append(
                pltpu.make_async_copy(msgs[i].at[:, pl.ds(width, ext.shape[2])], ext.at[i], sem_e.at[i])
            )
    for copy in copies:
        copy.start()
    ids = ids_ref[...]
    places = []
    overflow = jnp.zeros((tokens, 16), F32)
    for i, dist in enumerate(dists):
        slot = jnp.transpose(jnp.broadcast_to(slot_row(ids, here ^ dist), (LANES, tokens)))
        slot = slot[:, 0:1]
        at = lax.broadcasted_iota(jnp.int32, (tokens, base), 1).astype(F32)
        places.append(jnp.where(at == slot, 1.0, 0.0).astype(BF16))
        if extra:
            mine = lax.broadcasted_iota(jnp.int32, (tokens, 16), 1) == i
            overflow = overflow + jnp.where(mine & (slot == float(base)), 1.0, 0.0)
    for copy in copies:
        copy.wait()
    if extra:
        row32[...] = jnp.zeros_like(row32)
        for i in range(n):
            unfold(row32, i, ext[i].astype(F32), pieces, 0, base)
        rows[full:, :] = row32[...].astype(BF16)
    overflow = overflow.astype(BF16)
    for at in range(0, width, 512):
        cols = slice(at, at + 512)
        total = grad_ref[:, cols].astype(F32)
        for i in range(n):
            total = total + jnp.dot(
                places[i], rows[i * base : (i + 1) * base, cols], preferred_element_type=F32
            )
        if extra:
            total = total + jnp.dot(overflow, rows[full:, cols], preferred_element_type=F32)
        out[:, cols] = total.astype(BF16)


def combine(dists, base, extra, ids_t, grad, msgs):
    n = len(dists)
    tokens, width = grad.shape
    rows = n * base + 16 * extra
    ext = fold_columns(width // LANES, base)
    anywhere, vmem = pl.BlockSpec(memory_space=pl.ANY), pl.BlockSpec(memory_space=pltpu.VMEM)
    return pl.pallas_call(
        functools.partial(combine_kernel, dists, base, extra),
        out_shape=jax.ShapeDtypeStruct((tokens, width), BF16),
        in_specs=[vmem, vmem] + [anywhere] * n,
        out_specs=vmem,
        scratch_shapes=[
            pltpu.VMEM((rows, width), BF16),
            pltpu.VMEM((n, base, ext), BF16),
            pltpu.VMEM((16, width), F32),
            pltpu.SemaphoreType.DMA((n,)),
            pltpu.SemaphoreType.DMA((n,)),
        ],
        compiler_params=pltpu.CompilerParams(vmem_limit_bytes=24 * MIB),
        cost_estimate=pl.CostEstimate(
            flops=2 * rows * tokens * width,
            bytes_accessed=2 * rows * width + 4 * tokens * width,
            transcendentals=0,
        ),
        name="combine",
    )(ids_t, grad, *msgs)


def swap(value, axis, apart):
    return lax.ppermute(value, axis, [(i, i ^ apart) for i in range(lax.axis_size(axis))])


def swap_back(value, apart):
    sections, places = lax.axis_size("section"), lax.axis_size("expert")
    pairs = [
        (s * places + i, (s ^ 1) * places + (i ^ apart)) for s in range(sections) for i in range(places)
    ]
    return lax.ppermute(value, ("section", "expert"), pairs)


def groups_of(experts):
    if experts == 4:
        return [[2], [3], [1, 0]]
    order = list(range(experts - 1, -1, -1))
    size = -(-experts // 4)
    return [order[i : i + size] for i in range(0, experts, size)]


def body(tokens, grad_out, expert_ids, gate_values, w_in, w_out_t):
    tok, grad = tokens[0], grad_out[0]
    ids_t, gates_t = expert_ids[0].T, gate_values[0].T
    experts = lax.axis_size("expert") // 2
    base, extra = slots_of(tok.shape[0], ids_t.shape[0], experts)
    groups = groups_of(experts)
    w_own, v_own = w_in[0, 0], w_out_t[0, 0]
    w_columns = [w_own] + [swap(w_own, "dp", apart) for apart in range(1, lax.axis_size("dp"))]
    v_columns = [v_own] + [swap(v_own, "dp", apart) for apart in range(1, lax.axis_size("dp"))]
    sent = [dispatch(group, base, extra, ids_t, gates_t, tok, grad) for group in groups]
    got = [
        [swap(msg, "expert", 2 * dist) if dist else msg for dist, msg in zip(group, msgs)]
        for group, msgs in zip(groups, sent)
    ]
    w_shards = [shard for own in w_columns for shard in (own, swap(own, "expert", 1))]
    v_shards = [shard for own in v_columns for shard in (own, swap(own, "expert", 1))]
    other_grad, other_ids = swap(grad, "section", 1), swap(ids_t, "section", 1)
    dists, returned = [], []
    for group, msgs in zip(groups, got):
        backs = expert(msgs, base, extra, w_shards, v_shards)
        dists += group
        returned += [swap_back(back, 2 * dist) for dist, back in zip(group, backs)]
    return combine(dists, base, extra, other_ids, other_grad, returned)[None]


def solution(mesh):
    rows = P("section", ("expert", "dp"), None)
    weights = P("section", "expert", None, "dp")
    return jax.shard_map(
        body,
        mesh=mesh,
        in_specs=(rows, rows, rows, rows, weights, weights),
        out_specs=rows,
        check_vma=False,
    )
```

time: 302 us -> 238 us (0.79)
  local copies, waits for them, and re-layouts: 122 us -> 3.76 us
  waiting for transfers between devices: 68.2 us -> 183 us
  blocking collectives: 51.9 us -> 0 us
  Pallas kernels: 0 us -> 31.8 us
  other arithmetic: 15.5 us -> 0 us
  matrix products: 15 us -> 0 us
  between operations: 13.5 us -> 0.29 us
  starting transfers between devices: 13.8 us -> 18.4 us
    ppermute x3 -> x15, waiting for transfers between devices: 22.6 us -> 183 us  [the longest x11 153 us: swap(): lax.ppermute(value, axis, [(i, i ^ apart) for i in range(lax.axis_size(ax...]
    scatter x2 -> x0, local copies, waits for them, and re-layouts: 70.5 us -> none  [the longest x1 35.4 us: body(): empty.at[flat_ids, :, rank].set(tok_rows[source].reshape(-1, 2, half))]
    all_to_all x1 -> x0, blocking collectives: 51.9 us -> none  [body(): lax.all_to_all(back, 'expert', split_axis=0, concat_axis=0, tiled=True)]
    all_to_all x2 -> x0, waiting for transfers between devices: 44.3 us -> none  [the longest x1 44.3 us: body(): lax.all_to_all(grad_send, 'expert', split_axis=0, concat_axis=0, tiled=True)]
    pallas_call x0 -> x7, Pallas kernels: none -> 31.8 us  [the longest x3 22.8 us: expert(): pl.pallas_call(functools.partial(expert_kernel, n, base, extra, shards),...]
    reshape x7 -> x0, local copies, waits for them, and re-layouts: 20.6 us -> none  [the longest x1 3.49 us: body(): grad_flat = grad_in.reshape(sources * slots, half)]
    ppermute x3 -> x15, starting transfers between devices: 2.15 us -> 18.4 us  [the longest x11 11.3 us: swap(): lax.ppermute(value, axis, [(i, i ^ apart) for i in range(lax.axis_size(ax...]
    dot_general x3 -> x0, matrix products: 15 us -> none  [the longest x1 5.45 us: body(): lax.dot_general(act_grad, w_in_full, (((1,), (1,)), ((), ())), preferred_...]
  transfers between devices with their start and end apart: 7 -> 15, of which waited for: 3 -> 7; matrix products, arithmetic and copies ran while one was open for 39% -> 0% of each run, Pallas kernels for 0% -> 12%
where the time goes in v1:
time: 238 us; the launch traced here: 237 us
  waiting for transfers between devices  183 us (77%)
  Pallas kernels  31.8 us (13%)
  starting transfers between devices  18.4 us (8%)
  local copies, waits for them, and re-layouts  3.76 us (2%)
    ppermute x11, waiting for transfers between devices, swap(): lax.ppermute(value, axis, [(i, i ^ apart) for i in range(lax.axis_size(ax...  153 us
    ppermute x4, waiting for transfers between devices, swap_back(): return lax.ppermute(value, ('section', 'expert'), pairs)  30.1 us
    pallas_call x3, Pallas kernels, expert(): pl.pallas_call(functools.partial(expert_kernel, n, base, extra, shards),...  22.8 us
    ppermute x11, starting transfers between devices, swap(): lax.ppermute(value, axis, [(i, i ^ apart) for i in range(lax.axis_size(ax...  11.3 us
    ppermute x4, starting transfers between devices, swap_back(): return lax.ppermute(value, ('section', 'expert'), pairs)  7.14 us
    pallas_call x3, Pallas kernels, dispatch(): pl.pallas_call(functools.partial(dispatch_kernel, dists, base, extra), ou...  5.93 us
  transfers between devices with their start and end apart: 15, of which 7 were waited for; matrix products, arithmetic and copies ran while one was open for 0% of the time, Pallas kernels for 12%

profile of v1, /device:TPU:0, one launch (start us, length us, event | category | flops | bytes accessed | tf_op | source)
XLA Modules:
  0.0 237.5 jit_solution(6613381754400197829)
XLA Ops:
  0.0 3.0 %collective-permute-start.4 = (bf16[1792,512]{1,0:T(8,128)(2,1)}, bf16[1792,512]{1,0:T(8,128)(2,1)S(1)}, u32[]{:S(2)}, u32[]{:S(2)}) collective-permute-start(bf16[1792,512]{1,0:T(8,128)(2,1)} %bitcast.11), channel_id=1, source_target_pairs={{0,1},{1,0},{2,3},{3,2},{4,5},{5,4},{6,7},{7,6},{8,9},{9,8},{10,11... | collective-permute-start | bytes 5505032 | tf_op jit(solution)/shard_map/ppermute | solution.py:315
  3.0 0.0 collective-permute-start.7
  3.0 0.0 collective-permute-start.3
  3.0 0.5 collective-permute-start.6
  3.5 40.5 %collective-permute-done.4.refs_3_.refs_4_ = bf16[1792,512]{1,0:T(8,128)(2,1)S(1)} collective-permute-done((bf16[1792,512]{1,0:T(8,128)(2,1)}, bf16[1792,512]{1,0:T(8,128)(2,1)S(1)}, u32[]{:S(2)}, u32[]{:S(2)}) %collective-permute-start.4) | collective-permute-done | bytes 1835040 | tf_op jit(solution)/shard_map/ppermute | solution.py:315
  44.0 0.0 collective-permute-start.5
  44.0 38.5 %collective-permute-done.7.refs_7_.refs_8_ = bf16[1792,512]{1,0:T(8,128)(2,1)S(1)} collective-permute-done((bf16[1792,512]{1,0:T(8,128)(2,1)}, bf16[1792,512]{1,0:T(8,128)(2,1)S(1)}, u32[]{:S(2)}, u32[]{:S(2)}) %collective-permute-start.7) | collective-permute-done | bytes 1835040 | tf_op jit(solution)/shard_map/ppermute | solution.py:315
  82.5 0.0 copy-start.2
  82.5 0.0 collective-permute-start.8
  82.5 0.0 copy-start.4
  82.5 1.8 copy-done.4
  84.4 0.0 copy-start.5
  84.4 0.7 copy-done.5
  85.0 2.2 dispatch.5
  87.3 1.9 collective-permute-start.12
  89.1 0.0 copy-start.1
  89.1 1.9 dispatch.4
  91.1 0.0 copy-done.2
  91.1 0.0 copy-start
  91.1 18.8 %collective-permute-done.12.refs_0_ = bf16[64,7296]{1,0:T(8,128)(2,1)S(1)} collective-permute-done((bf16[64,7296]{1,0:T(8,128)(2,1)S(1)}, bf16[64,7296]{1,0:T(8,128)(2,1)S(1)}, u32[]{:S(2)}, u32[]{:S(2)}) %collective-permute-start.12) | collective-permute-done | bytes 933920 | tf_op jit(solution)/shard_map/ppermute | solution.py:315
  109.8 3.8 %collective-permute-start.10 = (bf16[64,7296]{1,0:T(8,128)(2,1)S(1)}, bf16[64,7296]{1,0:T(8,128)(2,1)S(1)}, u32[]{:S(2)}, u32[]{:S(2)}) collective-permute-start(bf16[64,7296]{1,0:T(8,128)(2,1)S(1)} %dispatch.4), channel_id=1, source_target_pairs={{0,12},{2,14},{4,8},{6,10},{8,4},{10,6},{12,0},{14,2},{1,13},{3,15... | collective-permute-start | bytes 2801672 | tf_op jit(solution)/shard_map/ppermute | solution.py:315
  113.6 1.8 dispatch.3
  115.4 0.0 collective-permute-done.3.refs_2_.refs_3_
  115.4 0.1 collective-permute-start.2
  115.5 0.0 collective-permute-done.6.refs_6_.refs_7_
  115.5 1.6 collective-permute-start.1
  117.0 0.0 collective-permute-done.5.refs_4_.refs_5_
  117.1 0.5 collective-permute-start
  117.6 0.0 collective-permute-done.8.refs_8_.refs_9_
  117.6 0.0 copy-start.6
  117.6 1.2 copy-done.6
  118.8 0.0 copy-done.1
  118.8 0.0 copy-done
  118.8 0.0 copy-start.3
  118.8 7.5 %expert.5 = (bf16[64,3712]{1,0:T(8,128)(2,1)S(1)}, bf16[64,3712]{1,0:T(8,128)(2,1)S(1)}) custom-call(bf16[64,7296]{1,0:T(8,128)(2,1)S(1)} %collective-permute-done.12.refs_0_, bf16[64,7296]{1,0:T(8,128)(2,1)S(1)} %get-tuple-element.10.refs_1_, bf16[1792,512]{1,0:T(8,128)(2,1)S(1)} %bitcast.13, bf16[1792,512]{1,0:T(8,128)(2,1)S(1)} %collective-permute-done.3.refs_2_.refs_3_, ...), custom_call_target="tpu_custom_call" | custom-call | flops 3170893824 | bytes 17776640 | tf_op jit(solution)/shard_map/expert/pallas_call | solution.py:206
  126.3 1.7 collective-permute-start.13
  128.0 7.4 %collective-permute-done.10.refs_0_ = bf16[64,7296]{1,0:T(8,128)(2,1)S(1)} collective-permute-done((bf16[64,7296]{1,0:T(8,128)(2,1)S(1)}, bf16[64,7296]{1,0:T(8,128)(2,1)S(1)}, u32[]{:S(2)}, u32[]{:S(2)}) %collective-permute-start.10) | collective-permute-done | bytes 933920 | tf_op jit(solution)/shard_map/ppermute | solution.py:315
  135.4 1.7 collective-permute-start.14
  137.0 0.0 copy-done.3
  137.0 7.6 %expert.4 = bf16[64,3712]{1,0:T(8,128)(2,1)S(1)} custom-call(bf16[64,7296]{1,0:T(8,128)(2,1)S(1)} %collective-permute-done.10.refs_0_, bf16[1792,512]{1,0:T(8,128)(2,1)S(1)} %bitcast.14, bf16[1792,512]{1,0:T(8,128)(2,1)S(1)} %collective-permute-done.3.refs_2_.refs_3_, bf16[1792,512]{1,0:T(8,128)(2,1)S(1)} %collective-permute-done.4.refs_3_.refs_4_, ...), custom_call_target="tpu_custom_call" | custom-call | flops 1761607680 | bytes 16400384 | tf_op jit(solution)/shard_map/expert/pallas_call | solution.py:206
  144.6 48.0 %collective-permute-done.2.refs_0_ = bf16[64,7296]{1,0:T(8,128)(2,1)S(1)} collective-permute-done((bf16[64,7296]{1,0:T(8,128)(2,1)S(1)}, bf16[64,7296]{1,0:T(8,128)(2,1)S(1)}, u32[]{:S(2)}, u32[]{:S(2)}) %collective-permute-start.2) | collective-permute-done | bytes 933920 | tf_op jit(solution)/shard_map/ppermute | solution.py:315
  192.6 3.7 %collective-permute-start.11 = (bf16[64,3712]{1,0:T(8,128)(2,1)S(1)}, bf16[64,3712]{1,0:T(8,128)(2,1)S(1)}, u32[]{:S(2)}, u32[]{:S(2)}) collective-permute-start(bf16[64,3712]{1,0:T(8,128)(2,1)S(1)} %expert.4), channel_id=1, source_target_pairs={{0,28},{2,30},{4,24},{6,26},{8,20},{10,22},{12,16},{14,18},{16,12}... | collective-permute-start | bytes 1425416 | tf_op jit(solution)/shard_map/ppermute | solution.py:323
  196.3 7.8 %expert.3 = bf16[64,3712]{1,0:T(8,128)(2,1)S(1)} custom-call(bf16[64,7296]{1,0:T(8,128)(2,1)S(1)} %collective-permute-done.2.refs_0_, bf16[1792,512]{1,0:T(8,128)(2,1)S(1)} %bitcast.15, bf16[1792,512]{1,0:T(8,128)(2,1)S(1)} %collective-permute-done.3.refs_2_.refs_3_, bf16[1792,512]{1,0:T(8,128)(2,1)S(1)} %collective-permute-done.4.refs_3_.refs_4_, ...), custom_call_target="tpu_custom_call" | custom-call | flops 1761607680 | bytes 16400384 | tf_op jit(solution)/shard_map/expert/pallas_call | solution.py:206
  204.1 0.0 collective-permute-done.ids_ref
  204.1 0.1 collective-permute-start.9
  204.2 0.0 collective-permute-done.1.grad_ref
  204.2 0.0 collective-permute-done.13.refs_2_
  204.2 0.0 collective-permute-done.14.refs_3_
  204.2 5.0 %collective-permute-done.11.refs_1_ = bf16[64,3712]{1,0:T(8,128)(2,1)S(1)} collective-permute-done((bf16[64,3712]{1,0:T(8,128)(2,1)S(1)}, bf16[64,3712]{1,0:T(8,128)(2,1)S(1)}, u32[]{:S(2)}, u32[]{:S(2)}) %collective-permute-start.11) | collective-permute-done | bytes 475168 | tf_op jit(solution)/shard_map/ppermute | solution.py:323
  209.2 25.1 %collective-permute-done.9.refs_0_ = bf16[64,3712]{1,0:T(8,128)(2,1)S(1)} collective-permute-done((bf16[64,3712]{1,0:T(8,128)(2,1)S(1)}, bf16[64,3712]{1,0:T(8,128)(2,1)S(1)}, u32[]{:S(2)}, u32[]{:S(2)}) %collective-permute-start.9) | collective-permute-done | bytes 475168 | tf_op jit(solution)/shard_map/ppermute | solution.py:323
  234.3 3.0 %combine.1 = bf16[128,3584]{1,0:T(8,128)(2,1)} custom-call(s32[2,128]{1,0:T(2,128)S(1)} %collective-permute-done.ids_ref, bf16[128,3584]{1,0:T(8,128)(2,1)S(1)} %collective-permute-done.1.grad_ref, bf16[64,3712]{1,0:T(8,128)(2,1)S(1)} %collective-permute-done.9.refs_0_, bf16[64,3712]{1,0:T(8,128)(2,1)S(1)} %collective-permute-done.11.refs_1_, ...), custom_call_target="tpu_custom_call" | custom-call | flops 249561088 | bytes 3784704 | tf_op jit(solution)/shard_map/combine/pallas_call | solution.py:292
Async XLA Ops:
  0.0 44.0 %collective-permute-start.4 = (bf16[1792,512]{1,0:T(8,128)(2,1)}, bf16[1792,512]{1,0:T(8,128)(2,1)S(1)}, u32[]{:S(2)}, u32[]{:S(2)}) collective-permute-start(bf16[1792,512]{1,0:T(8,128)(2,1)} %bitcast.11), channel_id=1, source_target_pairs={{0,1},{1,0},{2,3},{3,2},{4,5},{5,4},{6,7},{7,6},{8,9},{9,8},{10,11... | collective-permute-start | bytes 5505032 | tf_op jit(solution)/shard_map/ppermute | solution.py:315
  3.0 79.5 %collective-permute-start.7 = (bf16[1792,512]{1,0:T(8,128)(2,1)}, bf16[1792,512]{1,0:T(8,128)(2,1)S(1)}, u32[]{:S(2)}, u32[]{:S(2)}) collective-permute-start(bf16[1792,512]{1,0:T(8,128)(2,1)} %bitcast.16), channel_id=1, source_target_pairs={{0,1},{1,0},{2,3},{3,2},{4,5},{5,4},{6,7},{7,6},{8,9},{9,8},{10,11... | collective-permute-start | bytes 5505032 | tf_op jit(solution)/shard_map/ppermute | solution.py:315
  3.0 112.4 %collective-permute-start.3 = (bf16[1792,512]{1,0:T(8,128)(2,1)}, bf16[1792,512]{1,0:T(8,128)(2,1)S(1)}, u32[]{:S(2)}, u32[]{:S(2)}) collective-permute-start(bf16[1792,512]{1,0:T(8,128)(2,1)} %bitcast.12), channel_id=1, source_target_pairs={{0,2},{2,0},{4,6},{6,4},{8,10},{10,8},{12,14},{14,12},{1,3},{3,1},... | collective-permute-start | bytes 5505032 | tf_op jit(solution)/shard_map/ppermute | solution.py:315
  3.0 112.5 %collective-permute-start.6 = (bf16[1792,512]{1,0:T(8,128)(2,1)}, bf16[1792,512]{1,0:T(8,128)(2,1)S(1)}, u32[]{:S(2)}, u32[]{:S(2)}) collective-permute-start(bf16[1792,512]{1,0:T(8,128)(2,1)} %bitcast.17), channel_id=1, source_target_pairs={{0,2},{2,0},{4,6},{6,4},{8,10},{10,8},{12,14},{14,12},{1,3},{3,1},... | collective-permute-start | bytes 5505032 | tf_op jit(solution)/shard_map/ppermute | solution.py:315
  44.0 73.0 %collective-permute-start.5 = (bf16[1792,512]{1,0:T(8,128)(2,1)S(1)}, bf16[1792,512]{1,0:T(8,128)(2,1)S(1)}, u32[]{:S(2)}, u32[]{:S(2)}) collective-permute-start(bf16[1792,512]{1,0:T(8,128)(2,1)S(1)} %collective-permute-done.4.refs_3_.refs_4_), channel_id=1, source_target_pairs={{0,2},{2,0},{4,6},{6,4},{8,10},{10,8},{12,14},{14,12},{1,3},{3,1},... | collective-permute-start | bytes 5505032 | tf_op jit(solution)/shard_map/ppermute | solution.py:315
  82.5 8.5 %copy-start.2 = (bf16[1792,512]{1,0:T(8,128)(2,1)}, bf16[1792,512]{1,0:T(8,128)(2,1)S(1)}, u32[]{:S(2)}) copy-start(bf16[1792,512]{1,0:T(8,128)(2,1)S(1)} %collective-permute-done.7.refs_7_.refs_8_) | copy-start | bytes 5505028
  82.5 35.1 %collective-permute-start.8 = (bf16[1792,512]{1,0:T(8,128)(2,1)S(1)}, bf16[1792,512]{1,0:T(8,128)(2,1)S(1)}, u32[]{:S(2)}, u32[]{:S(2)}) collective-permute-start(bf16[1792,512]{1,0:T(8,128)(2,1)S(1)} %collective-permute-done.7.refs_7_.refs_8_), channel_id=1, source_target_pairs={{0,2},{2,0},{4,6},{6,4},{8,10},{10,8},{12,14},{14,12},{1,3},{3,1},... | collective-permute-start | bytes 5505032 | tf_op jit(solution)/shard_map/ppermute | solution.py:315
  82.5 1.8 copy-start.4
  84.4 0.7 copy-start.5
  87.3 22.6 %collective-permute-start.12 = (bf16[64,7296]{1,0:T(8,128)(2,1)S(1)}, bf16[64,7296]{1,0:T(8,128)(2,1)S(1)}, u32[]{:S(2)}, u32[]{:S(2)}) collective-permute-start(bf16[64,7296]{1,0:T(8,128)(2,1)S(1)} %get-tuple-element.9), channel_id=1, source_target_pairs={{0,4},{2,6},{4,0},{6,2},{8,12},{10,14},{12,8},{14,10},{1,5},{3,7},... | collective-permute-start | bytes 2801672 | tf_op jit(solution)/shard_map/ppermute | solution.py:315
  89.1 29.7 %copy-start.1 = (bf16[1,1,1792,512]{3,2,1,0:T(8,128)(2,1)S(1)}, bf16[1,1,1792,512]{3,2,1,0:T(8,128)(2,1)}, u32[]{:S(2)}) copy-start(bf16[1,1,1792,512]{3,2,1,0:T(8,128)(2,1)} %param.11) | copy-start | bytes 5505028
  91.1 27.8 %copy-start = (bf16[1,1,1792,512]{3,2,1,0:T(8,128)(2,1)S(1)}, bf16[1,1,1792,512]{3,2,1,0:T(8,128)(2,1)}, u32[]{:S(2)}) copy-start(bf16[1,1,1792,512]{3,2,1,0:T(8,128)(2,1)} %param.10) | copy-start | bytes 5505028
  109.8 25.5 %collective-permute-start.10 = (bf16[64,7296]{1,0:T(8,128)(2,1)S(1)}, bf16[64,7296]{1,0:T(8,128)(2,1)S(1)}, u32[]{:S(2)}, u32[]{:S(2)}) collective-permute-start(bf16[64,7296]{1,0:T(8,128)(2,1)S(1)} %dispatch.4), channel_id=1, source_target_pairs={{0,12},{2,14},{4,8},{6,10},{8,4},{10,6},{12,0},{14,2},{1,13},{3,15... | collective-permute-start | bytes 2801672 | tf_op jit(solution)/shard_map/ppermute | solution.py:315
  115.4 77.2 %collective-permute-start.2 = (bf16[64,7296]{1,0:T(8,128)(2,1)S(1)}, bf16[64,7296]{1,0:T(8,128)(2,1)S(1)}, u32[]{:S(2)}, u32[]{:S(2)}) collective-permute-start(bf16[64,7296]{1,0:T(8,128)(2,1)S(1)} %dispatch.3), channel_id=1, source_target_pairs={{0,8},{2,10},{4,12},{6,14},{8,0},{10,2},{12,4},{14,6},{1,9},{3,11}... | collective-permute-start | bytes 2801672 | tf_op jit(solution)/shard_map/ppermute | solution.py:315
  115.5 88.7 %collective-permute-start.1 = (bf16[128,3584]{1,0:T(8,128)(2,1)}, bf16[128,3584]{1,0:T(8,128)(2,1)S(1)}, u32[]{:S(2)}, u32[]{:S(2)}) collective-permute-start(bf16[128,3584]{1,0:T(8,128)(2,1)} %bitcast.2.grad_ref), channel_id=1, source_target_pairs={{0,16},{16,0},{1,17},{17,1},{2,18},{18,2},{3,19},{19,3},{4,20},{20... | collective-permute-start | bytes 2752520 | tf_op jit(solution)/shard_map/ppermute | solution.py:315
  117.1 87.1 %collective-permute-start = (s32[2,128]{1,0:T(2,128)}, s32[2,128]{1,0:T(2,128)S(1)}, u32[]{:S(2)}, u32[]{:S(2)}) collective-permute-start(s32[2,128]{1,0:T(2,128)} %bitcast.1.ids_ref), channel_id=1, source_target_pairs={{0,16},{16,0},{1,17},{17,1},{2,18},{18,2},{3,19},{19,3},{4,20},{20... | collective-permute-start | bytes 3080 | tf_op jit(solution)/shard_map/ppermute | solution.py:315
  117.6 1.2 copy-start.6
  118.8 18.2 %copy-start.3 = (bf16[1792,512]{1,0:T(8,128)(2,1)S(1)}, bf16[1792,512]{1,0:T(8,128)(2,1)}, u32[]{:S(2)}) copy-start(bf16[1792,512]{1,0:T(8,128)(2,1)} %copy-done.2) | copy-start | bytes 5505028
  126.3 77.9 %collective-permute-start.13 = (bf16[64,3712]{1,0:T(8,128)(2,1)S(1)}, bf16[64,3712]{1,0:T(8,128)(2,1)S(1)}, u32[]{:S(2)}, u32[]{:S(2)}) collective-permute-start(bf16[64,3712]{1,0:T(8,128)(2,1)S(1)} %get-tuple-element.11), channel_id=1, source_target_pairs={{0,20},{2,22},{4,16},{6,18},{8,28},{10,30},{12,24},{14,26},{16,4},... | collective-permute-start | bytes 1425416 | tf_op jit(solution)/shard_map/ppermute | solution.py:323
  135.4 68.8 %collective-permute-start.14 = (bf16[64,3712]{1,0:T(8,128)(2,1)S(1)}, bf16[64,3712]{1,0:T(8,128)(2,1)S(1)}, u32[]{:S(2)}, u32[]{:S(2)}) collective-permute-start(bf16[64,3712]{1,0:T(8,128)(2,1)S(1)} %get-tuple-element.12), channel_id=1, source_target_pairs={{0,16},{2,18},{4,20},{6,22},{8,24},{10,26},{12,28},{14,30},{16,0},... | collective-permute-start | bytes 1425416 | tf_op jit(solution)/shard_map/ppermute | solution.py:323
  192.6 16.6 %collective-permute-start.11 = (bf16[64,3712]{1,0:T(8,128)(2,1)S(1)}, bf16[64,3712]{1,0:T(8,128)(2,1)S(1)}, u32[]{:S(2)}, u32[]{:S(2)}) collective-permute-start(bf16[64,3712]{1,0:T(8,128)(2,1)S(1)} %expert.4), channel_id=1, source_target_pairs={{0,28},{2,30},{4,24},{6,26},{8,20},{10,22},{12,16},{14,18},{16,12}... | collective-permute-start | bytes 1425416 | tf_op jit(solution)/shard_map/ppermute | solution.py:323
  204.1 30.2 %collective-permute-start.9 = (bf16[64,3712]{1,0:T(8,128)(2,1)S(1)}, bf16[64,3712]{1,0:T(8,128)(2,1)S(1)}, u32[]{:S(2)}, u32[]{:S(2)}) collective-permute-start(bf16[64,3712]{1,0:T(8,128)(2,1)S(1)} %expert.3), channel_id=1, source_target_pairs={{0,24},{2,26},{4,28},{6,30},{8,16},{10,18},{12,20},{14,22},{16,8},... | collective-permute-start | bytes 1425416 | tf_op jit(solution)/shard_map/ppermute | solution.py:323

commit v2 on v1

--- a/solution.py
+++ b/solution.py
@@ -96,7 +96,7 @@
         in_specs=[vmem] * 4,
         out_specs=[vmem] * len(dists),
         scratch_shapes=[pltpu.VMEM((base, ext), F32)],
-        compiler_params=pltpu.CompilerParams(vmem_limit_bytes=24 * MIB),
+        compiler_params=pltpu.CompilerParams(vmem_limit_bytes=60 * MIB),
         cost_estimate=pl.CostEstimate(
             flops=4 * len(dists) * (base + 16) * tokens * width,
             bytes_accessed=4 * tokens * width + 2 * len(dists) * base * cols,
@@ -111,127 +111,175 @@
     return sig * (1.0 + pre * (1.0 - sig))
 
 
-def expert_kernel(n, base, extra, shards, *refs):
+def begin(src, dst, sem):
+    copy = pltpu.make_async_copy(src, dst, sem)
+    copy.start()
+    return copy
+
+
+def begin_weights(pieces, layout, whole, sems):
+    half = whole.shape[0] // 2
+    core = lax.axis_index("expert") % 2
+    copies = {}
+    for i, (piece, (block, other, row, columns)) in enumerate(zip(pieces, layout)):
+        at = pl.multiple_of((1 - core if other else core) * half + row, 16)
+        rows = pl.ds(at, piece.shape[0])
+        dst = whole.at[rows, pl.ds(block * columns, columns)]
+        copies.setdefault(block, []).append(begin(piece, dst, sems.at[i]))
+    return copies
+
+
+def begin_rows(msgs, rows, ext, start, sems, ext_sems):
+    base = msgs[0].shape[0]
+    width = rows.shape[1]
+    copies = []
+    for i, msg in enumerate(msgs):
+        copies.append(begin(msg.at[:, pl.ds(start, width)], rows.at[pl.ds(i * base, base), :], sems.at[i]))
+        if ext is not None:
+            copies.append(begin(msg.at[:, pl.ds(2 * width, ext.shape[2])], ext.at[i], ext_sems.at[i]))
+    return copies
+
+
+def finish(copies):
+    for copy in copies:
+        copy.wait()
+
+
+def put_extra(rows, row32, ext, n, base, first):
+    row32[...] = jnp.zeros_like(row32)
+    for i in range(n):
+        unfold(row32, i, ext[i].astype(F32), rows.shape[1] // LANES, first, base)
+    rows[n * base :, :] = row32[...].astype(BF16)
+
+
+def expert_kernel(n, base, extra, stage, w_layout, v_layout, *refs):
     msgs, refs = refs[:n], refs[n:]
-    w_shards, v_shards, refs = refs[:shards], refs[shards : 2 * shards], refs[2 * shards :]
-    outs, refs = refs[:n], refs[n:]
-    w, v, x, g, slope, act, ext, row32, ext32, sem_x, sem_g, sem_e, sem_w, sem_v = refs
-    width, ff = w.shape
-    parts = shards // 2
-    half, fh = width // 2, ff // parts
+    w_pieces, refs = refs[: len(w_layout)], refs[len(w_layout) :]
+    v_pieces, refs = refs[: len(v_layout)], refs[len(v_layout) :]
+    if stage == "late":
+        slope, partial, refs = refs[0], refs[1], refs[2:]
+        outs, refs = refs[:n], refs[n:]
+    elif stage == "early":
+        slope_late, partial_out, slope, refs = refs[0], refs[1], refs[2], refs[3:]
+    else:
+        outs, slope, refs = refs[:n], refs[n], refs[n + 1 :]
+    w, v, x, g, act, ext, row32, ext32, sem_x, sem_g, sem_e, sem_w, sem_v = refs
+    width = w.shape[0]
+    half_ff = w_layout[0][3]
     pieces = width // LANES
     full = n * base
-    core = lax.axis_index("expert") % 2
-
-    def start(src, dst, sem):
-        copy = pltpu.make_async_copy(src, dst, sem)
-        copy.start()
-        return copy
-
-    x_in, g_in, e_in = [], [], []
-    for i in range(n):
-        rows = pl.ds(i * base, base)
-        x_in.append(start(msgs[i].at[:, pl.ds(0, width)], x.at[rows, :], sem_x.at[i]))
-        if extra:
-            e_in.append(start(msgs[i].at[:, pl.ds(2 * width, ext.shape[2])], ext.at[i], sem_e.at[i]))
-
-    def shards_in(given, whole, sems):
-        copies = []
-        for y in range(parts):
-            for c in range(2):
-                at = pl.multiple_of((core if c == 0 else 1 - core) * half, half)
-                copies.append(
-                    start(given[2 * y + c], whole.at[pl.ds(at, half), pl.ds(y * fh, fh)], sems.at[2 * y + c])
-                )
-        return copies
-
-    w_in = shards_in(w_shards, w, sem_w)
-    for i in range(n):
-        g_in.append(start(msgs[i].at[:, pl.ds(width, width)], g.at[pl.ds(i * base, base), :], sem_g.at[i]))
-    v_in = shards_in(v_shards, v, sem_v)
-
-    def put_extra(rows_ref, first):
-        row32[...] = jnp.zeros_like(row32)
+    x_in = []
+    if stage != "late":
+        x_in = begin_rows(msgs, x, ext if extra else None, 0, sem_x, sem_e)
+    w_in = begin_weights(w_pieces, w_layout, w, sem_w)
+    g_in = begin_rows(msgs, g, ext if extra and stage == "late" else None, width, sem_g, sem_e)
+    v_in = begin_weights(v_pieces, v_layout, v, sem_v)
+    if stage != "late":
+        finish(x_in)
+        if extra:
+            put_extra(x, row32, ext, n, base, 0)
+        for block in sorted(w_in):
+            finish(w_in[block])
+            for at in range(block * half_ff, (block + 1) * half_ff, TILE):
+                value = silu_slope(jnp.dot(x[...], w[:, at : at + TILE], preferred_element_type=F32))
+                if stage == "early" and block > 0:
+                    slope_late[:, at - half_ff : at - half_ff + TILE] = value
+                else:
+                    slope[:, at : at + TILE] = value
+    finish(g_in)
+    if extra:
+        put_extra(g, row32, ext, n, base, pieces)
+    for block in sorted(v_in):
+        finish(v_in[block])
+        for at in range(block * half_ff, (block + 1) * half_ff, TILE):
+            hid = jnp.dot(g[...], v[:, at : at + TILE], preferred_element_type=F32)
+            act[:, at : at + TILE] = (hid * slope[:, at : at + TILE]).astype(BF16)
+    if stage == "late":
+        for block in sorted(w_in):
+            finish(w_in[block])
+    if extra and stage != "early":
+        ext32[...] = jnp.zeros_like(ext32)
+    hidden = act.shape[1]
+    for at in range(0, width, TILE):
+        cols = slice(at, at + TILE)
+        back = lax.dot_general(
+            act[...], w[cols, :hidden], (((1,), (1,)), ((), ())), preferred_element_type=F32
+        )
+        if stage == "early":
+            partial_out[:, cols] = back
+            continue
+        if stage == "late":
+            back = back + partial[:, cols]
         for i in range(n):
-            unfold(row32, i, ext[i].astype(F32), pieces, first, base)
-        rows_ref[full:, :] = row32[...].astype(BF16)
-
-    for copy in x_in + e_in:
-        copy.wait()
-    if extra:
-        put_extra(x, 0)
-    for y in range(parts):
-        for copy in w_in[2 * y : 2 * y + 2]:
-            copy.wait()
-        for at in range(y * fh, (y + 1) * fh, TILE):
-            cols = slice(at, at + TILE)
-            slope[:, cols] = silu_slope(jnp.dot(x[...], w[:, cols], preferred_element_type=F32))
-    for copy in g_in:
-        copy.wait()
-    if extra:
-        put_extra(g, pieces)
-    for y in range(parts):
-        for copy in v_in[2 * y : 2 * y + 2]:
-            copy.wait()
-        for at in range(y * fh, (y + 1) * fh, TILE):
-            cols = slice(at, at + TILE)
-            hid = jnp.dot(g[...], v[:, cols], preferred_element_type=F32)
-            act[:, cols] = (hid * slope[:, cols]).astype(BF16)
-    if extra:
-        ext32[...] = jnp.zeros_like(ext32)
-    for at in range(0, width, TILE):
-        back = lax.dot_general(
-            act[...], w[at : at + TILE, :], (((1,), (1,)), ((), ())), preferred_element_type=F32
-        )
-        for i in range(n):
-            outs[i][:, at : at + TILE] = back[i * base : (i + 1) * base].astype(BF16)
+            outs[i][:, cols] = back[i * base : (i + 1) * base].astype(BF16)
             if extra:
                 fold(ext32.at[i], back[full + i : full + i + 1], TILE // LANES, at // LANES, base)
-    if extra:
+    if extra and stage != "early":
         for i in range(n):
             outs[i][:, width:] = ext32[i].astype(BF16)
 
 
-def expert(msgs, base, extra, w_shards, v_shards):
+def expert(msgs, base, extra, w_columns, v_columns, stage="whole", carried=()):
     n = len(msgs)
-    half, fh = w_shards[0].shape
-    shards = len(w_shards)
-    width, ff = 2 * half, shards // 2 * fh
+
+    def flat(columns):
+        arrays, layout = [], []
+        for block, cores in enumerate(columns):
+            for other, pieces in enumerate(cores):
+                row = 0
+                for piece in pieces:
+                    arrays.append(piece)
+                    layout.append((block, other, row, piece.shape[1]))
+                    row += piece.shape[0]
+        return arrays, layout, row
+
+    w_pieces, w_layout, half = flat(w_columns)
+    v_pieces, v_layout, _ = flat(v_columns)
+    width, block_ff = 2 * half, w_layout[0][3]
+    w_ff, v_ff = len(w_columns) * block_ff, len(v_columns) * block_ff
     rows = n * base + -(-n * extra // 16) * 16
     ext = fold_columns(2 * width // LANES, base)
     back_ext = fold_columns(width // LANES, base)
     cols = width + extra * back_ext
     anywhere, vmem = pl.BlockSpec(memory_space=pl.ANY), pl.BlockSpec(memory_space=pltpu.VMEM)
     spare = max(16, rows - n * base)
+    own_slope = [] if stage == "late" else [pltpu.VMEM((rows, v_ff), F32)]
+    if stage == "early":
+        out_shape = [
+            jax.ShapeDtypeStruct((rows, w_ff - block_ff), F32),
+            jax.ShapeDtypeStruct((rows, width), F32),
+        ]
+    else:
+        out_shape = [jax.ShapeDtypeStruct((base, cols), BF16) for _ in msgs]
     return pl.pallas_call(
-        functools.partial(expert_kernel, n, base, extra, shards),
-        out_shape=[jax.ShapeDtypeStruct((base, cols), BF16) for _ in msgs],
-        in_specs=[anywhere] * (n + 2 * shards),
-        out_specs=[vmem] * n,
-        scratch_shapes=[
-            pltpu.VMEM((width, ff), BF16),
-            pltpu.VMEM((width, ff), BF16),
+        functools.partial(expert_kernel, n, base, extra, stage, w_layout, v_layout),
+        out_shape=out_shape,
+        in_specs=[anywhere] * (n + len(w_pieces) + len(v_pieces)) + [vmem] * len(carried),
+        out_specs=[vmem] * len(out_shape),
+        scratch_shapes=own_slope
+        + [
+            pltpu.VMEM((width, w_ff), BF16),
+            pltpu.VMEM((width, v_ff), BF16),
             pltpu.VMEM((rows, width), BF16),
             pltpu.VMEM((rows, width), BF16),
-            pltpu.VMEM((rows, ff), F32),
-            pltpu.VMEM((rows, ff), BF16),
+            pltpu.VMEM((rows, v_ff), BF16),
             pltpu.VMEM((n, base, ext), BF16),
             pltpu.VMEM((spare, width), F32),
             pltpu.VMEM((n, base, back_ext), F32),
             pltpu.SemaphoreType.DMA((n,)),
             pltpu.SemaphoreType.DMA((n,)),
             pltpu.SemaphoreType.DMA((n,)),
-            pltpu.SemaphoreType.DMA((shards,)),
-            pltpu.SemaphoreType.DMA((shards,)),
+            pltpu.SemaphoreType.DMA((len(w_pieces),)),
+            pltpu.SemaphoreType.DMA((len(v_pieces),)),
         ],
-        compiler_params=pltpu.CompilerParams(vmem_limit_bytes=40 * MIB),
+        compiler_params=pltpu.CompilerParams(vmem_limit_bytes=24 * MIB),
         cost_estimate=pl.CostEstimate(
-            flops=6 * rows * width * ff,
-            bytes_accessed=4 * width * ff + 6 * rows * width,
-            transcendentals=rows * ff,
+            flops=2 * rows * width * (w_ff + 2 * v_ff),
+            bytes_accessed=2 * width * (w_ff + v_ff) + 6 * rows * width,
+            transcendentals=rows * w_ff,
         ),
-        name="expert",
-    )(*msgs, *w_shards, *v_shards)
+        name="expert_" + stage,
+    )(*msgs, *w_pieces, *v_pieces, *carried)
 
 
 def combine_kernel(dists, base, extra, ids_ref, grad_ref, *refs):
@@ -323,12 +371,17 @@
     return lax.ppermute(value, ("section", "expert"), pairs)
 
 
+def after(*values):
+    return lax.optimization_barrier(values)
+
+
 def groups_of(experts):
     if experts == 4:
-        return [[2], [3], [1, 0]]
+        return [[2], [3], [1, 0]], [[2, 0], [3, 1]]
     order = list(range(experts - 1, -1, -1))
     size = -(-experts // 4)
-    return [order[i : i + size] for i in range(0, experts, size)]
+    groups = [order[i : i + size] for i in range(0, experts, size)]
+    return groups, groups
 
 
 def body(tokens, grad_out, expert_ids, gate_values, w_in, w_out_t):
@@ -336,21 +389,42 @@
     ids_t, gates_t = expert_ids[0].T, gate_values[0].T
     experts = lax.axis_size("expert") // 2
     base, extra = slots_of(tok.shape[0], ids_t.shape[0], experts)
-    groups = groups_of(experts)
+    sends, works = groups_of(experts)
+    others = range(1, lax.axis_size("dp"))
     w_own, v_own = w_in[0, 0], w_out_t[0, 0]
-    w_columns = [w_own] + [swap(w_own, "dp", apart) for apart in range(1, lax.axis_size("dp"))]
-    v_columns = [v_own] + [swap(v_own, "dp", apart) for apart in range(1, lax.axis_size("dp"))]
-    sent = [dispatch(group, base, extra, ids_t, gates_t, tok, grad) for group in groups]
-    got = [
-        [swap(msg, "expert", 2 * dist) if dist else msg for dist, msg in zip(group, msgs)]
-        for group, msgs in zip(groups, sent)
-    ]
-    w_shards = [shard for own in w_columns for shard in (own, swap(own, "expert", 1))]
-    v_shards = [shard for own in v_columns for shard in (own, swap(own, "expert", 1))]
+    sent = [dispatch(group, base, extra, ids_t, gates_t, tok, grad) for group in sends]
+    sent[0], w_own, v_own = after(sent[0], w_own, v_own)
+    w_far = [swap(w_own, "dp", apart) for apart in others]
+    v_far = [swap(v_own, "dp", apart) for apart in others]
+    got = {}
+    for group, msgs in zip(sends, sent):
+        for dist, msg in zip(group, msgs):
+            got[dist] = swap(msg, "expert", 2 * dist) if dist else msg
+    first, rest = sends[0], [dist for group in sends[1:] for dist in group]
+
+    w_other, v_other = [swap(w_own, "expert", 1)], [swap(v_own, "expert", 1)]
+    w_far, heads, sent, w_other, v_other = after(w_far, [got[dist] for dist in first], sent, w_other, v_other)
+    got.update(zip(first, heads))
+    w_other += [swap(block, "expert", 1) for block in w_far]
+    w_columns = [[[block], [other]] for block, other in zip([w_own] + w_far, w_other)]
+    v_columns = [[[v_own], [v_other[0]]]]
+    carried = expert([got[dist] for dist in works[0]], base, extra, w_columns, v_columns, "early")
+    grad, ids_t, w_other = after(grad, ids_t, w_other)
     other_grad, other_ids = swap(grad, "section", 1), swap(ids_t, "section", 1)
+    v_far, tails, other_grad, other_ids, carried = after(
+        v_far, [got[dist] for dist in rest], other_grad, other_ids, carried
+    )
+    got.update(zip(rest, tails))
+    v_columns += [[[block], [swap(block, "expert", 1)]] for block in v_far]
+
     dists, returned = [], []
-    for group, msgs in zip(groups, got):
-        backs = expert(msgs, base, extra, w_shards, v_shards)
+    for i, group in enumerate(works):
+        msgs = [got[dist] for dist in group]
+        if i == 0:
+            backs = expert(msgs, base, extra, w_columns[1:], v_columns[1:], "late", carried)
+            backs, got = after(backs, got)
+        else:
+            backs = expert(msgs, base, extra, w_columns, v_columns)
         dists += group
         returned += [swap_back(back, 2 * dist) for dist, back in zip(group, backs)]
     return combine(dists, base, extra, other_ids, other_grad, returned)[None]

time: 238 us -> 152 us (0.64)
  waiting for transfers between devices: 183 us -> 100 us
  Pallas kernels: 31.8 us -> 29.4 us
    ppermute x11, waiting for transfers between devices: 153 us -> 69.1 us  [swap(): lax.ppermute(value, axis, [(i, i ^ apart) for i in range(lax.axis_size(ax...]
    pallas_call x3, Pallas kernels: 22.8 us -> 16.4 us  [expert(): pl.pallas_call(functools.partial(expert_kernel, n, base, extra, stage, w_...]
    pallas_call x3, Pallas kernels: 5.93 us -> 9.97 us  [dispatch(): pl.pallas_call(functools.partial(dispatch_kernel, dists, base, extra), ou...]
  transfers between devices with their start and end apart: 15 -> 15, of which waited for: 7 -> 6; matrix products, arithmetic and copies ran while one was open for 0% -> 0% of each run, Pallas kernels for 12% -> 13%
where the time goes in v2:
time: 152 us
  waiting for transfers between devices  100 us (66%)
  Pallas kernels  29.4 us (19%)
  starting transfers between devices  18.9 us (12%)
  local copies, waits for them, and re-layouts  2.7 us (2%)
    ppermute x11, waiting for transfers between devices, swap(): lax.ppermute(value, axis, [(i, i ^ apart) for i in range(lax.axis_size(ax...  69.1 us
    ppermute x4, waiting for transfers between devices, swap_back(): return lax.ppermute(value, ('section', 'expert'), pairs)  31.3 us
    pallas_call x3, Pallas kernels, expert(): pl.pallas_call(functools.partial(expert_kernel, n, base, extra, stage, w_...  16.4 us
    ppermute x11, starting transfers between devices, swap(): lax.ppermute(value, axis, [(i, i ^ apart) for i in range(lax.axis_size(ax...  12.3 us
    pallas_call x3, Pallas kernels, dispatch(): pl.pallas_call(functools.partial(dispatch_kernel, dists, base, extra), ou...  9.97 us
    ppermute x4, starting transfers between devices, swap_back(): return lax.ppermute(value, ('section', 'expert'), pairs)  6.59 us
    pallas_call x1, Pallas kernels, combine(): pl.pallas_call(functools.partial(combine_kernel, dists, base, extra), out...  3.04 us
  transfers between devices with their start and end apart: 15, of which 6 were waited for; matrix products, arithmetic and copies ran while one was open for 0% of the time, Pallas kernels for 13%

profile of v2, /device:TPU:0, one launch (start us, length us, event | category | flops | bytes accessed | tf_op | source)
XLA Modules:
  0.0 151.7 jit_solution(1875211451182675782)
XLA Ops:
  0.0 0.0 copy-start
  0.0 3.2 %dispatch.3 = bf16[64,7296]{1,0:T(8,128)(2,1)} custom-call(s32[2,128]{1,0:T(2,128)} %bitcast.29, f32[2,128]{1,0:T(2,128)} %bitcast.26, bf16[128,3584]{1,0:T(8,128)(2,1)} %bitcast.19, bf16[128,3584]{1,0:T(8,128)(2,1)} %bitcast.22), custom_call_target="tpu_custom_call" | custom-call | flops 146800640 | bytes 2768896 | tf_op jit(solution)/shard_map/dispatch/pallas_call | solution.py:93
  3.2 0.0 copy-start.5
  3.2 0.5 collective-permute-start.6
  3.6 0.0 copy-done
  3.6 0.1 collective-permute-start.5
  3.7 3.0 %collective-permute-start.3 = (bf16[1792,512]{1,0:T(8,128)(2,1)S(1)}, bf16[1792,512]{1,0:T(8,128)(2,1)S(1)}, u32[]{:S(2)}, u32[]{:S(2)}) collective-permute-start(bf16[1792,512]{1,0:T(8,128)(2,1)S(1)} %bitcast.12), channel_id=1, source_target_pairs={{0,1},{1,0},{2,3},{3,2},{4,5},{5,4},{6,7},{7,6},{8,9},{9,8},{10,11... | collective-permute-start | bytes 5505032 | tf_op jit(solution)/shard_map/ppermute | solution.py:363
  6.7 2.6 %collective-permute-start.4 = (bf16[64,7296]{1,0:T(8,128)(2,1)}, bf16[64,7296]{1,0:T(8,128)(2,1)}, u32[]{:S(2)}, u32[]{:S(2)}) collective-permute-start(bf16[64,7296]{1,0:T(8,128)(2,1)} %dispatch.3), channel_id=1, source_target_pairs={{0,8},{2,10},{4,12},{6,14},{8,0},{10,2},{12,4},{14,6},{1,9},{3,11}... | collective-permute-start | bytes 2801672 | tf_op jit(solution)/shard_map/ppermute | solution.py:363
  9.2 3.1 %dispatch.4 = bf16[64,7296]{1,0:T(8,128)(2,1)} custom-call(s32[2,128]{1,0:T(2,128)} %bitcast.30, f32[2,128]{1,0:T(2,128)} %bitcast.27, bf16[128,3584]{1,0:T(8,128)(2,1)} %bitcast.20, bf16[128,3584]{1,0:T(8,128)(2,1)} %bitcast.23), custom_call_target="tpu_custom_call" | custom-call | flops 146800640 | bytes 2768896 | tf_op jit(solution)/shard_map/dispatch/pallas_call | solution.py:93
  12.3 3.7 %dispatch.5 = (bf16[64,7296]{1,0:T(8,128)(2,1)}, bf16[64,7296]{1,0:T(8,128)(2,1)}) custom-call(s32[2,128]{1,0:T(2,128)} %bitcast.31, f32[2,128]{1,0:T(2,128)} %bitcast.28, bf16[128,3584]{1,0:T(8,128)(2,1)} %bitcast.21, bf16[128,3584]{1,0:T(8,128)(2,1)} %bitcast.24), custom_call_target="tpu_custom_call" | custom-call | flops 293601280 | bytes 3702784 | tf_op jit(solution)/shard_map/dispatch/pallas_call | solution.py:93
  16.0 34.2 %collective-permute-done.4.refs_0_ = bf16[64,7296]{1,0:T(8,128)(2,1)} collective-permute-done((bf16[64,7296]{1,0:T(8,128)(2,1)}, bf16[64,7296]{1,0:T(8,128)(2,1)}, u32[]{:S(2)}, u32[]{:S(2)}) %collective-permute-start.4) | collective-permute-done | bytes 933920 | tf_op jit(solution)/shard_map/ppermute | solution.py:363
  50.3 0.0 collective-permute-done.6.refs_7_
  50.3 0.0 collective-permute-done.5.refs_3_
  50.3 0.0 collective-permute-done.3.refs_4_.refs_2_
  50.3 0.1 collective-permute-start.7
  50.4 0.5 collective-permute-start
  50.9 3.5 %collective-permute-start.1 = (bf16[64,7296]{1,0:T(8,128)(2,1)}, bf16[64,7296]{1,0:T(8,128)(2,1)S(1)}, u32[]{:S(2)}, u32[]{:S(2)}) collective-permute-start(bf16[64,7296]{1,0:T(8,128)(2,1)} %dispatch.4), channel_id=1, source_target_pairs={{0,12},{2,14},{4,8},{6,10},{8,4},{10,6},{12,0},{14,2},{1,13},{3,15... | collective-permute-start | bytes 2801672 | tf_op jit(solution)/shard_map/ppermute | solution.py:363
  54.4 0.0 collective-permute-start.2
  54.4 0.0 collective-permute-done.7.refs_5_.refs_3_
  54.4 1.5 collective-permute-start.8
  55.9 0.0 copy-done.5
  55.9 0.5 collective-permute-start.9
  56.5 0.0 copy-start.1
  56.5 1.5 copy-done.1
  58.0 0.0 copy-start.3
  58.0 1.2 copy-done.3
  59.2 0.0 copy-start.4
  59.2 5.5 %expert_early.1 = (f32[144,512]{1,0:T(8,128)S(1)}, f32[144,3584]{1,0:T(8,128)S(1)}) custom-call(bf16[64,7296]{1,0:T(8,128)(2,1)} %collective-permute-done.4.refs_0_, bf16[64,7296]{1,0:T(8,128)(2,1)S(1)} %copy-done.3, bf16[1792,512]{1,0:T(8,128)(2,1)S(1)} %bitcast.13, bf16[1792,512]{1,0:T(8,128)(2,1)} %collective-permute-done.5.refs_3_, ...), custom_call_target="tpu_custom_call" | custom-call | flops 2113929216 | bytes 14106624 | tf_op jit(solution)/shard_map/expert_early/pallas_call | solution.py:254
  64.7 11.8 %collective-permute-done.1.refs_0_ = bf16[64,7296]{1,0:T(8,128)(2,1)S(1)} collective-permute-done((bf16[64,7296]{1,0:T(8,128)(2,1)}, bf16[64,7296]{1,0:T(8,128)(2,1)S(1)}, u32[]{:S(2)}, u32[]{:S(2)}) %collective-permute-start.1) | collective-permute-done | bytes 933920 | tf_op jit(solution)/shard_map/ppermute | solution.py:363
  76.5 19.2 %collective-permute-done.2.refs_1_ = bf16[64,7296]{1,0:T(8,128)(2,1)S(1)} collective-permute-done((bf16[64,7296]{1,0:T(8,128)(2,1)}, bf16[64,7296]{1,0:T(8,128)(2,1)S(1)}, u32[]{:S(2)}, u32[]{:S(2)}) %collective-permute-start.2) | collective-permute-done | bytes 933920 | tf_op jit(solution)/shard_map/ppermute | solution.py:363
  95.8 0.0 collective-permute-done.refs_4_.refs_8_
  95.8 0.0 collective-permute-done.9.ids_ref
  95.8 0.0 collective-permute-done.8.grad_ref
  95.8 0.0 copy-start.2
  95.8 0.1 collective-permute-start.10
  95.9 3.8 %collective-permute-done.10.refs_5_.refs_9_ = bf16[1792,512]{1,0:T(8,128)(2,1)S(1)} collective-permute-done((bf16[1792,512]{1,0:T(8,128)(2,1)S(1)}, bf16[1792,512]{1,0:T(8,128)(2,1)S(1)}, u32[]{:S(2)}, u32[]{:S(2)}) %collective-permute-start.10) | collective-permute-done | bytes 1835040 | tf_op jit(solution)/shard_map/ppermute | solution.py:363
  99.7 0.0 copy-done.4
  99.7 3.5 %expert_late.1 = (bf16[64,3712]{1,0:T(8,128)(2,1)S(1)}, bf16[64,3712]{1,0:T(8,128)(2,1)S(1)}) custom-call(bf16[64,7296]{1,0:T(8,128)(2,1)} %collective-permute-done.4.refs_0_, bf16[64,7296]{1,0:T(8,128)(2,1)S(1)} %copy-done.4, bf16[1792,512]{1,0:T(8,128)(2,1)S(1)} %collective-permute-done.3.refs_4_.refs_2_, ...), custom_call_target="tpu_custom_call" | custom-call | flops 1585446912 | bytes 10436608 | tf_op jit(solution)/shard_map/expert_late/pallas_call | solution.py:254
  103.2 1.6 %collective-permute-start.11 = (bf16[64,3712]{1,0:T(8,128)(2,1)S(1)}, bf16[64,3712]{1,0:T(8,128)(2,1)S(1)}, u32[]{:S(2)}, u32[]{:S(2)}) collective-permute-start(bf16[64,3712]{1,0:T(8,128)(2,1)S(1)} %get-tuple-element.57), channel_id=1, source_target_pairs={{0,24},{2,26},{4,28},{6,30},{8,16},{10,18},{12,20},{14,22},{16,8},... | collective-permute-start | bytes 1425416 | tf_op jit(solution)/shard_map/ppermute | solution.py:371
  104.8 0.5 collective-permute-start.12
  105.2 0.0 copy-done.2
  105.2 7.4 %expert_whole.1 = (bf16[64,3712]{1,0:T(8,128)(2,1)S(1)}, bf16[64,3712]{1,0:T(8,128)(2,1)S(1)}) custom-call(bf16[64,7296]{1,0:T(8,128)(2,1)S(1)} %collective-permute-done.1.refs_0_, bf16[64,7296]{1,0:T(8,128)(2,1)S(1)} %collective-permute-done.2.refs_1_, bf16[1792,512]{1,0:T(8,128)(2,1)S(1)} %bitcast.14, bf16[1792,512]{1,0:T(8,128)(2,1)} %collective-permute-done.5.refs_3_, ...), custom_call_target="tpu_custom_call" | custom-call | flops 3170893824 | bytes 17776640 | tf_op jit(solution)/shard_map/expert_whole/pallas_call | solution.py:254
  112.7 4.5 %collective-permute-start.13 = (bf16[64,3712]{1,0:T(8,128)(2,1)S(1)}, bf16[64,3712]{1,0:T(8,128)(2,1)S(1)}, u32[]{:S(2)}, u32[]{:S(2)}) collective-permute-start(bf16[64,3712]{1,0:T(8,128)(2,1)S(1)} %get-tuple-element.61), channel_id=1, source_target_pairs={{0,28},{2,30},{4,24},{6,26},{8,20},{10,22},{12,16},{14,18},{16,12}... | collective-permute-start | bytes 1425416 | tf_op jit(solution)/shard_map/ppermute | solution.py:371
  117.2 0.0 collective-permute-start.14
  117.2 22.0 %collective-permute-done.11.refs_0_ = bf16[64,3712]{1,0:T(8,128)(2,1)S(1)} collective-permute-done((bf16[64,3712]{1,0:T(8,128)(2,1)S(1)}, bf16[64,3712]{1,0:T(8,128)(2,1)S(1)}, u32[]{:S(2)}, u32[]{:S(2)}) %collective-permute-start.11) | collective-permute-done | bytes 475168 | tf_op jit(solution)/shard_map/ppermute | solution.py:371
  139.1 0.0 collective-permute-done.12.refs_1_
  139.2 0.0 collective-permute-done.13.refs_2_
  139.2 9.3 %collective-permute-done.14.refs_3_ = bf16[64,3712]{1,0:T(8,128)(2,1)S(1)} collective-permute-done((bf16[64,3712]{1,0:T(8,128)(2,1)S(1)}, bf16[64,3712]{1,0:T(8,128)(2,1)S(1)}, u32[]{:S(2)}, u32[]{:S(2)}) %collective-permute-start.14) | collective-permute-done | bytes 475168 | tf_op jit(solution)/shard_map/ppermute | solution.py:371
  148.5 3.0 %combine.1 = bf16[128,3584]{1,0:T(8,128)(2,1)} custom-call(s32[2,128]{1,0:T(2,128)S(1)} %collective-permute-done.9.ids_ref, bf16[128,3584]{1,0:T(8,128)(2,1)S(1)} %collective-permute-done.8.grad_ref, bf16[64,3712]{1,0:T(8,128)(2,1)S(1)} %collective-permute-done.11.refs_0_, bf16[64,3712]{1,0:T(8,128)(2,1)S(1)} %collective-permute-done.12.refs_1_, ...), custom_call_target="tpu_custom_call" | custom-call | flops 249561088 | bytes 3784704 | tf_op jit(solution)/shard_map/combine/pallas_call | solution.py:340
Async XLA Ops:
  0.0 3.6 %copy-start = (bf16[1,1,1792,512]{3,2,1,0:T(8,128)(2,1)S(1)}, bf16[1,1,1792,512]{3,2,1,0:T(8,128)(2,1)}, u32[]{:S(2)}) copy-start(bf16[1,1,1792,512]{3,2,1,0:T(8,128)(2,1)} %param.10) | copy-start | bytes 5505028
  3.2 52.8 %copy-start.5 = (s32[1,128,2]{1,2,0:T(2,128)S(1)}, s32[1,128,2]{1,2,0:T(2,128)}, u32[]{:S(2)}) copy-start(s32[1,128,2]{1,2,0:T(2,128)} %param.8) | copy-start | bytes 3076
  3.2 47.1 %collective-permute-start.6 = (bf16[1792,512]{1,0:T(8,128)(2,1)}, bf16[1792,512]{1,0:T(8,128)(2,1)}, u32[]{:S(2)}, u32[]{:S(2)}) collective-permute-start(bf16[1792,512]{1,0:T(8,128)(2,1)} %bitcast.15), channel_id=1, source_target_pairs={{0,2},{2,0},{4,6},{6,4},{8,10},{10,8},{12,14},{14,12},{1,3},{3,1},... | collective-permute-start | bytes 5505032 | tf_op jit(solution)/shard_map/ppermute | solution.py:363
  3.6 46.7 %collective-permute-start.5 = (bf16[1792,512]{1,0:T(8,128)(2,1)S(1)}, bf16[1792,512]{1,0:T(8,128)(2,1)}, u32[]{:S(2)}, u32[]{:S(2)}) collective-permute-start(bf16[1792,512]{1,0:T(8,128)(2,1)S(1)} %bitcast.11), channel_id=1, source_target_pairs={{0,2},{2,0},{4,6},{6,4},{8,10},{10,8},{12,14},{14,12},{1,3},{3,1},... | collective-permute-start | bytes 5505032 | tf_op jit(solution)/shard_map/ppermute | solution.py:363
  3.7 46.6 %collective-permute-start.3 = (bf16[1792,512]{1,0:T(8,128)(2,1)S(1)}, bf16[1792,512]{1,0:T(8,128)(2,1)S(1)}, u32[]{:S(2)}, u32[]{:S(2)}) collective-permute-start(bf16[1792,512]{1,0:T(8,128)(2,1)S(1)} %bitcast.12), channel_id=1, source_target_pairs={{0,1},{1,0},{2,3},{3,2},{4,5},{5,4},{6,7},{7,6},{8,9},{9,8},{10,11... | collective-permute-start | bytes 5505032 | tf_op jit(solution)/shard_map/ppermute | solution.py:363
  6.7 43.6 %collective-permute-start.4 = (bf16[64,7296]{1,0:T(8,128)(2,1)}, bf16[64,7296]{1,0:T(8,128)(2,1)}, u32[]{:S(2)}, u32[]{:S(2)}) collective-permute-start(bf16[64,7296]{1,0:T(8,128)(2,1)} %dispatch.3), channel_id=1, source_target_pairs={{0,8},{2,10},{4,12},{6,14},{8,0},{10,2},{12,4},{14,6},{1,9},{3,11}... | collective-permute-start | bytes 2801672 | tf_op jit(solution)/shard_map/ppermute | solution.py:363
  50.3 4.2 %collective-permute-start.7 = (bf16[1792,512]{1,0:T(8,128)(2,1)S(1)}, bf16[1792,512]{1,0:T(8,128)(2,1)S(1)}, u32[]{:S(2)}, u32[]{:S(2)}) collective-permute-start(bf16[1792,512]{1,0:T(8,128)(2,1)S(1)} %collective-permute-done.3.refs_4_.refs_2_), channel_id=1, source_target_pairs={{0,2},{2,0},{4,6},{6,4},{8,10},{10,8},{12,14},{14,12},{1,3},{3,1},... | collective-permute-start | bytes 5505032 | tf_op jit(solution)/shard_map/ppermute | solution.py:363
  50.4 45.4 %collective-permute-start = (bf16[1792,512]{1,0:T(8,128)(2,1)}, bf16[1792,512]{1,0:T(8,128)(2,1)S(1)}, u32[]{:S(2)}, u32[]{:S(2)}) collective-permute-start(bf16[1792,512]{1,0:T(8,128)(2,1)} %bitcast.16), channel_id=1, source_target_pairs={{0,1},{1,0},{2,3},{3,2},{4,5},{5,4},{6,7},{7,6},{8,9},{9,8},{10,11... | collective-permute-start | bytes 5505032 | tf_op jit(solution)/shard_map/ppermute | solution.py:363
  50.9 25.6 %collective-permute-start.1 = (bf16[64,7296]{1,0:T(8,128)(2,1)}, bf16[64,7296]{1,0:T(8,128)(2,1)S(1)}, u32[]{:S(2)}, u32[]{:S(2)}) collective-permute-start(bf16[64,7296]{1,0:T(8,128)(2,1)} %dispatch.4), channel_id=1, source_target_pairs={{0,12},{2,14},{4,8},{6,10},{8,4},{10,6},{12,0},{14,2},{1,13},{3,15... | collective-permute-start | bytes 2801672 | tf_op jit(solution)/shard_map/ppermute | solution.py:363
  54.4 41.4 %collective-permute-start.2 = (bf16[64,7296]{1,0:T(8,128)(2,1)}, bf16[64,7296]{1,0:T(8,128)(2,1)S(1)}, u32[]{:S(2)}, u32[]{:S(2)}) collective-permute-start(bf16[64,7296]{1,0:T(8,128)(2,1)} %get-tuple-element.35), channel_id=1, source_target_pairs={{0,4},{2,6},{4,0},{6,2},{8,12},{10,14},{12,8},{14,10},{1,5},{3,7},... | collective-permute-start | bytes 2801672 | tf_op jit(solution)/shard_map/ppermute | solution.py:363
  54.4 41.4 %collective-permute-start.8 = (bf16[128,3584]{1,0:T(8,128)(2,1)}, bf16[128,3584]{1,0:T(8,128)(2,1)S(1)}, u32[]{:S(2)}, u32[]{:S(2)}) collective-permute-start(bf16[128,3584]{1,0:T(8,128)(2,1)} %bitcast.25), channel_id=1, source_target_pairs={{0,16},{16,0},{1,17},{17,1},{2,18},{18,2},{3,19},{19,3},{4,20},{20... | collective-permute-start | bytes 2752520 | tf_op jit(solution)/shard_map/ppermute | solution.py:363
  55.9 39.9 %collective-permute-start.9 = (s32[2,128]{1,0:T(2,128)S(1)}, s32[2,128]{1,0:T(2,128)S(1)}, u32[]{:S(2)}, u32[]{:S(2)}) collective-permute-start(s32[2,128]{1,0:T(2,128)S(1)} %bitcast.32), channel_id=1, source_target_pairs={{0,16},{16,0},{1,17},{17,1},{2,18},{18,2},{3,19},{19,3},{4,20},{20... | collective-permute-start | bytes 3080 | tf_op jit(solution)/shard_map/ppermute | solution.py:363
  56.5 1.5 copy-start.1
  58.0 1.2 copy-start.3
  59.2 40.5 %copy-start.4 = (bf16[64,7296]{1,0:T(8,128)(2,1)S(1)}, bf16[64,7296]{1,0:T(8,128)(2,1)}, u32[]{:S(2)}) copy-start(bf16[64,7296]{1,0:T(8,128)(2,1)} %get-tuple-element.49.refs_1_) | copy-start | bytes 2801668
  95.8 9.4 %copy-start.2 = (bf16[1,1,1792,512]{3,2,1,0:T(8,128)(2,1)S(1)}, bf16[1,1,1792,512]{3,2,1,0:T(8,128)(2,1)}, u32[]{:S(2)}) copy-start(bf16[1,1,1792,512]{3,2,1,0:T(8,128)(2,1)} %param.11) | copy-start | bytes 5505028
  95.8 3.9 %collective-permute-start.10 = (bf16[1792,512]{1,0:T(8,128)(2,1)S(1)}, bf16[1792,512]{1,0:T(8,128)(2,1)S(1)}, u32[]{:S(2)}, u32[]{:S(2)}) collective-permute-start(bf16[1792,512]{1,0:T(8,128)(2,1)S(1)} %collective-permute-done.refs_4_.refs_8_), channel_id=1, source_target_pairs={{0,2},{2,0},{4,6},{6,4},{8,10},{10,8},{12,14},{14,12},{1,3},{3,1},... | collective-permute-start | bytes 5505032 | tf_op jit(solution)/shard_map/ppermute | solution.py:363
  103.2 36.0 %collective-permute-start.11 = (bf16[64,3712]{1,0:T(8,128)(2,1)S(1)}, bf16[64,3712]{1,0:T(8,128)(2,1)S(1)}, u32[]{:S(2)}, u32[]{:S(2)}) collective-permute-start(bf16[64,3712]{1,0:T(8,128)(2,1)S(1)} %get-tuple-element.57), channel_id=1, source_target_pairs={{0,24},{2,26},{4,28},{6,30},{8,16},{10,18},{12,20},{14,22},{16,8},... | collective-permute-start | bytes 1425416 | tf_op jit(solution)/shard_map/ppermute | solution.py:371
  104.8 34.4 %collective-permute-start.12 = (bf16[64,3712]{1,0:T(8,128)(2,1)S(1)}, bf16[64,3712]{1,0:T(8,128)(2,1)S(1)}, u32[]{:S(2)}, u32[]{:S(2)}) collective-permute-start(bf16[64,3712]{1,0:T(8,128)(2,1)S(1)} %get-tuple-element.58), channel_id=1, source_target_pairs={{0,16},{2,18},{4,20},{6,22},{8,24},{10,26},{12,28},{14,30},{16,0},... | collective-permute-start | bytes 1425416 | tf_op jit(solution)/shard_map/ppermute | solution.py:371
  112.7 26.5 %collective-permute-start.13 = (bf16[64,3712]{1,0:T(8,128)(2,1)S(1)}, bf16[64,3712]{1,0:T(8,128)(2,1)S(1)}, u32[]{:S(2)}, u32[]{:S(2)}) collective-permute-start(bf16[64,3712]{1,0:T(8,128)(2,1)S(1)} %get-tuple-element.61), channel_id=1, source_target_pairs={{0,28},{2,30},{4,24},{6,26},{8,20},{10,22},{12,16},{14,18},{16,12}... | collective-permute-start | bytes 1425416 | tf_op jit(solution)/shard_map/ppermute | solution.py:371
  117.2 31.3 %collective-permute-start.14 = (bf16[64,3712]{1,0:T(8,128)(2,1)S(1)}, bf16[64,3712]{1,0:T(8,128)(2,1)S(1)}, u32[]{:S(2)}, u32[]{:S(2)}) collective-permute-start(bf16[64,3712]{1,0:T(8,128)(2,1)S(1)} %get-tuple-element.62), channel_id=1, source_target_pairs={{0,20},{2,22},{4,16},{6,18},{8,28},{10,30},{12,24},{14,26},{16,4},... | collective-permute-start | bytes 1425416 | tf_op jit(solution)/shard_map/ppermute | solution.py:371

commit v3 on v2

v3 whole, which is shorter than its diff:
```python
import functools

import jax
import jax.numpy as jnp
from jax import lax
from jax.experimental import pallas as pl
from jax.experimental.pallas import tpu as pltpu
from jax.sharding import PartitionSpec as P

LANES = 128
TILE = 256
F32 = jnp.float32
BF16 = jnp.bfloat16
MIB = 1 << 20
CHUNK = 512
PARTS = 4
LIMIT = 57
CUTS = 3


def slots_of(tok_dev, top, experts):
    capacity = min(tok_dev, max(2, tok_dev * top // experts + 1))
    if capacity % 16 == 1 and capacity > 1:
        return capacity - 1, 1
    return -(-capacity // 16) * 16, 0


def fold_columns(pieces, base):
    return -(-(pieces + 1) // base) * LANES


def place_of(piece, base):
    return piece % base, piece // base * LANES


def fold(ext_ref, row, pieces, first, base):
    for k in range(pieces):
        at, column = place_of(first + k, base)
        ext_ref[at : at + 1, column : column + LANES] = row[:, k * LANES : (k + 1) * LANES]


def unfold(row_ref, at_row, ext, pieces, first, base):
    for k in range(pieces):
        at, column = place_of(first + k, base)
        row_ref[at_row : at_row + 1, k * LANES : (k + 1) * LANES] = ext[at : at + 1, column : column + LANES]


def slot_row(ids, expert):
    tokens = ids.shape[1]
    hit = jnp.where(ids == expert, 1.0, 0.0).astype(F32)
    mask = jnp.sum(hit, axis=0, keepdims=True)
    earlier = lax.broadcasted_iota(jnp.int32, (tokens, tokens), 0) < lax.broadcasted_iota(
        jnp.int32, (tokens, tokens), 1
    )
    before = jnp.dot(
        jnp.broadcast_to(mask, (16, tokens)).astype(BF16),
        jnp.where(earlier, 1.0, 0.0).astype(BF16),
        preferred_element_type=F32,
    )[0:1]
    return jnp.where(mask > 0.5, before, -1.0)


def begin(src, dst, sem):
    copy = pltpu.make_async_copy(src, dst, sem)
    copy.start()
    return copy


def finish(copies):
    for copy in copies:
        copy.wait()


def dispatch_kernel(dists, base, extra, ids_hbm, gates_hbm, tok_hbm, grad_hbm, *refs):
    n = len(dists)
    outs, refs = refs[:n], refs[n:]
    ids_ref, gates_ref, tok_ref, grad_ref, msg_ref, ext_ref, sem_i, sem_t, sem_g, sem_o = refs
    here = lax.axis_index("expert") // 2
    tokens, width = tok_ref.shape
    pieces = width // LANES
    rows = base + 16 * extra
    step = tokens // PARTS
    parts = [pl.ds(i * step, step) for i in range(PARTS)]
    small = [begin(ids_hbm, ids_ref, sem_i.at[0]), begin(gates_hbm, gates_ref, sem_i.at[1])]
    tok_in = [begin(tok_hbm.at[p, :], tok_ref.at[p, :], sem_t.at[i]) for i, p in enumerate(parts)]
    grad_in = [begin(grad_hbm.at[p, :], grad_ref.at[p, :], sem_g.at[i]) for i, p in enumerate(parts)]
    finish(small)
    ids, gates = ids_ref[...], gates_ref[...]
    onehots, scales = [], []
    for dist in dists:
        slot = slot_row(ids, here ^ dist)
        gate = jnp.sum(jnp.where(ids == (here ^ dist), gates, 0.0), axis=0, keepdims=True)
        picks = lax.broadcasted_iota(jnp.int32, (rows, tokens), 0).astype(F32) == slot
        onehots.append(jnp.where(picks, 1.0, 0.0).astype(BF16))
        scales.append(jnp.sum(jnp.where(picks, gate, 0.0), axis=1, keepdims=True))
    ext_ref[...] = jnp.zeros_like(ext_ref)
    count = lax.broadcasted_iota(jnp.int32, (16, tokens), 1) + 1
    for d in range(n):
        holders = lax.dot_general(
            count.astype(F32).astype(BF16), onehots[d], (((1,), (1,)), ((), ())), preferred_element_type=F32
        )
        at, column = place_of(2 * pieces * extra, base)
        ext_ref[d, at : at + 1, column : column + rows] = holders[0:1]
    sent = []
    for part, copies in enumerate((tok_in, grad_in)):
        finish(copies)
        for d in range(n):
            for at in range(0, width, CHUNK):
                value = jnp.dot(
                    onehots[d],
                    (grad_ref if part else tok_ref)[:, at : at + CHUNK],
                    preferred_element_type=F32,
                )
                if part:
                    value = value * scales[d]
                msg_ref[d, :, part * width + at : part * width + at + CHUNK] = value[:base].astype(BF16)
                if extra:
                    first = part * pieces + at // LANES
                    fold(ext_ref.at[d], value[base : base + 1], CHUNK // LANES, first, base)
            stop = (part + 1) * width
            if part:
                msg_ref[d, :, stop:] = ext_ref[d].astype(BF16)
                stop = msg_ref.shape[2]
            cols = pl.ds(part * width, stop - part * width)
            sent.append(begin(msg_ref.at[d, :, cols], outs[d].at[:, cols], sem_o.at[d, part]))
    finish(sent)


def dispatch(dists, base, extra, ids_t, gates_t, tok, grad, limit):
    tokens, width = tok.shape
    n, ext = len(dists), fold_columns(2 * width // LANES * extra, base)
    cols = 2 * width + ext
    anywhere = pl.BlockSpec(memory_space=pl.ANY)
    return pl.pallas_call(
        functools.partial(dispatch_kernel, dists, base, extra),
        out_shape=[jax.ShapeDtypeStruct((base, cols), BF16) for _ in dists],
        in_specs=[anywhere] * 4,
        out_specs=[anywhere] * n,
        scratch_shapes=[
            pltpu.VMEM(ids_t.shape, jnp.int32),
            pltpu.VMEM(gates_t.shape, F32),
            pltpu.VMEM((tokens, width), BF16),
            pltpu.VMEM((tokens, width), BF16),
            pltpu.VMEM((n, base, cols), BF16),
            pltpu.VMEM((n, base, ext), F32),
            pltpu.SemaphoreType.DMA((2,)),
            pltpu.SemaphoreType.DMA((PARTS,)),
            pltpu.SemaphoreType.DMA((PARTS,)),
            pltpu.SemaphoreType.DMA((n, 2)),
        ],
        compiler_params=pltpu.CompilerParams(vmem_limit_bytes=limit * MIB),
        cost_estimate=pl.CostEstimate(
            flops=4 * n * (base + 16) * tokens * width,
            bytes_accessed=4 * tokens * width + 2 * n * base * cols,
            transcendentals=0,
        ),
        name="dispatch",
    )(ids_t, gates_t, tok, grad)


def silu_slope(pre):
    sig = jax.nn.sigmoid(pre)
    return sig * (1.0 + pre * (1.0 - sig))


def begin_weights(pieces, layout, whole, sems):
    half = whole.shape[0] // 2
    core = lax.axis_index("expert") % 2
    copies = {}
    for i, (piece, (block, other, row, columns)) in enumerate(zip(pieces, layout)):
        at = pl.multiple_of((1 - core if other else core) * half + row, 16)
        rows = pl.ds(at, piece.shape[0])
        dst = whole.at[rows, pl.ds(block * columns, columns)]
        copies.setdefault(block, []).append(begin(piece, dst, sems.at[i]))
    return copies


def begin_rows(msgs, rows, ext, start, sems, ext_sems):
    base = msgs[0].shape[0]
    width = rows.shape[1]
    copies = []
    for i, msg in enumerate(msgs):
        copies.append(begin(msg.at[:, pl.ds(start, width)], rows.at[pl.ds(i * base, base), :], sems.at[i]))
        if ext is not None:
            copies.append(begin(msg.at[:, pl.ds(2 * width, ext.shape[2])], ext.at[i], ext_sems.at[i]))
    return copies


def put_extra(rows, row32, ext, n, base, first):
    row32[...] = jnp.zeros_like(row32)
    for i in range(n):
        unfold(row32, i, ext[i].astype(F32), rows.shape[1] // LANES, first, base)
    rows[n * base :, :] = row32[...].astype(BF16)


def expert_kernel(n, base, extra, stage, w_layout, v_layout, *refs):
    msgs, refs = refs[:n], refs[n:]
    w_pieces, refs = refs[: len(w_layout)], refs[len(w_layout) :]
    v_pieces, refs = refs[: len(v_layout)], refs[len(v_layout) :]
    if stage == "late":
        slope, partial, refs = refs[0], refs[1], refs[2:]
        outs, refs = refs[:n], refs[n:]
    elif stage == "early":
        slope_late, partial_out, slope, refs = refs[0], refs[1], refs[2], refs[3:]
    else:
        outs, slope, refs = refs[:n], refs[n], refs[n + 1 :]
    w, v, x, g, act, ext, row32, ext32, sem_x, sem_g, sem_e, sem_w, sem_v = refs
    width = w.shape[0]
    half_ff = w_layout[0][3]
    pieces = width // LANES
    full = n * base
    x_in = []
    if stage != "late":
        x_in = begin_rows(msgs, x, ext, 0, sem_x, sem_e)
    w_in = begin_weights(w_pieces, w_layout, w, sem_w)
    g_in = begin_rows(msgs, g, ext if stage == "late" else None, width, sem_g, sem_e)
    v_in = begin_weights(v_pieces, v_layout, v, sem_v)
    if stage != "late":
        finish(x_in)
        if extra:
            put_extra(x, row32, ext, n, base, 0)
        for block in sorted(w_in):
            finish(w_in[block])
            for at in range(block * half_ff, (block + 1) * half_ff, TILE):
                value = silu_slope(jnp.dot(x[...], w[:, at : at + TILE], preferred_element_type=F32))
                if stage == "early" and block > 0:
                    slope_late[:, at - half_ff : at - half_ff + TILE] = value
                else:
                    slope[:, at : at + TILE] = value
    finish(g_in)
    if extra:
        put_extra(g, row32, ext, n, base, pieces)
    for block in sorted(v_in):
        finish(v_in[block])
        for at in range(block * half_ff, (block + 1) * half_ff, TILE):
            hid = jnp.dot(g[...], v[:, at : at + TILE], preferred_element_type=F32)
            act[:, at : at + TILE] = (hid * slope[:, at : at + TILE]).astype(BF16)
    if stage == "late":
        for block in sorted(w_in):
            finish(w_in[block])
    if stage != "early":
        ext32[...] = jnp.zeros_like(ext32)
        (at, column), (to, to_column) = place_of(2 * pieces * extra, base), place_of(pieces * extra, base)
        for i in range(n):
            holders = ext[i].astype(F32)[at : at + 1, column : column + LANES]
            ext32[i, to : to + 1, to_column : to_column + LANES] = holders
    hidden = act.shape[1]
    for at in range(0, width, TILE):
        cols = slice(at, at + TILE)
        back = lax.dot_general(
            act[...], w[cols, :hidden], (((1,), (1,)), ((), ())), preferred_element_type=F32
        )
        if stage == "early":
            partial_out[:, cols] = back
            continue
        if stage == "late":
            back = back + partial[:, cols]
        for i in range(n):
            outs[i][:, cols] = back[i * base : (i + 1) * base].astype(BF16)
            if extra:
                fold(ext32.at[i], back[full + i : full + i + 1], TILE // LANES, at // LANES, base)
    if stage != "early":
        for i in range(n):
            outs[i][:, width:] = ext32[i].astype(BF16)


def expert(msgs, base, extra, w_columns, v_columns, stage="whole", carried=()):
    n = len(msgs)

    def flat(columns):
        arrays, layout = [], []
        for block, cores in enumerate(columns):
            for other, pieces in enumerate(cores):
                row = 0
                for piece in pieces:
                    arrays.append(piece)
                    layout.append((block, other, row, piece.shape[1]))
                    row += piece.shape[0]
        return arrays, layout, row

    w_pieces, w_layout, half = flat(w_columns)
    v_pieces, v_layout, _ = flat(v_columns)
    width, block_ff = 2 * half, w_layout[0][3]
    w_ff, v_ff = len(w_columns) * block_ff, len(v_columns) * block_ff
    rows = n * base + -(-n * extra // 16) * 16
    ext = fold_columns(2 * width // LANES * extra, base)
    back_ext = fold_columns(width // LANES * extra, base)
    cols = width + back_ext
    anywhere, vmem = pl.BlockSpec(memory_space=pl.ANY), pl.BlockSpec(memory_space=pltpu.VMEM)
    spare = max(16, rows - n * base)
    own_slope = [] if stage == "late" else [pltpu.VMEM((rows, v_ff), F32)]
    if stage == "early":
        out_shape = [
            jax.ShapeDtypeStruct((rows, w_ff - block_ff), F32),
            jax.ShapeDtypeStruct((rows, width), F32),
        ]
    else:
        out_shape = [jax.ShapeDtypeStruct((base, cols), BF16) for _ in msgs]
    return pl.pallas_call(
        functools.partial(expert_kernel, n, base, extra, stage, w_layout, v_layout),
        out_shape=out_shape,
        in_specs=[anywhere] * (n + len(w_pieces) + len(v_pieces)) + [vmem] * len(carried),
        out_specs=[vmem] * len(out_shape),
        scratch_shapes=own_slope
        + [
            pltpu.VMEM((width, w_ff), BF16),
            pltpu.VMEM((width, v_ff), BF16),
            pltpu.VMEM((rows, width), BF16),
            pltpu.VMEM((rows, width), BF16),
            pltpu.VMEM((rows, v_ff), BF16),
            pltpu.VMEM((n, base, ext), BF16),
            pltpu.VMEM((spare, width), F32),
            pltpu.VMEM((n, base, back_ext), F32),
            pltpu.SemaphoreType.DMA((n,)),
            pltpu.SemaphoreType.DMA((n,)),
            pltpu.SemaphoreType.DMA((n,)),
            pltpu.SemaphoreType.DMA((len(w_pieces),)),
            pltpu.SemaphoreType.DMA((len(v_pieces),)),
        ],
        compiler_params=pltpu.CompilerParams(vmem_limit_bytes=24 * MIB),
        cost_estimate=pl.CostEstimate(
            flops=0 if stage == "early" else 2 * rows * width * (w_ff + 2 * v_ff),
            bytes_accessed=0 if stage == "early" else 2 * width * (w_ff + v_ff) + 6 * rows * width,
            transcendentals=0 if stage == "early" else rows * w_ff,
        ),
        name="expert_" + stage,
    )(*msgs, *w_pieces, *v_pieces, *carried)


def add_kernel(n, extra, start_ref, *refs):
    msgs, (out, rows, ext, row32, places, sem_b, sem_e) = refs[:n], refs[n:]
    tokens, width = start_ref.shape
    base = ext.shape[1]
    pieces = width // LANES
    copies = []
    for i, msg in enumerate(msgs):
        copies.append(begin(msg.at[:, pl.ds(width, ext.shape[2])], ext.at[i], sem_e.at[i]))
    rows_in = [
        begin(msg.at[:, pl.ds(0, width)], rows.at[pl.ds(i * base, base), :], sem_b.at[i])
        for i, msg in enumerate(msgs)
    ]
    finish(copies)
    folded = jnp.zeros((tokens, 16), F32)
    at, column = place_of(pieces * extra, base)
    for i in range(n):
        holders = ext[i].astype(F32)[at : at + 1, column : column + LANES]
        token = lax.broadcasted_iota(jnp.int32, (tokens, LANES), 0) + 1
        place = jnp.where(holders == token.astype(F32), 1.0, 0.0)
        places[:, i * base : (i + 1) * base] = place[:, :base].astype(BF16)
        if extra:
            mine = lax.broadcasted_iota(jnp.int32, (tokens, 16), 1) == i
            folded = folded + jnp.where(mine, place[:, base : base + 1], 0.0)
    if extra:
        places[:, n * base :] = folded.astype(BF16)
        put_extra(rows, row32, ext, n, base, 0)
    finish(rows_in)
    place = places[...]
    for at in range(0, width, CHUNK):
        cols = slice(at, at + CHUNK)
        back = jnp.dot(place, rows[:, cols], preferred_element_type=F32)
        out[:, cols] = (start_ref[:, cols].astype(F32) + back).astype(out.dtype)


def add_returned(start, msgs, extra, kind, name):
    tokens, width = start.shape
    n, base = len(msgs), msgs[0].shape[0]
    slots = n * base + 16 * extra
    anywhere, vmem = pl.BlockSpec(memory_space=pl.ANY), pl.BlockSpec(memory_space=pltpu.VMEM)
    return pl.pallas_call(
        functools.partial(add_kernel, n, extra),
        out_shape=jax.ShapeDtypeStruct((tokens, width), kind),
        in_specs=[vmem] + [anywhere] * n,
        out_specs=vmem,
        scratch_shapes=[
            pltpu.VMEM((slots, width), BF16),
            pltpu.VMEM((n, base, msgs[0].shape[1] - width), BF16),
            pltpu.VMEM((16, width), F32),
            pltpu.VMEM((tokens, slots), BF16),
            pltpu.SemaphoreType.DMA((n,)),
            pltpu.SemaphoreType.DMA((n,)),
        ],
        compiler_params=pltpu.CompilerParams(vmem_limit_bytes=24 * MIB),
        cost_estimate=pl.CostEstimate(
            flops=2 * slots * tokens * width,
            bytes_accessed=2 * slots * width + 6 * tokens * width,
            transcendentals=0,
        ),
        name=name,
    )(start, *msgs)


def swap(value, axis, apart):
    return lax.ppermute(value, axis, [(i, i ^ apart) for i in range(lax.axis_size(axis))])


def swap_back(value, apart):
    sections, places = lax.axis_size("section"), lax.axis_size("expert")
    pairs = [
        (s * places + i, (s ^ 1) * places + (i ^ apart)) for s in range(sections) for i in range(places)
    ]
    return lax.ppermute(value, ("section", "expert"), pairs)


def after(*values):
    return lax.optimization_barrier(values)


def cut(weight):
    step = -(-weight.shape[0] // (16 * CUTS)) * 16
    return [weight[at : at + step] for at in range(0, weight.shape[0], step)]


def groups_of(experts):
    if experts == 4:
        return [[2], [1, 0], [3]], [[2, 0], [3, 1]]
    order = list(range(experts - 1, -1, -1))
    size = -(-experts // 4)
    groups = [order[i : i + size] for i in range(0, experts, size)]
    return groups, groups


def body(tokens, grad_out, expert_ids, gate_values, w_in, w_out_t):
    tok, grad = tokens[0], grad_out[0]
    ids_t, gates_t = expert_ids[0].T, gate_values[0].T
    experts = lax.axis_size("expert") // 2
    base, extra = slots_of(tok.shape[0], ids_t.shape[0], experts)
    sends, works = groups_of(experts)
    others = range(1, lax.axis_size("dp"))
    w_own, v_own = w_in[0, 0], w_out_t[0, 0]
    sent = [
        dispatch(group, base, extra, ids_t, gates_t, tok, grad, 24 if i else LIMIT)
        for i, group in enumerate(sends)
    ]
    w_far = [swap(w_own, "dp", apart) for apart in others]
    w_other, v_other = swap(w_own, "expert", 1), swap(v_own, "expert", 1)
    other_grad = swap(grad, "section", 1)
    v_late, w_other, v_other = after(v_own, w_other, v_other)
    v_far = [swap(v_late, "dp", apart) for apart in others]
    sent[-1], other_grad = after(sent[-1], other_grad)
    got = {}
    for group, msgs in zip(sends, sent):
        for dist, msg in zip(group, msgs):
            got[dist] = swap(msg, "expert", 2 * dist) if dist else msg
    first, last = [dist for group in sends[:-1] for dist in group], sends[-1]

    w_far, heads = after(w_far, [got[dist] for dist in first])
    got.update(zip(first, heads))
    w_columns = [[[w_own], [w_other]]]
    w_columns += [[[block], [swap(piece, "expert", 1) for piece in cut(block)]] for block in w_far]
    v_columns = [[[v_own], [v_other]]]
    carried = expert([got[dist] for dist in works[0]], base, extra, w_columns, v_columns, "early")
    v_far, tails, carried = after(v_far, [got[dist] for dist in last], carried)
    got.update(zip(last, tails))
    v_columns += [[[block], [swap(block, "expert", 1)]] for block in v_far]

    total = other_grad
    for i, group in enumerate(works):
        msgs = [got[dist] for dist in group]
        if i == 0:
            backs = expert(msgs, base, extra, w_columns[1:], v_columns[1:], "late", carried)
            backs, got = after(backs, got)
        else:
            backs = expert(msgs, base, extra, w_columns, v_columns)
        returned = [swap_back(back, 2 * dist) for dist, back in zip(group, backs)]
        ends = i == len(works) - 1
        total = add_returned(total, returned, extra, BF16 if ends else F32, "finish" if ends else "settle")
    return total[None]


def solution(mesh):
    rows = P("section", ("expert", "dp"), None)
    weights = P("section", "expert", None, "dp")
    return jax.shard_map(
        body,
        mesh=mesh,
        in_specs=(rows, rows, rows, rows, weights, weights),
        out_specs=rows,
        check_vma=False,
    )
```

time: 152 us -> 145 us (0.954)
  waiting for transfers between devices: 100 us -> 90.6 us
  starting transfers between devices: 18.9 us -> 25.4 us
  local copies, waits for them, and re-layouts: 2.7 us -> 0.14 us
    ppermute x11 -> x12, waiting for transfers between devices: 69.1 us -> 58.6 us  [swap(): lax.ppermute(value, axis, [(i, i ^ apart) for i in range(lax.axis_size(ax...]
    ppermute x4, starting transfers between devices: 6.59 us -> 11 us  [swap_back(): return lax.ppermute(value, ('section', 'expert'), pairs)]
    unnamed x12, local copies, waits for them, and re-layouts: 2.7 us -> 0.02 us
    ppermute x11 -> x12, starting transfers between devices: 12.3 us -> 14.4 us  [swap(): lax.ppermute(value, axis, [(i, i ^ apart) for i in range(lax.axis_size(ax...]
    pallas_call x1 -> x2, Pallas kernels: 3.04 us -> 2.26 us  [add_returned(): pl.pallas_call(functools.partial(add_kernel, n, extra), out_shape=jax.Sha...]
  transfers between devices with their start and end apart: 15 -> 16, of which waited for: 6 -> 7; matrix products, arithmetic and copies ran while one was open for 0% -> 0% of each run, Pallas kernels for 13% -> 17%
where the time goes in v3:
time: 145 us
  waiting for transfers between devices  90.6 us (62%)
  Pallas kernels  29.1 us (20%)
  starting transfers between devices  25.4 us (18%)
    ppermute x12, waiting for transfers between devices, swap(): lax.ppermute(value, axis, [(i, i ^ apart) for i in range(lax.axis_size(ax...  58.6 us
    ppermute x4, waiting for transfers between devices, swap_back(): return lax.ppermute(value, ('section', 'expert'), pairs)  32 us
    pallas_call x3, Pallas kernels, expert(): pl.pallas_call(functools.partial(expert_kernel, n, base, extra, stage, w_...  16.1 us
    ppermute x12, starting transfers between devices, swap(): lax.ppermute(value, axis, [(i, i ^ apart) for i in range(lax.axis_size(ax...  14.4 us
    ppermute x4, starting transfers between devices, swap_back(): return lax.ppermute(value, ('section', 'expert'), pairs)  11 us
    pallas_call x3, Pallas kernels, dispatch(): pl.pallas_call(functools.partial(dispatch_kernel, dists, base, extra), ou...  10.7 us
  transfers between devices with their start and end apart: 16, of which 7 were waited for; matrix products, arithmetic and copies ran while one was open for 0% of the time, Pallas kernels for 17%

profile of v3, /device:TPU:0, one launch (start us, length us, event | category | flops | bytes accessed | tf_op | source)
XLA Modules:
  0.0 145.3 jit_solution(9446635578713843509)
XLA Ops:
  0.0 0.0 copy-start.1
  0.0 0.0 copy-start.5
  0.0 0.0 copy-start.4
  0.0 0.0 copy-start
  0.0 0.5 collective-permute-start.7
  0.5 0.1 collective-permute-start.8
  0.6 2.9 %collective-permute-start.1 = (bf16[1792,512]{1,0:T(8,128)(2,1)}, bf16[1792,512]{1,0:T(8,128)(2,1)S(1)}, u32[]{:S(2)}, u32[]{:S(2)}) collective-permute-start(bf16[1792,512]{1,0:T(8,128)(2,1)} %bitcast.19), channel_id=1, source_target_pairs={{0,1},{1,0},{2,3},{3,2},{4,5},{5,4},{6,7},{7,6},{8,9},{9,8},{10,11... | collective-permute-start | bytes 5505032 | tf_op jit(solution)/shard_map/ppermute | solution.py:393
  3.6 1.5 %collective-permute-start = (bf16[128,3584]{1,0:T(8,128)(2,1)}, bf16[128,3584]{1,0:T(8,128)(2,1)S(1)}, u32[]{:S(2)}, u32[]{:S(2)}) collective-permute-start(bf16[128,3584]{1,0:T(8,128)(2,1)} %bitcast.14), channel_id=1, source_target_pairs={{0,16},{16,0},{1,17},{17,1},{2,18},{18,2},{3,19},{19,3},{4,20},{20... | collective-permute-start | bytes 2752520 | tf_op jit(solution)/shard_map/ppermute | solution.py:393
  5.1 3.1 %dispatch.4 = bf16[64,7296]{1,0:T(8,128)(2,1)} custom-call(s32[2,128]{1,0:T(2,128)} %bitcast.26, f32[2,128]{1,0:T(2,128)} %bitcast.29, bf16[128,3584]{1,0:T(8,128)(2,1)} %bitcast.11, bf16[128,3584]{1,0:T(8,128)(2,1)} %bitcast.15), custom_call_target="tpu_custom_call" | custom-call | flops 146800640 | bytes 2768896 | tf_op jit(solution)/shard_map/dispatch/pallas_call | solution.py:134
  8.1 2.6 %collective-permute-start.2 = (bf16[64,7296]{1,0:T(8,128)(2,1)}, bf16[64,7296]{1,0:T(8,128)(2,1)S(1)}, u32[]{:S(2)}, u32[]{:S(2)}) collective-permute-start(bf16[64,7296]{1,0:T(8,128)(2,1)} %dispatch.4), channel_id=1, source_target_pairs={{0,8},{2,10},{4,12},{6,14},{8,0},{10,2},{12,4},{14,6},{1,9},{3,11}... | collective-permute-start | bytes 2801672 | tf_op jit(solution)/shard_map/ppermute | solution.py:393
  10.8 0.0 collective-permute-done.7.refs_3_
  10.8 0.0 collective-permute-done.8.refs_9_
  10.8 0.5 collective-permute-start.9
  11.3 0.0 copy-done.1
  11.3 0.0 copy-done.5
  11.3 0.0 copy-done.4
  11.3 0.0 copy-done
  11.3 4.2 %dispatch.5 = (bf16[64,7296]{1,0:T(8,128)(2,1)S(1)}, bf16[64,7296]{1,0:T(8,128)(2,1)S(1)}) custom-call(s32[2,128]{1,0:T(2,128)S(1)} %bitcast.27, f32[2,128]{1,0:T(2,128)S(1)} %bitcast.30, bf16[128,3584]{1,0:T(8,128)(2,1)S(1)} %bitcast.12, bf16[128,3584]{1,0:T(8,128)(2,1)S(1)} %bitcast.16), custom_call_target="tpu_custom_call" | custom-call | flops 293601280 | bytes 3702784 | tf_op jit(solution)/shard_map/dispatch/pallas_call | solution.py:134
  15.5 1.6 %collective-permute-start.3 = (bf16[64,7296]{1,0:T(8,128)(2,1)S(1)}, bf16[64,7296]{1,0:T(8,128)(2,1)S(1)}, u32[]{:S(2)}, u32[]{:S(2)}) collective-permute-start(bf16[64,7296]{1,0:T(8,128)(2,1)S(1)} %get-tuple-element.31), channel_id=1, source_target_pairs={{0,4},{2,6},{4,0},{6,2},{8,12},{10,14},{12,8},{14,10},{1,5},{3,7},... | collective-permute-start | bytes 2801672 | tf_op jit(solution)/shard_map/ppermute | solution.py:393
  17.2 3.4 %dispatch.3 = bf16[64,7296]{1,0:T(8,128)(2,1)S(1)} custom-call(s32[2,128]{1,0:T(2,128)S(1)} %bitcast.28, f32[2,128]{1,0:T(2,128)S(1)} %bitcast.31, bf16[128,3584]{1,0:T(8,128)(2,1)S(1)} %bitcast.13, bf16[128,3584]{1,0:T(8,128)(2,1)S(1)} %bitcast.17), custom_call_target="tpu_custom_call" | custom-call | flops 146800640 | bytes 2768896 | tf_op jit(solution)/shard_map/dispatch/pallas_call | solution.py:134
  20.6 5.2 %collective-permute-done.start_ref = bf16[128,3584]{1,0:T(8,128)(2,1)S(1)} collective-permute-done((bf16[128,3584]{1,0:T(8,128)(2,1)}, bf16[128,3584]{1,0:T(8,128)(2,1)S(1)}, u32[]{:S(2)}, u32[]{:S(2)}) %collective-permute-start) | collective-permute-done | bytes 917536 | tf_op jit(solution)/shard_map/ppermute | solution.py:393
  25.8 3.6 %collective-permute-start.10 = (bf16[64,7296]{1,0:T(8,128)(2,1)S(1)}, bf16[64,7296]{1,0:T(8,128)(2,1)S(1)}, u32[]{:S(2)}, u32[]{:S(2)}) collective-permute-start(bf16[64,7296]{1,0:T(8,128)(2,1)S(1)} %dispatch.3), channel_id=1, source_target_pairs={{0,12},{2,14},{4,8},{6,10},{8,4},{10,6},{12,0},{14,2},{1,13},{3,15... | collective-permute-start | bytes 2801672 | tf_op jit(solution)/shard_map/ppermute | solution.py:393
  29.4 43.3 %collective-permute-done.2.refs_0_ = bf16[64,7296]{1,0:T(8,128)(2,1)S(1)} collective-permute-done((bf16[64,7296]{1,0:T(8,128)(2,1)}, bf16[64,7296]{1,0:T(8,128)(2,1)S(1)}, u32[]{:S(2)}, u32[]{:S(2)}) %collective-permute-start.2) | collective-permute-done | bytes 933920 | tf_op jit(solution)/shard_map/ppermute | solution.py:393
  72.7 3.4 %collective-permute-done.3.refs_1_ = bf16[64,7296]{1,0:T(8,128)(2,1)S(1)} collective-permute-done((bf16[64,7296]{1,0:T(8,128)(2,1)S(1)}, bf16[64,7296]{1,0:T(8,128)(2,1)S(1)}, u32[]{:S(2)}, u32[]{:S(2)}) %collective-permute-start.3) | collective-permute-done | bytes 933920 | tf_op jit(solution)/shard_map/ppermute | solution.py:393
  76.1 0.0 collective-permute-done.1.refs_4_.refs_2_
  76.1 0.0 copy-start.2
  76.1 0.0 copy-start.3
  76.1 0.1 fusion
  76.1 0.1 collective-permute-start.5
  76.2 0.5 collective-permute-start.4
  76.8 0.1 collective-permute-start.6
  76.9 3.1 %collective-permute-done.6.refs_7_.refs_5_ = bf16[576,512]{1,0:T(8,128)(2,1)S(1)} collective-permute-done((bf16[576,512]{1,0:T(8,128)(2,1)S(1)}, bf16[576,512]{1,0:T(8,128)(2,1)S(1)}, u32[]{:S(2)}, u32[]{:S(2)}) %collective-permute-start.6) | collective-permute-done | bytes 589856 | tf_op jit(solution)/shard_map/ppermute | solution.py:393
  80.0 0.0 collective-permute-done.5.refs_6_.refs_4_
  80.0 0.0 collective-permute-done.4.refs_5_.refs_3_
  80.0 0.0 copy-done.2
  80.0 0.0 copy-done.3
  80.0 5.2 %expert_early.1 = (f32[144,512]{1,0:T(8,128)S(1)}, f32[144,3584]{1,0:T(8,128)S(1)}) custom-call(bf16[64,7296]{1,0:T(8,128)(2,1)S(1)} %collective-permute-done.2.refs_0_, bf16[64,7296]{1,0:T(8,128)(2,1)S(1)} %get-tuple-element.34.refs_1_, bf16[1792,512]{1,0:T(8,128)(2,1)S(1)} %bitcast.20, bf16[1792,512]{1,0:T(8,128)(2,1)S(1)} %collective-permute-done.7.refs_3_, ...), custom_call_target="tpu_custom_call" | custom-call | tf_op jit(solution)/shard_map/expert_early/pallas_call | solution.py:299
  85.2 0.0 collective-permute-done.10.refs_0_
  85.2 0.0 collective-permute-done.9.refs_6_.refs_10_
  85.2 0.2 collective-permute-start.11
  85.4 3.6 %collective-permute-done.11.refs_7_.refs_11_ = bf16[1792,512]{1,0:T(8,128)(2,1)S(1)} collective-permute-done((bf16[1792,512]{1,0:T(8,128)(2,1)S(1)}, bf16[1792,512]{1,0:T(8,128)(2,1)S(1)}, u32[]{:S(2)}, u32[]{:S(2)}) %collective-permute-start.11) | collective-permute-done | bytes 1835040 | tf_op jit(solution)/shard_map/ppermute | solution.py:393
  89.1 3.1 %expert_late.1 = (bf16[64,3712]{1,0:T(8,128)(2,1)S(1)}, bf16[64,3712]{1,0:T(8,128)(2,1)S(1)}) custom-call(bf16[64,7296]{1,0:T(8,128)(2,1)S(1)} %collective-permute-done.2.refs_0_, bf16[64,7296]{1,0:T(8,128)(2,1)S(1)} %get-tuple-element.34.refs_1_, bf16[1792,512]{1,0:T(8,128)(2,1)S(1)} %collective-permute-done.1.refs_4_.refs_2_, ...), custom_call_target="tpu_custom_call" | custom-call | flops 1585446912 | bytes 10436608 | tf_op jit(solution)/shard_map/expert_late/pallas_call | solution.py:299
  92.2 8.8 %collective-permute-start.12 = (bf16[64,3712]{1,0:T(8,128)(2,1)S(1)}, bf16[64,3712]{1,0:T(8,128)(2,1)S(1)}, u32[]{:S(2)}, u32[]{:S(2)}) collective-permute-start(bf16[64,3712]{1,0:T(8,128)(2,1)S(1)} %get-tuple-element.49), channel_id=1, source_target_pairs={{0,24},{2,26},{4,28},{6,30},{8,16},{10,18},{12,20},{14,22},{16,8},... | collective-permute-start | bytes 1425416 | tf_op jit(solution)/shard_map/ppermute | solution.py:401
  101.1 1.5 %collective-permute-start.13 = (bf16[64,3712]{1,0:T(8,128)(2,1)S(1)}, bf16[64,3712]{1,0:T(8,128)(2,1)S(1)}, u32[]{:S(2)}, u32[]{:S(2)}) collective-permute-start(bf16[64,3712]{1,0:T(8,128)(2,1)S(1)} %get-tuple-element.50), channel_id=1, source_target_pairs={{0,16},{2,18},{4,20},{6,22},{8,24},{10,26},{12,28},{14,30},{16,0},... | collective-permute-start | bytes 1425416 | tf_op jit(solution)/shard_map/ppermute | solution.py:401
  102.5 7.8 %expert_whole.1 = (bf16[64,3712]{1,0:T(8,128)(2,1)S(1)}, bf16[64,3712]{1,0:T(8,128)(2,1)S(1)}) custom-call(bf16[64,7296]{1,0:T(8,128)(2,1)S(1)} %collective-permute-done.10.refs_0_, bf16[64,7296]{1,0:T(8,128)(2,1)S(1)} %collective-permute-done.3.refs_1_, bf16[1792,512]{1,0:T(8,128)(2,1)S(1)} %bitcast.21, ...), custom_call_target="tpu_custom_call" | custom-call | flops 3170893824 | bytes 17776640 | tf_op jit(solution)/shard_map/expert_whole/pallas_call | solution.py:299
  110.4 0.5 collective-permute-start.14
  110.9 0.2 collective-permute-start.15
  111.1 22.2 %collective-permute-done.12.refs_0_ = bf16[64,3712]{1,0:T(8,128)(2,1)S(1)} collective-permute-done((bf16[64,3712]{1,0:T(8,128)(2,1)S(1)}, bf16[64,3712]{1,0:T(8,128)(2,1)S(1)}, u32[]{:S(2)}, u32[]{:S(2)}) %collective-permute-start.12) | collective-permute-done | bytes 475168 | tf_op jit(solution)/shard_map/ppermute | solution.py:401
  133.2 9.8 %collective-permute-done.13.refs_1_ = bf16[64,3712]{1,0:T(8,128)(2,1)S(1)} collective-permute-done((bf16[64,3712]{1,0:T(8,128)(2,1)S(1)}, bf16[64,3712]{1,0:T(8,128)(2,1)S(1)}, u32[]{:S(2)}, u32[]{:S(2)}) %collective-permute-start.13) | collective-permute-done | bytes 475168 | tf_op jit(solution)/shard_map/ppermute | solution.py:401
  143.0 0.7 settle.1.start_ref
  143.7 0.0 collective-permute-done.14.refs_0_
  143.7 0.0 collective-permute-done.15.refs_1_
  143.7 1.6 %finish.1 = bf16[128,3584]{1,0:T(8,128)(2,1)} custom-call(f32[128,3584]{1,0:T(8,128)S(1)} %settle.1.start_ref, bf16[64,3712]{1,0:T(8,128)(2,1)S(1)} %collective-permute-done.14.refs_0_, bf16[64,3712]{1,0:T(8,128)(2,1)S(1)} %collective-permute-done.15.refs_1_), custom_call_target="tpu_custom_call" | custom-call | flops 132120576 | bytes 3784704 | tf_op jit(solution)/shard_map/finish/pallas_call | solution.py:369
  (1 shorter events, 0.0 us)
Async XLA Ops:
  0.0 11.3 %copy-start.1 = (bf16[1,128,3584]{2,1,0:T(8,128)(2,1)S(1)}, bf16[1,128,3584]{2,1,0:T(8,128)(2,1)}, u32[]{:S(2)}) copy-start(bf16[1,128,3584]{2,1,0:T(8,128)(2,1)} %param.7) | copy-start | bytes 2752516
  0.0 11.3 %copy-start.5 = (f32[1,128,2]{1,2,0:T(2,128)S(1)}, f32[1,128,2]{1,2,0:T(2,128)}, u32[]{:S(2)}) copy-start(f32[1,128,2]{1,2,0:T(2,128)} %param.9) | copy-start | bytes 3076
  0.0 11.3 %copy-start.4 = (s32[1,128,2]{1,2,0:T(2,128)S(1)}, s32[1,128,2]{1,2,0:T(2,128)}, u32[]{:S(2)}) copy-start(s32[1,128,2]{1,2,0:T(2,128)} %param.8) | copy-start | bytes 3076
  0.0 11.3 %copy-start = (bf16[1,128,3584]{2,1,0:T(8,128)(2,1)S(1)}, bf16[1,128,3584]{2,1,0:T(8,128)(2,1)}, u32[]{:S(2)}) copy-start(bf16[1,128,3584]{2,1,0:T(8,128)(2,1)} %param.6) | copy-start | bytes 2752516
  0.0 10.8 %collective-permute-start.7 = (bf16[1792,512]{1,0:T(8,128)(2,1)}, bf16[1792,512]{1,0:T(8,128)(2,1)S(1)}, u32[]{:S(2)}, u32[]{:S(2)}) collective-permute-start(bf16[1792,512]{1,0:T(8,128)(2,1)} %bitcast.18), channel_id=1, source_target_pairs={{0,2},{2,0},{4,6},{6,4},{8,10},{10,8},{12,14},{14,12},{1,3},{3,1},... | collective-permute-start | bytes 5505032 | tf_op jit(solution)/shard_map/ppermute | solution.py:393
  0.5 10.2 %collective-permute-start.8 = (bf16[1792,512]{1,0:T(8,128)(2,1)}, bf16[1792,512]{1,0:T(8,128)(2,1)}, u32[]{:S(2)}, u32[]{:S(2)}) collective-permute-start(bf16[1792,512]{1,0:T(8,128)(2,1)} %bitcast.22), channel_id=1, source_target_pairs={{0,2},{2,0},{4,6},{6,4},{8,10},{10,8},{12,14},{14,12},{1,3},{3,1},... | collective-permute-start | bytes 5505032 | tf_op jit(solution)/shard_map/ppermute | solution.py:393
  0.6 75.4 %collective-permute-start.1 = (bf16[1792,512]{1,0:T(8,128)(2,1)}, bf16[1792,512]{1,0:T(8,128)(2,1)S(1)}, u32[]{:S(2)}, u32[]{:S(2)}) collective-permute-start(bf16[1792,512]{1,0:T(8,128)(2,1)} %bitcast.19), channel_id=1, source_target_pairs={{0,1},{1,0},{2,3},{3,2},{4,5},{5,4},{6,7},{7,6},{8,9},{9,8},{10,11... | collective-permute-start | bytes 5505032 | tf_op jit(solution)/shard_map/ppermute | solution.py:393
  3.6 22.3 %collective-permute-start = (bf16[128,3584]{1,0:T(8,128)(2,1)}, bf16[128,3584]{1,0:T(8,128)(2,1)S(1)}, u32[]{:S(2)}, u32[]{:S(2)}) collective-permute-start(bf16[128,3584]{1,0:T(8,128)(2,1)} %bitcast.14), channel_id=1, source_target_pairs={{0,16},{16,0},{1,17},{17,1},{2,18},{18,2},{3,19},{19,3},{4,20},{20... | collective-permute-start | bytes 2752520 | tf_op jit(solution)/shard_map/ppermute | solution.py:393
  8.1 64.6 %collective-permute-start.2 = (bf16[64,7296]{1,0:T(8,128)(2,1)}, bf16[64,7296]{1,0:T(8,128)(2,1)S(1)}, u32[]{:S(2)}, u32[]{:S(2)}) collective-permute-start(bf16[64,7296]{1,0:T(8,128)(2,1)} %dispatch.4), channel_id=1, source_target_pairs={{0,8},{2,10},{4,12},{6,14},{8,0},{10,2},{12,4},{14,6},{1,9},{3,11}... | collective-permute-start | bytes 2801672 | tf_op jit(solution)/shard_map/ppermute | solution.py:393
  10.8 74.5 %collective-permute-start.9 = (bf16[1792,512]{1,0:T(8,128)(2,1)}, bf16[1792,512]{1,0:T(8,128)(2,1)S(1)}, u32[]{:S(2)}, u32[]{:S(2)}) collective-permute-start(bf16[1792,512]{1,0:T(8,128)(2,1)} %bitcast.23), channel_id=1, source_target_pairs={{0,1},{1,0},{2,3},{3,2},{4,5},{5,4},{6,7},{7,6},{8,9},{9,8},{10,11... | collective-permute-start | bytes 5505032 | tf_op jit(solution)/shard_map/ppermute | solution.py:393
  15.5 60.5 %collective-permute-start.3 = (bf16[64,7296]{1,0:T(8,128)(2,1)S(1)}, bf16[64,7296]{1,0:T(8,128)(2,1)S(1)}, u32[]{:S(2)}, u32[]{:S(2)}) collective-permute-start(bf16[64,7296]{1,0:T(8,128)(2,1)S(1)} %get-tuple-element.31), channel_id=1, source_target_pairs={{0,4},{2,6},{4,0},{6,2},{8,12},{10,14},{12,8},{14,10},{1,5},{3,7},... | collective-permute-start | bytes 2801672 | tf_op jit(solution)/shard_map/ppermute | solution.py:393
  25.8 59.4 %collective-permute-start.10 = (bf16[64,7296]{1,0:T(8,128)(2,1)S(1)}, bf16[64,7296]{1,0:T(8,128)(2,1)S(1)}, u32[]{:S(2)}, u32[]{:S(2)}) collective-permute-start(bf16[64,7296]{1,0:T(8,128)(2,1)S(1)} %dispatch.3), channel_id=1, source_target_pairs={{0,12},{2,14},{4,8},{6,10},{8,4},{10,6},{12,0},{14,2},{1,13},{3,15... | collective-permute-start | bytes 2801672 | tf_op jit(solution)/shard_map/ppermute | solution.py:393
  76.1 4.0 %copy-start.2 = (bf16[1,1,1792,512]{3,2,1,0:T(8,128)(2,1)S(1)}, bf16[1,1,1792,512]{3,2,1,0:T(8,128)(2,1)}, u32[]{:S(2)}) copy-start(bf16[1,1,1792,512]{3,2,1,0:T(8,128)(2,1)} %param.10) | copy-start | bytes 5505028
  76.1 4.0 %copy-start.3 = (bf16[1,1,1792,512]{3,2,1,0:T(8,128)(2,1)S(1)}, bf16[1,1,1792,512]{3,2,1,0:T(8,128)(2,1)}, u32[]{:S(2)}) copy-start(bf16[1,1,1792,512]{3,2,1,0:T(8,128)(2,1)} %param.11) | copy-start | bytes 5505028
  76.1 3.9 %collective-permute-start.5 = (bf16[608,512]{1,0:T(8,128)(2,1)S(1)}, bf16[608,512]{1,0:T(8,128)(2,1)S(1)}, u32[]{:S(2)}, u32[]{:S(2)}) collective-permute-start(bf16[608,512]{1,0:T(8,128)(2,1)S(1)} %get-tuple-element.55), channel_id=1, source_target_pairs={{0,2},{2,0},{4,6},{6,4},{8,10},{10,8},{12,14},{14,12},{1,3},{3,1},... | collective-permute-start | bytes 1867784 | tf_op jit(solution)/shard_map/ppermute | solution.py:393
  76.2 3.8 %collective-permute-start.4 = (bf16[608,512]{1,0:T(8,128)(2,1)S(1)}, bf16[608,512]{1,0:T(8,128)(2,1)S(1)}, u32[]{:S(2)}, u32[]{:S(2)}) collective-permute-start(bf16[608,512]{1,0:T(8,128)(2,1)S(1)} %get-tuple-element.56), channel_id=1, source_target_pairs={{0,2},{2,0},{4,6},{6,4},{8,10},{10,8},{12,14},{14,12},{1,3},{3,1},... | collective-permute-start | bytes 1867784 | tf_op jit(solution)/shard_map/ppermute | solution.py:393
  76.8 3.2 %collective-permute-start.6 = (bf16[576,512]{1,0:T(8,128)(2,1)S(1)}, bf16[576,512]{1,0:T(8,128)(2,1)S(1)}, u32[]{:S(2)}, u32[]{:S(2)}) collective-permute-start(bf16[576,512]{1,0:T(8,128)(2,1)S(1)} %slice.11), channel_id=1, source_target_pairs={{0,2},{2,0},{4,6},{6,4},{8,10},{10,8},{12,14},{14,12},{1,3},{3,1},... | collective-permute-start | bytes 1769480 | tf_op jit(solution)/shard_map/ppermute | solution.py:393
  85.2 3.9 %collective-permute-start.11 = (bf16[1792,512]{1,0:T(8,128)(2,1)S(1)}, bf16[1792,512]{1,0:T(8,128)(2,1)S(1)}, u32[]{:S(2)}, u32[]{:S(2)}) collective-permute-start(bf16[1792,512]{1,0:T(8,128)(2,1)S(1)} %collective-permute-done.9.refs_6_.refs_10_), channel_id=1, source_target_pairs={{0,2},{2,0},{4,6},{6,4},{8,10},{10,8},{12,14},{14,12},{1,3},{3,1},... | collective-permute-start | bytes 5505032 | tf_op jit(solution)/shard_map/ppermute | solution.py:393
  92.2 41.0 %collective-permute-start.12 = (bf16[64,3712]{1,0:T(8,128)(2,1)S(1)}, bf16[64,3712]{1,0:T(8,128)(2,1)S(1)}, u32[]{:S(2)}, u32[]{:S(2)}) collective-permute-start(bf16[64,3712]{1,0:T(8,128)(2,1)S(1)} %get-tuple-element.49), channel_id=1, source_target_pairs={{0,24},{2,26},{4,28},{6,30},{8,16},{10,18},{12,20},{14,22},{16,8},... | collective-permute-start | bytes 1425416 | tf_op jit(solution)/shard_map/ppermute | solution.py:401
  101.1 42.0 %collective-permute-start.13 = (bf16[64,3712]{1,0:T(8,128)(2,1)S(1)}, bf16[64,3712]{1,0:T(8,128)(2,1)S(1)}, u32[]{:S(2)}, u32[]{:S(2)}) collective-permute-start(bf16[64,3712]{1,0:T(8,128)(2,1)S(1)} %get-tuple-element.50), channel_id=1, source_target_pairs={{0,16},{2,18},{4,20},{6,22},{8,24},{10,26},{12,28},{14,30},{16,0},... | collective-permute-start | bytes 1425416 | tf_op jit(solution)/shard_map/ppermute | solution.py:401
  110.4 33.4 %collective-permute-start.14 = (bf16[64,3712]{1,0:T(8,128)(2,1)S(1)}, bf16[64,3712]{1,0:T(8,128)(2,1)S(1)}, u32[]{:S(2)}, u32[]{:S(2)}) collective-permute-start(bf16[64,3712]{1,0:T(8,128)(2,1)S(1)} %get-tuple-element.53), channel_id=1, source_target_pairs={{0,28},{2,30},{4,24},{6,26},{8,20},{10,22},{12,16},{14,18},{16,12}... | collective-permute-start | bytes 1425416 | tf_op jit(solution)/shard_map/ppermute | solution.py:401
  110.9 32.8 %collective-permute-start.15 = (bf16[64,3712]{1,0:T(8,128)(2,1)S(1)}, bf16[64,3712]{1,0:T(8,128)(2,1)S(1)}, u32[]{:S(2)}, u32[]{:S(2)}) collective-permute-start(bf16[64,3712]{1,0:T(8,128)(2,1)S(1)} %get-tuple-element.54), channel_id=1, source_target_pairs={{0,20},{2,22},{4,16},{6,18},{8,28},{10,30},{12,24},{14,26},{16,4},... | collective-permute-start | bytes 1425416 | tf_op jit(solution)/shard_map/ppermute | solution.py:401

commit v4 on v3

--- a/solution.py
+++ b/solution.py
@@ -15,6 +15,7 @@
 CHUNK = 512
 PARTS = 4
 LIMIT = 57
+TAIL = 9
 CUTS = 3
 
 
@@ -71,9 +72,9 @@
         copy.wait()
 
 
-def dispatch_kernel(dists, base, extra, ids_hbm, gates_hbm, tok_hbm, grad_hbm, *refs):
+def dispatch_kernel(dists, base, extra, split, ids_hbm, gates_hbm, tok_hbm, grad_hbm, *refs):
     n = len(dists)
-    outs, refs = refs[:n], refs[n:]
+    outs, refs = refs[: n * len(split)], refs[n * len(split) :]
     ids_ref, gates_ref, tok_ref, grad_ref, msg_ref, ext_ref, sem_i, sem_t, sem_g, sem_o = refs
     here = lax.axis_index("expert") // 2
     tokens, width = tok_ref.shape
@@ -121,21 +122,27 @@
             if part:
                 msg_ref[d, :, stop:] = ext_ref[d].astype(BF16)
                 stop = msg_ref.shape[2]
-            cols = pl.ds(part * width, stop - part * width)
-            sent.append(begin(msg_ref.at[d, :, cols], outs[d].at[:, cols], sem_o.at[d, part]))
+            for i, (start, end) in enumerate(split):
+                low, high = max(start, part * width), min(end, stop)
+                if low < high:
+                    src = msg_ref.at[d, :, pl.ds(low, high - low)]
+                    dst = outs[d * len(split) + i].at[:, pl.ds(low - start, high - low)]
+                    sent.append(begin(src, dst, sem_o.at[d, part, i]))
     finish(sent)
 
 
-def dispatch(dists, base, extra, ids_t, gates_t, tok, grad, limit):
+def dispatch(dists, base, extra, ids_t, gates_t, tok, grad, limit, whole=True):
     tokens, width = tok.shape
     n, ext = len(dists), fold_columns(2 * width // LANES * extra, base)
     cols = 2 * width + ext
+    cutoff = 2 * width - TAIL * LANES
+    split = [(0, cols)] if whole else [(0, cutoff), (cutoff, cols)]
     anywhere = pl.BlockSpec(memory_space=pl.ANY)
-    return pl.pallas_call(
-        functools.partial(dispatch_kernel, dists, base, extra),
-        out_shape=[jax.ShapeDtypeStruct((base, cols), BF16) for _ in dists],
+    outs = pl.pallas_call(
+        functools.partial(dispatch_kernel, dists, base, extra, split),
+        out_shape=[jax.ShapeDtypeStruct((base, end - start), BF16) for _ in dists for start, end in split],
         in_specs=[anywhere] * 4,
-        out_specs=[anywhere] * n,
+        out_specs=[anywhere] * (n * len(split)),
         scratch_shapes=[
             pltpu.VMEM(ids_t.shape, jnp.int32),
             pltpu.VMEM(gates_t.shape, F32),
@@ -146,7 +153,7 @@
             pltpu.SemaphoreType.DMA((2,)),
             pltpu.SemaphoreType.DMA((PARTS,)),
             pltpu.SemaphoreType.DMA((PARTS,)),
-            pltpu.SemaphoreType.DMA((n, 2)),
+            pltpu.SemaphoreType.DMA((n, 2, len(split))),
         ],
         compiler_params=pltpu.CompilerParams(vmem_limit_bytes=limit * MIB),
         cost_estimate=pl.CostEstimate(
@@ -156,6 +163,7 @@
         ),
         name="dispatch",
     )(ids_t, gates_t, tok, grad)
+    return [tuple(outs[i : i + len(split)]) for i in range(0, len(outs), len(split))]
 
 
 def silu_slope(pre):
@@ -175,14 +183,25 @@
     return copies
 
 
+def begin_columns(parts, start, dst, sems):
+    copies, at = [], 0
+    for i, part in enumerate(parts):
+        low, high = max(start, at), min(start + dst.shape[1], at + part.shape[1])
+        if low < high:
+            src = part.at[:, pl.ds(low - at, high - low)]
+            copies.append(begin(src, dst.at[:, pl.ds(low - start, high - low)], sems.at[i]))
+        at += part.shape[1]
+    return copies
+
+
 def begin_rows(msgs, rows, ext, start, sems, ext_sems):
-    base = msgs[0].shape[0]
+    base = msgs[0][0].shape[0]
     width = rows.shape[1]
     copies = []
-    for i, msg in enumerate(msgs):
-        copies.append(begin(msg.at[:, pl.ds(start, width)], rows.at[pl.ds(i * base, base), :], sems.at[i]))
+    for i, parts in enumerate(msgs):
+        copies += begin_columns(parts, start, rows.at[pl.ds(i * base, base), :], sems.at[i])
         if ext is not None:
-            copies.append(begin(msg.at[:, pl.ds(2 * width, ext.shape[2])], ext.at[i], ext_sems.at[i]))
+            copies += begin_columns(parts, 2 * width, ext.at[i], ext_sems.at[i])
     return copies
 
 
@@ -193,8 +212,11 @@
     rows[n * base :, :] = row32[...].astype(BF16)
 
 
-def expert_kernel(n, base, extra, stage, w_layout, v_layout, *refs):
-    msgs, refs = refs[:n], refs[n:]
+def expert_kernel(n, base, extra, stage, w_layout, v_layout, lengths, *refs):
+    msgs = []
+    for length in lengths:
+        msgs.append(refs[:length])
+        refs = refs[length:]
     w_pieces, refs = refs[: len(w_layout)], refs[len(w_layout) :]
     v_pieces, refs = refs[: len(v_layout)], refs[len(v_layout) :]
     if stage == "late":
@@ -264,20 +286,120 @@
             outs[i][:, width:] = ext32[i].astype(BF16)
 
 
+def late_kernel(n, base, extra, blocks, w_layout, v_layout, *refs):
+    msgs, refs = refs[:n], refs[n:]
+    w_pieces, refs = refs[: len(w_layout)], refs[len(w_layout) :]
+    v_pieces, refs = refs[: len(v_layout)], refs[len(v_layout) :]
+    slope, partial, refs = refs[0], refs[1], refs[2:]
+    outs, (g, act, ext, row32, ext32, sem_g, sem_e) = refs[:n], refs[n:]
+    width = g.shape[1]
+    half, block_ff = width // 2, v_layout[0][3]
+    pieces = width // LANES
+    full = n * base
+    core = lax.axis_index("expert") % 2
+    copies = begin_rows([(msg,) for msg in msgs], g, ext, width, sem_g, sem_e)
+    finish(copies)
+    if extra:
+        put_extra(g, row32, ext, n, base, pieces)
+    ext32[...] = jnp.zeros_like(ext32)
+    (at, column), (to, to_column) = place_of(2 * pieces * extra, base), place_of(pieces * extra, base)
+    for i in range(n):
+        holders = ext[i].astype(F32)[at : at + 1, column : column + LANES]
+        ext32[i, to : to + 1, to_column : to_column + LANES] = holders
+
+    def work(here):
+        for block in range(blocks):
+            for at in range(0, block_ff, TILE):
+                hid = None
+                for ref, (of, other, row, _) in zip(v_pieces, v_layout):
+                    if of == block:
+                        first = (1 - here if other else here) * half + row
+                        term = jnp.dot(
+                            g[:, first : first + ref.shape[0]],
+                            ref[:, at : at + TILE],
+                            preferred_element_type=F32,
+                        )
+                        hid = term if hid is None else hid + term
+                cols = slice(block * block_ff + at, block * block_ff + at + TILE)
+                act[:, cols] = (hid * slope[:, cols]).astype(BF16)
+        places = {}
+        for ref, (of, other, row, _) in zip(w_pieces, w_layout):
+            for at in range(0, ref.shape[0], TILE):
+                size = min(TILE, ref.shape[0] - at)
+                first = (1 - here if other else here) * half + row + at
+                places.setdefault((first, size), []).append((of, ref, at))
+        for (first, size), terms in sorted(places.items()):
+            cols = slice(first, first + size)
+            back = partial[:, cols]
+            for of, ref, at in terms:
+                back = back + lax.dot_general(
+                    act[:, of * block_ff : (of + 1) * block_ff],
+                    ref[at : at + size, :],
+                    (((1,), (1,)), ((), ())),
+                    preferred_element_type=F32,
+                )
+            for i in range(n):
+                outs[i][:, cols] = back[i * base : (i + 1) * base].astype(BF16)
+                if extra:
+                    fold(ext32.at[i], back[full + i : full + i + 1], size // LANES, first // LANES, base)
+
+    for here in range(2):
+        pl.when(core == here)(functools.partial(work, here))
+    for i in range(n):
+        outs[i][:, width:] = ext32[i].astype(BF16)
+
+
+def flat(columns):
+    arrays, layout = [], []
+    for block, cores in enumerate(columns):
+        for other, pieces in enumerate(cores):
+            row = 0
+            for piece in pieces:
+                arrays.append(piece)
+                layout.append((block, other, row, piece.shape[1]))
+                row += piece.shape[0]
+    return arrays, layout, row
+
+
+def expert_late(msgs, base, extra, w_columns, v_columns, carried):
+    n = len(msgs)
+    msgs = [message for (message,) in msgs]
+    w_pieces, w_layout, half = flat(w_columns)
+    v_pieces, v_layout, _ = flat(v_columns)
+    width, ff = 2 * half, len(w_columns) * w_layout[0][3]
+    rows = n * base + -(-n * extra // 16) * 16
+    ext = fold_columns(2 * width // LANES * extra, base)
+    back_ext = fold_columns(width // LANES * extra, base)
+    anywhere, vmem = pl.BlockSpec(memory_space=pl.ANY), pl.BlockSpec(memory_space=pltpu.VMEM)
+    return pl.pallas_call(
+        functools.partial(late_kernel, n, base, extra, len(w_columns), w_layout, v_layout),
+        out_shape=[jax.ShapeDtypeStruct((base, width + back_ext), BF16) for _ in msgs],
+        in_specs=[anywhere] * n + [vmem] * (len(w_pieces) + len(v_pieces) + len(carried)),
+        out_specs=[vmem] * n,
+        scratch_shapes=[
+            pltpu.VMEM((rows, width), BF16),
+            pltpu.VMEM((rows, ff), BF16),
+            pltpu.VMEM((n, base, ext), BF16),
+            pltpu.VMEM((max(16, rows - n * base), width), F32),
+            pltpu.VMEM((n, base, back_ext), F32),
+            pltpu.SemaphoreType.DMA((n, 1)),
+            pltpu.SemaphoreType.DMA((n, 1)),
+        ],
+        compiler_params=pltpu.CompilerParams(vmem_limit_bytes=24 * MIB),
+        cost_estimate=pl.CostEstimate(
+            flops=4 * rows * width * ff,
+            bytes_accessed=4 * width * ff + 8 * rows * width,
+            transcendentals=0,
+        ),
+        name="expert_late",
+    )(*msgs, *w_pieces, *v_pieces, *carried)
+
+
 def expert(msgs, base, extra, w_columns, v_columns, stage="whole", carried=()):
     n = len(msgs)
 
-    def flat(columns):
-        arrays, layout = [], []
-        for block, cores in enumerate(columns):
-            for other, pieces in enumerate(cores):
-                row = 0
-                for piece in pieces:
-                    arrays.append(piece)
-                    layout.append((block, other, row, piece.shape[1]))
-                    row += piece.shape[0]
-        return arrays, layout, row
-
+    lengths = [len(parts) for parts in msgs]
+    most, parts = max(lengths), [part for message in msgs for part in message]
     w_pieces, w_layout, half = flat(w_columns)
     v_pieces, v_layout, _ = flat(v_columns)
     width, block_ff = 2 * half, w_layout[0][3]
@@ -297,9 +419,9 @@
     else:
         out_shape = [jax.ShapeDtypeStruct((base, cols), BF16) for _ in msgs]
     return pl.pallas_call(
-        functools.partial(expert_kernel, n, base, extra, stage, w_layout, v_layout),
+        functools.partial(expert_kernel, n, base, extra, stage, w_layout, v_layout, lengths),
         out_shape=out_shape,
-        in_specs=[anywhere] * (n + len(w_pieces) + len(v_pieces)) + [vmem] * len(carried),
+        in_specs=[anywhere] * (len(parts) + len(w_pieces) + len(v_pieces)) + [vmem] * len(carried),
         out_specs=[vmem] * len(out_shape),
         scratch_shapes=own_slope
         + [
@@ -311,9 +433,9 @@
             pltpu.VMEM((n, base, ext), BF16),
             pltpu.VMEM((spare, width), F32),
             pltpu.VMEM((n, base, back_ext), F32),
-            pltpu.SemaphoreType.DMA((n,)),
-            pltpu.SemaphoreType.DMA((n,)),
-            pltpu.SemaphoreType.DMA((n,)),
+            pltpu.SemaphoreType.DMA((n, most)),
+            pltpu.SemaphoreType.DMA((n, most)),
+            pltpu.SemaphoreType.DMA((n, most)),
             pltpu.SemaphoreType.DMA((len(w_pieces),)),
             pltpu.SemaphoreType.DMA((len(v_pieces),)),
         ],
@@ -324,7 +446,7 @@
             transcendentals=0 if stage == "early" else rows * w_ff,
         ),
         name="expert_" + stage,
-    )(*msgs, *w_pieces, *v_pieces, *carried)
+    )(*parts, *w_pieces, *v_pieces, *carried)
 
 
 def add_kernel(n, extra, start_ref, *refs):
@@ -406,7 +528,7 @@
 
 
 def cut(weight):
-    step = -(-weight.shape[0] // (16 * CUTS)) * 16
+    step = -(-weight.shape[0] // (LANES * CUTS)) * LANES
     return [weight[at : at + step] for at in range(0, weight.shape[0], step)]
 
 
@@ -428,7 +550,7 @@
     others = range(1, lax.axis_size("dp"))
     w_own, v_own = w_in[0, 0], w_out_t[0, 0]
     sent = [
-        dispatch(group, base, extra, ids_t, gates_t, tok, grad, 24 if i else LIMIT)
+        dispatch(group, base, extra, ids_t, gates_t, tok, grad, 24 if i else LIMIT, i < len(sends) - 1)
         for i, group in enumerate(sends)
     ]
     w_far = [swap(w_own, "dp", apart) for apart in others]
@@ -436,11 +558,11 @@
     other_grad = swap(grad, "section", 1)
     v_late, w_other, v_other = after(v_own, w_other, v_other)
     v_far = [swap(v_late, "dp", apart) for apart in others]
-    sent[-1], other_grad = after(sent[-1], other_grad)
+    sent[-1], other_grad, w_far = after(sent[-1], other_grad, w_far)
     got = {}
     for group, msgs in zip(sends, sent):
         for dist, msg in zip(group, msgs):
-            got[dist] = swap(msg, "expert", 2 * dist) if dist else msg
+            got[dist] = tuple(swap(part, "expert", 2 * dist) for part in msg) if dist else msg
     first, last = [dist for group in sends[:-1] for dist in group], sends[-1]
 
     w_far, heads = after(w_far, [got[dist] for dist in first])
@@ -449,15 +571,15 @@
     w_columns += [[[block], [swap(piece, "expert", 1) for piece in cut(block)]] for block in w_far]
     v_columns = [[[v_own], [v_other]]]
     carried = expert([got[dist] for dist in works[0]], base, extra, w_columns, v_columns, "early")
-    v_far, tails, carried = after(v_far, [got[dist] for dist in last], carried)
-    got.update(zip(last, tails))
+    v_far, tails, carried = after(v_far, [got[dist][0] for dist in last], carried)
+    got.update((dist, (tail,) + got[dist][1:]) for dist, tail in zip(last, tails))
     v_columns += [[[block], [swap(block, "expert", 1)]] for block in v_far]
 
     total = other_grad
     for i, group in enumerate(works):
         msgs = [got[dist] for dist in group]
         if i == 0:
-            backs = expert(msgs, base, extra, w_columns[1:], v_columns[1:], "late", carried)
+            backs = expert_late(msgs, base, extra, w_columns[1:], v_columns[1:], carried)
             backs, got = after(backs, got)
         else:
             backs = expert(msgs, base, extra, w_columns, v_columns)

time: 145 us -> 141 us (0.972)
  waiting for transfers between devices: 90.6 us -> 85.9 us
    ppermute x12 -> x13, starting transfers between devices: 14.4 us -> 18.5 us  [swap(): lax.ppermute(value, axis, [(i, i ^ apart) for i in range(lax.axis_size(ax...]
    ppermute x12 -> x13, waiting for transfers between devices: 58.6 us -> 54.7 us  [swap(): lax.ppermute(value, axis, [(i, i ^ apart) for i in range(lax.axis_size(ax...]
    ppermute x4, starting transfers between devices: 11 us -> 7.91 us  [swap_back(): return lax.ppermute(value, ('section', 'expert'), pairs)]
    pallas_call x3 -> x2, Pallas kernels: 16.1 us -> 13.2 us  [expert(): pl.pallas_call(functools.partial(expert_kernel, n, base, extra, stage, w_...]
    pallas_call x3 -> x4, Pallas kernels: 10.7 us -> 13.1 us  [the longest x3 10.8 us: dispatch(): pl.pallas_call(functools.partial(dispatch_kernel, dists, base, extra, spl...]
  transfers between devices with their start and end apart: 16 -> 17, of which waited for: 7 -> 9; matrix products, arithmetic and copies ran while one was open for 0% -> 0% of each run, Pallas kernels for 17% -> 19%
where the time goes in v4:
time: 141 us
  waiting for transfers between devices  85.9 us (61%)
  Pallas kernels  28.6 us (20%)
  starting transfers between devices  26.4 us (19%)
    ppermute x13, waiting for transfers between devices, swap(): lax.ppermute(value, axis, [(i, i ^ apart) for i in range(lax.axis_size(ax...  54.7 us
    ppermute x4, waiting for transfers between devices, swap_back(): return lax.ppermute(value, ('section', 'expert'), pairs)  31.2 us
    ppermute x13, starting transfers between devices, swap(): lax.ppermute(value, axis, [(i, i ^ apart) for i in range(lax.axis_size(ax...  18.5 us
    pallas_call x2, Pallas kernels, expert(): pl.pallas_call(functools.partial(expert_kernel, n, base, extra, stage, w_...  13.2 us
    pallas_call x3, Pallas kernels, dispatch(): pl.pallas_call(functools.partial(dispatch_kernel, dists, base, extra, spl...  10.8 us
    ppermute x4, starting transfers between devices, swap_back(): return lax.ppermute(value, ('section', 'expert'), pairs)  7.91 us
  transfers between devices with their start and end apart: 17, of which 9 were waited for; matrix products, arithmetic and copies ran while one was open for 0% of the time, Pallas kernels for 19%

profile of v4, /device:TPU:0, one launch (start us, length us, event | category | flops | bytes accessed | tf_op | source)
XLA Modules:
  0.0 141.3 jit_solution(9716677359692999125)
XLA Ops:
  0.0 0.0 copy-start.5
  0.0 0.0 copy-start.4
  0.0 0.0 copy-start.1
  0.0 0.0 copy-start
  0.0 0.5 collective-permute-start.7
  0.5 0.1 collective-permute-start.8
  0.6 2.9 %collective-permute-start.1 = (bf16[1792,512]{1,0:T(8,128)(2,1)}, bf16[1792,512]{1,0:T(8,128)(2,1)S(1)}, u32[]{:S(2)}, u32[]{:S(2)}) collective-permute-start(bf16[1792,512]{1,0:T(8,128)(2,1)} %bitcast.19), channel_id=1, source_target_pairs={{0,1},{1,0},{2,3},{3,2},{4,5},{5,4},{6,7},{7,6},{8,9},{9,8},{10,11... | collective-permute-start | bytes 5505032 | tf_op jit(solution)/shard_map/ppermute | solution.py:515
  3.6 0.0 copy-start.3
  3.6 3.1 %dispatch.4 = bf16[64,7296]{1,0:T(8,128)(2,1)} custom-call(s32[2,128]{1,0:T(2,128)} %bitcast.26, f32[2,128]{1,0:T(2,128)} %bitcast.29, bf16[128,3584]{1,0:T(8,128)(2,1)} %bitcast.11, bf16[128,3584]{1,0:T(8,128)(2,1)} %bitcast.14), custom_call_target="tpu_custom_call" | custom-call | flops 146800640 | bytes 2768896 | tf_op jit(solution)/shard_map/dispatch/pallas_call | solution.py:141
  6.7 2.7 %collective-permute-start.2 = (bf16[64,7296]{1,0:T(8,128)(2,1)}, bf16[64,7296]{1,0:T(8,128)(2,1)S(1)}, u32[]{:S(2)}, u32[]{:S(2)}) collective-permute-start(bf16[64,7296]{1,0:T(8,128)(2,1)} %dispatch.4), channel_id=1, source_target_pairs={{0,8},{2,10},{4,12},{6,14},{8,0},{10,2},{12,4},{14,6},{1,9},{3,11}... | collective-permute-start | bytes 2801672 | tf_op jit(solution)/shard_map/ppermute | solution.py:515
  9.4 0.0 copy-done.5
  9.4 0.0 copy-done.4
  9.4 0.0 copy-done.1
  9.4 0.0 copy-done
  9.4 4.2 %dispatch.5 = (bf16[64,7296]{1,0:T(8,128)(2,1)S(1)}, bf16[64,7296]{1,0:T(8,128)(2,1)S(1)}) custom-call(s32[2,128]{1,0:T(2,128)S(1)} %bitcast.27, f32[2,128]{1,0:T(2,128)S(1)} %bitcast.30, bf16[128,3584]{1,0:T(8,128)(2,1)S(1)} %bitcast.12, bf16[128,3584]{1,0:T(8,128)(2,1)S(1)} %bitcast.15), custom_call_target="tpu_custom_call" | custom-call | flops 293601280 | bytes 3702784 | tf_op jit(solution)/shard_map/dispatch/pallas_call | solution.py:141
  13.6 1.6 %collective-permute-start.3 = (bf16[64,7296]{1,0:T(8,128)(2,1)S(1)}, bf16[64,7296]{1,0:T(8,128)(2,1)S(1)}, u32[]{:S(2)}, u32[]{:S(2)}) collective-permute-start(bf16[64,7296]{1,0:T(8,128)(2,1)S(1)} %get-tuple-element.39), channel_id=1, source_target_pairs={{0,4},{2,6},{4,0},{6,2},{8,12},{10,14},{12,8},{14,10},{1,5},{3,7},... | collective-permute-start | bytes 2801672 | tf_op jit(solution)/shard_map/ppermute | solution.py:515
  15.2 0.0 collective-permute-done.7.refs_3_.refs_4_
  15.3 1.5 %collective-permute-start = (bf16[128,3584]{1,0:T(8,128)(2,1)S(1)}, bf16[128,3584]{1,0:T(8,128)(2,1)S(1)}, u32[]{:S(2)}, u32[]{:S(2)}) collective-permute-start(bf16[128,3584]{1,0:T(8,128)(2,1)S(1)} %bitcast.16), channel_id=1, source_target_pairs={{0,16},{16,0},{1,17},{17,1},{2,18},{18,2},{3,19},{19,3},{4,20},{20... | collective-permute-start | bytes 2752520 | tf_op jit(solution)/shard_map/ppermute | solution.py:515
  16.7 0.0 collective-permute-done.8.refs_9_.refs_10_
  16.7 0.0 copy-done.3
  16.7 0.5 collective-permute-start.9
  17.3 3.5 %dispatch.3 = (bf16[64,6016]{1,0:T(8,128)(2,1)S(1)}, bf16[64,1280]{1,0:T(8,128)(2,1)S(1)}) custom-call(s32[2,128]{1,0:T(2,128)S(1)} %bitcast.28, f32[2,128]{1,0:T(2,128)S(1)} %bitcast.31, bf16[128,3584]{1,0:T(8,128)(2,1)S(1)} %bitcast.13, bf16[128,3584]{1,0:T(8,128)(2,1)S(1)} %bitcast.17), custom_call_target="tpu_custom_call" | custom-call | flops 146800640 | bytes 2768896 | tf_op jit(solution)/shard_map/dispatch/pallas_call | solution.py:141
  20.7 16.0 %collective-permute-done.start_ref = bf16[128,3584]{1,0:T(8,128)(2,1)S(1)} collective-permute-done((bf16[128,3584]{1,0:T(8,128)(2,1)S(1)}, bf16[128,3584]{1,0:T(8,128)(2,1)S(1)}, u32[]{:S(2)}, u32[]{:S(2)}) %collective-permute-start) | collective-permute-done | bytes 917536 | tf_op jit(solution)/shard_map/ppermute | solution.py:515
  36.7 7.8 %collective-permute-done.1.refs_4_.refs_2_.refs_5_ = bf16[1792,512]{1,0:T(8,128)(2,1)S(1)} collective-permute-done((bf16[1792,512]{1,0:T(8,128)(2,1)}, bf16[1792,512]{1,0:T(8,128)(2,1)S(1)}, u32[]{:S(2)}, u32[]{:S(2)}) %collective-permute-start.1) | collective-permute-done | bytes 1835040 | tf_op jit(solution)/shard_map/ppermute | solution.py:515
  44.6 4.1 %collective-permute-start.10 = (bf16[64,6016]{1,0:T(8,128)(2,1)S(1)}, bf16[64,6016]{1,0:T(8,128)(2,1)S(1)}, u32[]{:S(2)}, u32[]{:S(2)}) collective-permute-start(bf16[64,6016]{1,0:T(8,128)(2,1)S(1)} %get-tuple-element.45), channel_id=1, source_target_pairs={{0,12},{2,14},{4,8},{6,10},{8,4},{10,6},{12,0},{14,2},{1,13},{3,15... | collective-permute-start | bytes 2310152 | tf_op jit(solution)/shard_map/ppermute | solution.py:515
  48.7 19.3 %collective-permute-done.2.refs_0_ = bf16[64,7296]{1,0:T(8,128)(2,1)S(1)} collective-permute-done((bf16[64,7296]{1,0:T(8,128)(2,1)}, bf16[64,7296]{1,0:T(8,128)(2,1)S(1)}, u32[]{:S(2)}, u32[]{:S(2)}) %collective-permute-start.2) | collective-permute-done | bytes 933920 | tf_op jit(solution)/shard_map/ppermute | solution.py:515
  68.0 3.2 %collective-permute-done.3.refs_2_ = bf16[64,7296]{1,0:T(8,128)(2,1)S(1)} collective-permute-done((bf16[64,7296]{1,0:T(8,128)(2,1)S(1)}, bf16[64,7296]{1,0:T(8,128)(2,1)S(1)}, u32[]{:S(2)}, u32[]{:S(2)}) %collective-permute-start.3) | collective-permute-done | bytes 933920 | tf_op jit(solution)/shard_map/ppermute | solution.py:515
  71.2 0.0 copy-start.2
  71.2 0.1 fusion
  71.3 0.1 collective-permute-start.5
  71.4 0.5 collective-permute-start.4
  71.9 0.1 collective-permute-start.6
  72.1 3.1 %collective-permute-done.6.refs_7_.refs_5_.refs_8_ = bf16[512,512]{1,0:T(8,128)(2,1)S(1)} collective-permute-done((bf16[512,512]{1,0:T(8,128)(2,1)S(1)}, bf16[512,512]{1,0:T(8,128)(2,1)S(1)}, u32[]{:S(2)}, u32[]{:S(2)}) %collective-permute-start.6) | collective-permute-done | bytes 524320 | tf_op jit(solution)/shard_map/ppermute | solution.py:515
  75.1 0.0 collective-permute-done.5.refs_6_.refs_4_.refs_7_
  75.1 0.0 collective-permute-done.4.refs_5_.refs_3_.refs_6_
  75.2 0.0 copy-done.2
  75.2 5.6 %expert_early.1 = (f32[144,512]{1,0:T(8,128)S(1)}, f32[144,3584]{1,0:T(8,128)S(1)}) custom-call(bf16[64,7296]{1,0:T(8,128)(2,1)S(1)} %collective-permute-done.2.refs_0_, bf16[64,7296]{1,0:T(8,128)(2,1)S(1)} %get-tuple-element.42.refs_1_, bf16[1792,512]{1,0:T(8,128)(2,1)S(1)} %bitcast.20, bf16[1792,512]{1,0:T(8,128)(2,1)} %collective-permute-done.7.refs_3_.refs_4_, ...), custom_call_target="tpu_custom_call" | custom-call | tf_op jit(solution)/shard_map/expert_early/pallas_call | solution.py:421
  80.7 0.0 collective-permute-done.10.refs_0_
  80.8 2.6 %collective-permute-done.9.refs_6_.refs_11_ = bf16[1792,512]{1,0:T(8,128)(2,1)S(1)} collective-permute-done((bf16[1792,512]{1,0:T(8,128)(2,1)S(1)}, bf16[1792,512]{1,0:T(8,128)(2,1)S(1)}, u32[]{:S(2)}, u32[]{:S(2)}) %collective-permute-start.9) | collective-permute-done | bytes 1835040 | tf_op jit(solution)/shard_map/ppermute | solution.py:515
  83.4 0.0 collective-permute-start.11
  83.4 3.8 %collective-permute-start.12 = (bf16[64,1280]{1,0:T(8,128)(2,1)S(1)}, bf16[64,1280]{1,0:T(8,128)(2,1)S(1)}, u32[]{:S(2)}, u32[]{:S(2)}) collective-permute-start(bf16[64,1280]{1,0:T(8,128)(2,1)S(1)} %get-tuple-element.57), channel_id=1, source_target_pairs={{0,12},{2,14},{4,8},{6,10},{8,4},{10,6},{12,0},{14,2},{1,13},{3,15... | collective-permute-start | bytes 491528 | tf_op jit(solution)/shard_map/ppermute | solution.py:515
  87.2 0.0 collective-permute-done.11.refs_7_.refs_12_
  87.2 2.3 %expert_late.1 = (bf16[64,3712]{1,0:T(8,128)(2,1)S(1)}, bf16[64,3712]{1,0:T(8,128)(2,1)S(1)}) custom-call(bf16[64,7296]{1,0:T(8,128)(2,1)S(1)} %collective-permute-done.2.refs_0_, bf16[64,7296]{1,0:T(8,128)(2,1)S(1)} %get-tuple-element.42.refs_1_, bf16[1792,512]{1,0:T(8,128)(2,1)S(1)} %collective-permute-done.1.refs_4_.refs_2_.refs_5_, ...), custom_call_target="tpu_custom_call" | custom-call | flops 1056964608 | bytes 11468800 | tf_op jit(solution)/shard_map/expert_late/pallas_call | solution.py:374
  89.5 2.7 %collective-permute-done.12.refs_1_ = bf16[64,1280]{1,0:T(8,128)(2,1)S(1)} collective-permute-done((bf16[64,1280]{1,0:T(8,128)(2,1)S(1)}, bf16[64,1280]{1,0:T(8,128)(2,1)S(1)}, u32[]{:S(2)}, u32[]{:S(2)}) %collective-permute-start.12) | collective-permute-done | bytes 163872 | tf_op jit(solution)/shard_map/ppermute | solution.py:515
  92.2 5.1 %collective-permute-start.13 = (bf16[64,3712]{1,0:T(8,128)(2,1)S(1)}, bf16[64,3712]{1,0:T(8,128)(2,1)S(1)}, u32[]{:S(2)}, u32[]{:S(2)}) collective-permute-start(bf16[64,3712]{1,0:T(8,128)(2,1)S(1)} %get-tuple-element.58), channel_id=1, source_target_pairs={{0,24},{2,26},{4,28},{6,30},{8,16},{10,18},{12,20},{14,22},{16,8},... | collective-permute-start | bytes 1425416 | tf_op jit(solution)/shard_map/ppermute | solution.py:523
  97.2 0.5 collective-permute-start.14
  97.8 7.6 %expert_whole.1 = (bf16[64,3712]{1,0:T(8,128)(2,1)S(1)}, bf16[64,3712]{1,0:T(8,128)(2,1)S(1)}) custom-call(bf16[64,6016]{1,0:T(8,128)(2,1)S(1)} %collective-permute-done.10.refs_0_, bf16[64,1280]{1,0:T(8,128)(2,1)S(1)} %collective-permute-done.12.refs_1_, bf16[64,7296]{1,0:T(8,128)(2,1)S(1)} %collective-permute-done.3.refs_2_, ...), custom_call_target="tpu_custom_call" | custom-call | flops 3170893824 | bytes 17776640 | tf_op jit(solution)/shard_map/expert_whole/pallas_call | solution.py:421
  105.4 2.3 %collective-permute-start.15 = (bf16[64,3712]{1,0:T(8,128)(2,1)S(1)}, bf16[64,3712]{1,0:T(8,128)(2,1)S(1)}, u32[]{:S(2)}, u32[]{:S(2)}) collective-permute-start(bf16[64,3712]{1,0:T(8,128)(2,1)S(1)} %get-tuple-element.63), channel_id=1, source_target_pairs={{0,28},{2,30},{4,24},{6,26},{8,20},{10,22},{12,16},{14,18},{16,12}... | collective-permute-start | bytes 1425416 | tf_op jit(solution)/shard_map/ppermute | solution.py:523
  107.7 0.0 collective-permute-start.16
  107.7 21.8 %collective-permute-done.13.refs_0_ = bf16[64,3712]{1,0:T(8,128)(2,1)S(1)} collective-permute-done((bf16[64,3712]{1,0:T(8,128)(2,1)S(1)}, bf16[64,3712]{1,0:T(8,128)(2,1)S(1)}, u32[]{:S(2)}, u32[]{:S(2)}) %collective-permute-start.13) | collective-permute-done | bytes 475168 | tf_op jit(solution)/shard_map/ppermute | solution.py:523
  129.4 9.4 %collective-permute-done.14.refs_1_ = bf16[64,3712]{1,0:T(8,128)(2,1)S(1)} collective-permute-done((bf16[64,3712]{1,0:T(8,128)(2,1)S(1)}, bf16[64,3712]{1,0:T(8,128)(2,1)S(1)}, u32[]{:S(2)}, u32[]{:S(2)}) %collective-permute-start.14) | collective-permute-done | bytes 475168 | tf_op jit(solution)/shard_map/ppermute | solution.py:523
  138.9 0.7 settle.1.start_ref
  139.5 0.0 collective-permute-done.15.refs_0_
  139.5 0.0 collective-permute-done.16.refs_1_
  139.6 1.6 %finish.1 = bf16[128,3584]{1,0:T(8,128)(2,1)} custom-call(f32[128,3584]{1,0:T(8,128)S(1)} %settle.1.start_ref, bf16[64,3712]{1,0:T(8,128)(2,1)S(1)} %collective-permute-done.15.refs_0_, bf16[64,3712]{1,0:T(8,128)(2,1)S(1)} %collective-permute-done.16.refs_1_), custom_call_target="tpu_custom_call" | custom-call | flops 132120576 | bytes 3784704 | tf_op jit(solution)/shard_map/finish/pallas_call | solution.py:491
  (1 shorter events, 0.0 us)
Async XLA Ops:
  0.0 9.4 %copy-start.5 = (f32[1,128,2]{1,2,0:T(2,128)S(1)}, f32[1,128,2]{1,2,0:T(2,128)}, u32[]{:S(2)}) copy-start(f32[1,128,2]{1,2,0:T(2,128)} %param.9) | copy-start | bytes 3076
  0.0 9.4 %copy-start.4 = (s32[1,128,2]{1,2,0:T(2,128)S(1)}, s32[1,128,2]{1,2,0:T(2,128)}, u32[]{:S(2)}) copy-start(s32[1,128,2]{1,2,0:T(2,128)} %param.8) | copy-start | bytes 3076
  0.0 9.4 %copy-start.1 = (bf16[1,128,3584]{2,1,0:T(8,128)(2,1)S(1)}, bf16[1,128,3584]{2,1,0:T(8,128)(2,1)}, u32[]{:S(2)}) copy-start(bf16[1,128,3584]{2,1,0:T(8,128)(2,1)} %param.7) | copy-start | bytes 2752516
  0.0 9.4 %copy-start = (bf16[1,128,3584]{2,1,0:T(8,128)(2,1)S(1)}, bf16[1,128,3584]{2,1,0:T(8,128)(2,1)}, u32[]{:S(2)}) copy-start(bf16[1,128,3584]{2,1,0:T(8,128)(2,1)} %param.6) | copy-start | bytes 2752516
  0.0 15.2 %collective-permute-start.7 = (bf16[1792,512]{1,0:T(8,128)(2,1)}, bf16[1792,512]{1,0:T(8,128)(2,1)}, u32[]{:S(2)}, u32[]{:S(2)}) collective-permute-start(bf16[1792,512]{1,0:T(8,128)(2,1)} %bitcast.18), channel_id=1, source_target_pairs={{0,2},{2,0},{4,6},{6,4},{8,10},{10,8},{12,14},{14,12},{1,3},{3,1},... | collective-permute-start | bytes 5505032 | tf_op jit(solution)/shard_map/ppermute | solution.py:515
  0.5 16.2 %collective-permute-start.8 = (bf16[1792,512]{1,0:T(8,128)(2,1)}, bf16[1792,512]{1,0:T(8,128)(2,1)}, u32[]{:S(2)}, u32[]{:S(2)}) collective-permute-start(bf16[1792,512]{1,0:T(8,128)(2,1)} %bitcast.22), channel_id=1, source_target_pairs={{0,2},{2,0},{4,6},{6,4},{8,10},{10,8},{12,14},{14,12},{1,3},{3,1},... | collective-permute-start | bytes 5505032 | tf_op jit(solution)/shard_map/ppermute | solution.py:515
  0.6 44.0 %collective-permute-start.1 = (bf16[1792,512]{1,0:T(8,128)(2,1)}, bf16[1792,512]{1,0:T(8,128)(2,1)S(1)}, u32[]{:S(2)}, u32[]{:S(2)}) collective-permute-start(bf16[1792,512]{1,0:T(8,128)(2,1)} %bitcast.19), channel_id=1, source_target_pairs={{0,1},{1,0},{2,3},{3,2},{4,5},{5,4},{6,7},{7,6},{8,9},{9,8},{10,11... | collective-permute-start | bytes 5505032 | tf_op jit(solution)/shard_map/ppermute | solution.py:515
  3.6 13.2 %copy-start.3 = (bf16[1,1,1792,512]{3,2,1,0:T(8,128)(2,1)S(1)}, bf16[1,1,1792,512]{3,2,1,0:T(8,128)(2,1)}, u32[]{:S(2)}) copy-start(bf16[1,1,1792,512]{3,2,1,0:T(8,128)(2,1)} %param.11) | copy-start | bytes 5505028
  6.7 61.3 %collective-permute-start.2 = (bf16[64,7296]{1,0:T(8,128)(2,1)}, bf16[64,7296]{1,0:T(8,128)(2,1)S(1)}, u32[]{:S(2)}, u32[]{:S(2)}) collective-permute-start(bf16[64,7296]{1,0:T(8,128)(2,1)} %dispatch.4), channel_id=1, source_target_pairs={{0,8},{2,10},{4,12},{6,14},{8,0},{10,2},{12,4},{14,6},{1,9},{3,11}... | collective-permute-start | bytes 2801672 | tf_op jit(solution)/shard_map/ppermute | solution.py:515
  13.6 57.6 %collective-permute-start.3 = (bf16[64,7296]{1,0:T(8,128)(2,1)S(1)}, bf16[64,7296]{1,0:T(8,128)(2,1)S(1)}, u32[]{:S(2)}, u32[]{:S(2)}) collective-permute-start(bf16[64,7296]{1,0:T(8,128)(2,1)S(1)} %get-tuple-element.39), channel_id=1, source_target_pairs={{0,4},{2,6},{4,0},{6,2},{8,12},{10,14},{12,8},{14,10},{1,5},{3,7},... | collective-permute-start | bytes 2801672 | tf_op jit(solution)/shard_map/ppermute | solution.py:515
  15.3 21.5 %collective-permute-start = (bf16[128,3584]{1,0:T(8,128)(2,1)S(1)}, bf16[128,3584]{1,0:T(8,128)(2,1)S(1)}, u32[]{:S(2)}, u32[]{:S(2)}) collective-permute-start(bf16[128,3584]{1,0:T(8,128)(2,1)S(1)} %bitcast.16), channel_id=1, source_target_pairs={{0,16},{16,0},{1,17},{17,1},{2,18},{18,2},{3,19},{19,3},{4,20},{20... | collective-permute-start | bytes 2752520 | tf_op jit(solution)/shard_map/ppermute | solution.py:515
  16.7 66.6 %collective-permute-start.9 = (bf16[1792,512]{1,0:T(8,128)(2,1)S(1)}, bf16[1792,512]{1,0:T(8,128)(2,1)S(1)}, u32[]{:S(2)}, u32[]{:S(2)}) collective-permute-start(bf16[1792,512]{1,0:T(8,128)(2,1)S(1)} %bitcast.23), channel_id=1, source_target_pairs={{0,1},{1,0},{2,3},{3,2},{4,5},{5,4},{6,7},{7,6},{8,9},{9,8},{10,11... | collective-permute-start | bytes 5505032 | tf_op jit(solution)/shard_map/ppermute | solution.py:515
  44.6 36.2 %collective-permute-start.10 = (bf16[64,6016]{1,0:T(8,128)(2,1)S(1)}, bf16[64,6016]{1,0:T(8,128)(2,1)S(1)}, u32[]{:S(2)}, u32[]{:S(2)}) collective-permute-start(bf16[64,6016]{1,0:T(8,128)(2,1)S(1)} %get-tuple-element.45), channel_id=1, source_target_pairs={{0,12},{2,14},{4,8},{6,10},{8,4},{10,6},{12,0},{14,2},{1,13},{3,15... | collective-permute-start | bytes 2310152 | tf_op jit(solution)/shard_map/ppermute | solution.py:515
  71.2 4.0 %copy-start.2 = (bf16[1,1,1792,512]{3,2,1,0:T(8,128)(2,1)S(1)}, bf16[1,1,1792,512]{3,2,1,0:T(8,128)(2,1)}, u32[]{:S(2)}) copy-start(bf16[1,1,1792,512]{3,2,1,0:T(8,128)(2,1)} %param.10) | copy-start | bytes 5505028
  71.3 3.9 %collective-permute-start.5 = (bf16[640,512]{1,0:T(8,128)(2,1)S(1)}, bf16[640,512]{1,0:T(8,128)(2,1)S(1)}, u32[]{:S(2)}, u32[]{:S(2)}) collective-permute-start(bf16[640,512]{1,0:T(8,128)(2,1)S(1)} %get-tuple-element.65), channel_id=1, source_target_pairs={{0,2},{2,0},{4,6},{6,4},{8,10},{10,8},{12,14},{14,12},{1,3},{3,1},... | collective-permute-start | bytes 1966088 | tf_op jit(solution)/shard_map/ppermute | solution.py:515
  71.4 3.8 %collective-permute-start.4 = (bf16[640,512]{1,0:T(8,128)(2,1)S(1)}, bf16[640,512]{1,0:T(8,128)(2,1)S(1)}, u32[]{:S(2)}, u32[]{:S(2)}) collective-permute-start(bf16[640,512]{1,0:T(8,128)(2,1)S(1)} %get-tuple-element.66), channel_id=1, source_target_pairs={{0,2},{2,0},{4,6},{6,4},{8,10},{10,8},{12,14},{14,12},{1,3},{3,1},... | collective-permute-start | bytes 1966088 | tf_op jit(solution)/shard_map/ppermute | solution.py:515
  71.9 3.2 %collective-permute-start.6 = (bf16[512,512]{1,0:T(8,128)(2,1)S(1)}, bf16[512,512]{1,0:T(8,128)(2,1)S(1)}, u32[]{:S(2)}, u32[]{:S(2)}) collective-permute-start(bf16[512,512]{1,0:T(8,128)(2,1)S(1)} %slice.11), channel_id=1, source_target_pairs={{0,2},{2,0},{4,6},{6,4},{8,10},{10,8},{12,14},{14,12},{1,3},{3,1},... | collective-permute-start | bytes 1572872 | tf_op jit(solution)/shard_map/ppermute | solution.py:515
  83.4 3.8 %collective-permute-start.11 = (bf16[1792,512]{1,0:T(8,128)(2,1)S(1)}, bf16[1792,512]{1,0:T(8,128)(2,1)S(1)}, u32[]{:S(2)}, u32[]{:S(2)}) collective-permute-start(bf16[1792,512]{1,0:T(8,128)(2,1)S(1)} %collective-permute-done.9.refs_6_.refs_11_), channel_id=1, source_target_pairs={{0,2},{2,0},{4,6},{6,4},{8,10},{10,8},{12,14},{14,12},{1,3},{3,1},... | collective-permute-start | bytes 5505032 | tf_op jit(solution)/shard_map/ppermute | solution.py:515
  83.4 8.8 %collective-permute-start.12 = (bf16[64,1280]{1,0:T(8,128)(2,1)S(1)}, bf16[64,1280]{1,0:T(8,128)(2,1)S(1)}, u32[]{:S(2)}, u32[]{:S(2)}) collective-permute-start(bf16[64,1280]{1,0:T(8,128)(2,1)S(1)} %get-tuple-element.57), channel_id=1, source_target_pairs={{0,12},{2,14},{4,8},{6,10},{8,4},{10,6},{12,0},{14,2},{1,13},{3,15... | collective-permute-start | bytes 491528 | tf_op jit(solution)/shard_map/ppermute | solution.py:515
  92.2 37.3 %collective-permute-start.13 = (bf16[64,3712]{1,0:T(8,128)(2,1)S(1)}, bf16[64,3712]{1,0:T(8,128)(2,1)S(1)}, u32[]{:S(2)}, u32[]{:S(2)}) collective-permute-start(bf16[64,3712]{1,0:T(8,128)(2,1)S(1)} %get-tuple-element.58), channel_id=1, source_target_pairs={{0,24},{2,26},{4,28},{6,30},{8,16},{10,18},{12,20},{14,22},{16,8},... | collective-permute-start | bytes 1425416 | tf_op jit(solution)/shard_map/ppermute | solution.py:523
  97.2 41.6 %collective-permute-start.14 = (bf16[64,3712]{1,0:T(8,128)(2,1)S(1)}, bf16[64,3712]{1,0:T(8,128)(2,1)S(1)}, u32[]{:S(2)}, u32[]{:S(2)}) collective-permute-start(bf16[64,3712]{1,0:T(8,128)(2,1)S(1)} %get-tuple-element.59), channel_id=1, source_target_pairs={{0,16},{2,18},{4,20},{6,22},{8,24},{10,26},{12,28},{14,30},{16,0},... | collective-permute-start | bytes 1425416 | tf_op jit(solution)/shard_map/ppermute | solution.py:523
  105.4 34.2 %collective-permute-start.15 = (bf16[64,3712]{1,0:T(8,128)(2,1)S(1)}, bf16[64,3712]{1,0:T(8,128)(2,1)S(1)}, u32[]{:S(2)}, u32[]{:S(2)}) collective-permute-start(bf16[64,3712]{1,0:T(8,128)(2,1)S(1)} %get-tuple-element.63), channel_id=1, source_target_pairs={{0,28},{2,30},{4,24},{6,26},{8,20},{10,22},{12,16},{14,18},{16,12}... | collective-permute-start | bytes 1425416 | tf_op jit(solution)/shard_map/ppermute | solution.py:523
  107.7 31.9 %collective-permute-start.16 = (bf16[64,3712]{1,0:T(8,128)(2,1)S(1)}, bf16[64,3712]{1,0:T(8,128)(2,1)S(1)}, u32[]{:S(2)}, u32[]{:S(2)}) collective-permute-start(bf16[64,3712]{1,0:T(8,128)(2,1)S(1)} %get-tuple-element.64), channel_id=1, source_target_pairs={{0,20},{2,22},{4,16},{6,18},{8,28},{10,30},{12,24},{14,26},{16,4},... | collective-permute-start | bytes 1425416 | tf_op jit(solution)/shard_map/ppermute | solution.py:523

commit v5 on v4

--- a/solution.py
+++ b/solution.py
@@ -13,9 +13,9 @@
 BF16 = jnp.bfloat16
 MIB = 1 << 20
 CHUNK = 512
-PARTS = 4
+PARTS = 1
 LIMIT = 57
-TAIL = 9
+TAIL = 5
 CUTS = 3
 
 
@@ -28,6 +28,15 @@
 
 def fold_columns(pieces, base):
     return -(-(pieces + 1) // base) * LANES
+
+
+def sides_of(base):
+    return 2 if base % 32 == 0 else 1
+
+
+def back_shape(base, width, extra):
+    sides = sides_of(base)
+    return base // sides, sides * width + fold_columns(width // LANES * extra, base // sides)
 
 
 def place_of(piece, base):
@@ -208,8 +217,20 @@
 def put_extra(rows, row32, ext, n, base, first):
     row32[...] = jnp.zeros_like(row32)
     for i in range(n):
-        unfold(row32, i, ext[i].astype(F32), rows.shape[1] // LANES, first, base)
+        unfold(row32, i, ext[i].astype(F32), rows.shape[1] // LANES, first, ext.shape[1])
     rows[n * base :, :] = row32[...].astype(BF16)
+
+
+def put_back(outs, ext32, back, at, size, n, base, extra, width):
+    part = outs[0].shape[0]
+    for i in range(n):
+        for side in range(base // part):
+            first = i * base + side * part
+            cols = slice(side * width + at, side * width + at + size)
+            outs[i][:, cols] = back[first : first + part].astype(BF16)
+        if extra:
+            row = back[n * base + i : n * base + i + 1]
+            fold(ext32.at[i], row, size // LANES, at // LANES, part)
 
 
 def expert_kernel(n, base, extra, stage, w_layout, v_layout, lengths, *refs):
@@ -262,7 +283,8 @@
             finish(w_in[block])
     if stage != "early":
         ext32[...] = jnp.zeros_like(ext32)
-        (at, column), (to, to_column) = place_of(2 * pieces * extra, base), place_of(pieces * extra, base)
+        at, column = place_of(2 * pieces * extra, base)
+        to, to_column = place_of(pieces * extra, ext32.shape[1])
         for i in range(n):
             holders = ext[i].astype(F32)[at : at + 1, column : column + LANES]
             ext32[i, to : to + 1, to_column : to_column + LANES] = holders
@@ -277,13 +299,10 @@
             continue
         if stage == "late":
             back = back + partial[:, cols]
-        for i in range(n):
-            outs[i][:, cols] = back[i * base : (i + 1) * base].astype(BF16)
-            if extra:
-                fold(ext32.at[i], back[full + i : full + i + 1], TILE // LANES, at // LANES, base)
+        put_back(outs, ext32, back, at, TILE, n, base, extra, width)
     if stage != "early":
         for i in range(n):
-            outs[i][:, width:] = ext32[i].astype(BF16)
+            outs[i][:, sides_of(base) * width :] = ext32[i].astype(BF16)
 
 
 def late_kernel(n, base, extra, blocks, w_layout, v_layout, *refs):
@@ -302,7 +321,8 @@
     if extra:
         put_extra(g, row32, ext, n, base, pieces)
     ext32[...] = jnp.zeros_like(ext32)
-    (at, column), (to, to_column) = place_of(2 * pieces * extra, base), place_of(pieces * extra, base)
+    at, column = place_of(2 * pieces * extra, base)
+    to, to_column = place_of(pieces * extra, ext32.shape[1])
     for i in range(n):
         holders = ext[i].astype(F32)[at : at + 1, column : column + LANES]
         ext32[i, to : to + 1, to_column : to_column + LANES] = holders
@@ -338,15 +358,12 @@
                     (((1,), (1,)), ((), ())),
                     preferred_element_type=F32,
                 )
-            for i in range(n):
-                outs[i][:, cols] = back[i * base : (i + 1) * base].astype(BF16)
-                if extra:
-                    fold(ext32.at[i], back[full + i : full + i + 1], size // LANES, first // LANES, base)
+            put_back(outs, ext32, back, first, size, n, base, extra, width)
 
     for here in range(2):
         pl.when(core == here)(functools.partial(work, here))
     for i in range(n):
-        outs[i][:, width:] = ext32[i].astype(BF16)
+        outs[i][:, sides_of(base) * width :] = ext32[i].astype(BF16)
 
 
 def flat(columns):
@@ -369,11 +386,11 @@
     width, ff = 2 * half, len(w_columns) * w_layout[0][3]
     rows = n * base + -(-n * extra // 16) * 16
     ext = fold_columns(2 * width // LANES * extra, base)
-    back_ext = fold_columns(width // LANES * extra, base)
+    back_rows, back_cols = back_shape(base, width, extra)
     anywhere, vmem = pl.BlockSpec(memory_space=pl.ANY), pl.BlockSpec(memory_space=pltpu.VMEM)
     return pl.pallas_call(
         functools.partial(late_kernel, n, base, extra, len(w_columns), w_layout, v_layout),
-        out_shape=[jax.ShapeDtypeStruct((base, width + back_ext), BF16) for _ in msgs],
+        out_shape=[jax.ShapeDtypeStruct((back_rows, back_cols), BF16) for _ in msgs],
         in_specs=[anywhere] * n + [vmem] * (len(w_pieces) + len(v_pieces) + len(carried)),
         out_specs=[vmem] * n,
         scratch_shapes=[
@@ -381,7 +398,7 @@
             pltpu.VMEM((rows, ff), BF16),
             pltpu.VMEM((n, base, ext), BF16),
             pltpu.VMEM((max(16, rows - n * base), width), F32),
-            pltpu.VMEM((n, base, back_ext), F32),
+            pltpu.VMEM((n, back_rows, back_cols - sides_of(base) * width), F32),
             pltpu.SemaphoreType.DMA((n, 1)),
             pltpu.SemaphoreType.DMA((n, 1)),
         ],
@@ -406,8 +423,7 @@
     w_ff, v_ff = len(w_columns) * block_ff, len(v_columns) * block_ff
     rows = n * base + -(-n * extra // 16) * 16
     ext = fold_columns(2 * width // LANES * extra, base)
-    back_ext = fold_columns(width // LANES * extra, base)
-    cols = width + back_ext
+    back_rows, back_cols = back_shape(base, width, extra)
     anywhere, vmem = pl.BlockSpec(memory_space=pl.ANY), pl.BlockSpec(memory_space=pltpu.VMEM)
     spare = max(16, rows - n * base)
     own_slope = [] if stage == "late" else [pltpu.VMEM((rows, v_ff), F32)]
@@ -417,7 +433,7 @@
             jax.ShapeDtypeStruct((rows, width), F32),
         ]
     else:
-        out_shape = [jax.ShapeDtypeStruct((base, cols), BF16) for _ in msgs]
+        out_shape = [jax.ShapeDtypeStruct((back_rows, back_cols), BF16) for _ in msgs]
     return pl.pallas_call(
         functools.partial(expert_kernel, n, base, extra, stage, w_layout, v_layout, lengths),
         out_shape=out_shape,
@@ -432,7 +448,7 @@
             pltpu.VMEM((rows, v_ff), BF16),
             pltpu.VMEM((n, base, ext), BF16),
             pltpu.VMEM((spare, width), F32),
-            pltpu.VMEM((n, base, back_ext), F32),
+            pltpu.VMEM((n, back_rows, back_cols - sides_of(base) * width), F32),
             pltpu.SemaphoreType.DMA((n, most)),
             pltpu.SemaphoreType.DMA((n, most)),
             pltpu.SemaphoreType.DMA((n, most)),
@@ -449,21 +465,24 @@
     )(*parts, *w_pieces, *v_pieces, *carried)
 
 
-def add_kernel(n, extra, start_ref, *refs):
-    msgs, (out, rows, ext, row32, places, sem_b, sem_e) = refs[:n], refs[n:]
+def add_kernel(n, base, extra, start_ref, *refs):
+    msgs, (out_hbm, out, rows, ext, row32, places, sem_b, sem_e, sem_o) = refs[:n], refs[n:]
     tokens, width = start_ref.shape
-    base = ext.shape[1]
     pieces = width // LANES
-    copies = []
-    for i, msg in enumerate(msgs):
-        copies.append(begin(msg.at[:, pl.ds(width, ext.shape[2])], ext.at[i], sem_e.at[i]))
-    rows_in = [
-        begin(msg.at[:, pl.ds(0, width)], rows.at[pl.ds(i * base, base), :], sem_b.at[i])
+    part, sides = msgs[0].shape[0], sides_of(base)
+    ext_in = [
+        begin(msg.at[:, pl.ds(sides * width, ext.shape[2])], ext.at[i], sem_e.at[i])
         for i, msg in enumerate(msgs)
     ]
-    finish(copies)
+    rows_in = []
+    for i, msg in enumerate(msgs):
+        for side in range(sides):
+            src = msg.at[:, pl.ds(side * width, width)]
+            dst = rows.at[pl.ds(i * base + side * part, part), :]
+            rows_in.append(begin(src, dst, sem_b.at[i, side]))
+    finish(ext_in)
     folded = jnp.zeros((tokens, 16), F32)
-    at, column = place_of(pieces * extra, base)
+    at, column = place_of(pieces * extra, part)
     for i in range(n):
         holders = ext[i].astype(F32)[at : at + 1, column : column + LANES]
         token = lax.broadcasted_iota(jnp.int32, (tokens, LANES), 0) + 1
@@ -475,31 +494,41 @@
     if extra:
         places[:, n * base :] = folded.astype(BF16)
         put_extra(rows, row32, ext, n, base, 0)
+    place = places[...]
     finish(rows_in)
-    place = places[...]
-    for at in range(0, width, CHUNK):
-        cols = slice(at, at + CHUNK)
-        back = jnp.dot(place, rows[:, cols], preferred_element_type=F32)
-        out[:, cols] = (start_ref[:, cols].astype(F32) + back).astype(out.dtype)
-
-
-def add_returned(start, msgs, extra, kind, name):
+    step = width // 4
+    sent = []
+    for h in range(4):
+        for at in range(h * step, (h + 1) * step, TILE):
+            cols = slice(at, min(at + TILE, (h + 1) * step))
+            back = jnp.dot(place, rows[:, cols], preferred_element_type=F32)
+            out[:, cols] = (start_ref[:, cols].astype(F32) + back).astype(out.dtype)
+        cols = pl.ds(h * step, step)
+        sent.append(begin(out.at[:, cols], out_hbm.at[:, cols], sem_o.at[h]))
+    finish(sent)
+
+
+def add_returned(start, msgs, base, extra, kind, name):
     tokens, width = start.shape
-    n, base = len(msgs), msgs[0].shape[0]
+    n = len(msgs)
     slots = n * base + 16 * extra
+    part, cols = msgs[0].shape
+    sides = sides_of(base)
     anywhere, vmem = pl.BlockSpec(memory_space=pl.ANY), pl.BlockSpec(memory_space=pltpu.VMEM)
     return pl.pallas_call(
-        functools.partial(add_kernel, n, extra),
+        functools.partial(add_kernel, n, base, extra),
         out_shape=jax.ShapeDtypeStruct((tokens, width), kind),
         in_specs=[vmem] + [anywhere] * n,
-        out_specs=vmem,
+        out_specs=anywhere,
         scratch_shapes=[
+            pltpu.VMEM((tokens, width), kind),
             pltpu.VMEM((slots, width), BF16),
-            pltpu.VMEM((n, base, msgs[0].shape[1] - width), BF16),
+            pltpu.VMEM((n, part, cols - sides * width), BF16),
             pltpu.VMEM((16, width), F32),
             pltpu.VMEM((tokens, slots), BF16),
+            pltpu.SemaphoreType.DMA((n, sides)),
             pltpu.SemaphoreType.DMA((n,)),
-            pltpu.SemaphoreType.DMA((n,)),
+            pltpu.SemaphoreType.DMA((4,)),
         ],
         compiler_params=pltpu.CompilerParams(vmem_limit_bytes=24 * MIB),
         cost_estimate=pl.CostEstimate(
@@ -534,7 +563,7 @@
 
 def groups_of(experts):
     if experts == 4:
-        return [[2], [1, 0], [3]], [[2, 0], [3, 1]]
+        return [[2], [1, 0], [3]], [[1, 2], [0, 3]]
     order = list(range(experts - 1, -1, -1))
     size = -(-experts // 4)
     groups = [order[i : i + size] for i in range(0, experts, size)]
@@ -585,7 +614,7 @@
             backs = expert(msgs, base, extra, w_columns, v_columns)
         returned = [swap_back(back, 2 * dist) for dist, back in zip(group, backs)]
         ends = i == len(works) - 1
-        total = add_returned(total, returned, extra, BF16 if ends else F32, "finish" if ends else "settle")
+        total = add_returned(total, returned, base, extra, BF16 if ends else F32, "finish" if ends else "settle")
     return total[None]
 
 

time: 141 us -> 139 us (0.986); the launches traced: 141 us -> 137 us
  Pallas kernels: 28.6 us -> 25.2 us
    pallas_call x3, Pallas kernels: 10.8 us -> 6.52 us  [dispatch(): pl.pallas_call(functools.partial(dispatch_kernel, dists, base, extra, spl...]
    ppermute x4, waiting for transfers between devices: 31.2 us -> 26.9 us  [swap_back(): return lax.ppermute(value, ('section', 'expert'), pairs)]
    ppermute x13, waiting for transfers between devices: 54.7 us -> 57.6 us  [swap(): lax.ppermute(value, axis, [(i, i ^ apart) for i in range(lax.axis_size(ax...]
  transfers between devices with their start and end apart: 17 -> 17, of which waited for: 9 -> 10; matrix products, arithmetic and copies ran while one was open for 0% -> 0% of each run, Pallas kernels for 19% -> 17%
where the time goes in v5:
time: 139 us; the launch traced here: 137 us
  waiting for transfers between devices  84.5 us (61%)
  starting transfers between devices  27.1 us (19%)
  Pallas kernels  25.2 us (18%)
    ppermute x13, waiting for transfers between devices, swap(): lax.ppermute(value, axis, [(i, i ^ apart) for i in range(lax.axis_size(ax...  57.6 us
    ppermute x4, waiting for transfers between devices, swap_back(): return lax.ppermute(value, ('section', 'expert'), pairs)  26.9 us
    ppermute x13, starting transfers between devices, swap(): lax.ppermute(value, axis, [(i, i ^ apart) for i in range(lax.axis_size(ax...  18.5 us
    pallas_call x2, Pallas kernels, expert(): pl.pallas_call(functools.partial(expert_kernel, n, base, extra, stage, w_...  13.1 us
    ppermute x4, starting transfers between devices, swap_back(): return lax.ppermute(value, ('section', 'expert'), pairs)  8.56 us
    pallas_call x3, Pallas kernels, dispatch(): pl.pallas_call(functools.partial(dispatch_kernel, dists, base, extra, spl...  6.52 us
    pallas_call x2, Pallas kernels, add_returned(): pl.pallas_call(functools.partial(add_kernel, n, base, extra), out_shape=j...  3.25 us
  transfers between devices with their start and end apart: 17, of which 10 were waited for; matrix products, arithmetic and copies ran while one was open for 0% of the time, Pallas kernels for 17%

profile of v5, /device:TPU:0, one launch (start us, length us, event | category | flops | bytes accessed | tf_op | source)
XLA Modules:
  0.0 137.2 jit_solution(10063446499992025941)
XLA Ops:
  0.0 0.0 copy-start.5
  0.0 0.0 copy-start.4
  0.0 0.0 copy-start.1
  0.0 0.0 copy-start
  0.0 0.5 collective-permute-start.7
  0.5 0.1 collective-permute-start.8
  0.6 2.9 %collective-permute-start.1 = (bf16[1792,512]{1,0:T(8,128)(2,1)}, bf16[1792,512]{1,0:T(8,128)(2,1)S(1)}, u32[]{:S(2)}, u32[]{:S(2)}) collective-permute-start(bf16[1792,512]{1,0:T(8,128)(2,1)} %bitcast.19), channel_id=1, source_target_pairs={{0,1},{1,0},{2,3},{3,2},{4,5},{5,4},{6,7},{7,6},{8,9},{9,8},{10,11... | collective-permute-start | bytes 5505032 | tf_op jit(solution)/shard_map/ppermute | solution.py:544
  3.6 0.0 copy-start.3
  3.6 2.8 %dispatch.4 = bf16[64,7296]{1,0:T(8,128)(2,1)} custom-call(s32[2,128]{1,0:T(2,128)} %bitcast.26, f32[2,128]{1,0:T(2,128)} %bitcast.29, bf16[128,3584]{1,0:T(8,128)(2,1)} %bitcast.11, bf16[128,3584]{1,0:T(8,128)(2,1)} %bitcast.14), custom_call_target="tpu_custom_call" | custom-call | flops 146800640 | bytes 2768896 | tf_op jit(solution)/shard_map/dispatch/pallas_call | solution.py:150
  6.4 2.7 %collective-permute-start.2 = (bf16[64,7296]{1,0:T(8,128)(2,1)}, bf16[64,7296]{1,0:T(8,128)(2,1)S(1)}, u32[]{:S(2)}, u32[]{:S(2)}) collective-permute-start(bf16[64,7296]{1,0:T(8,128)(2,1)} %dispatch.4), channel_id=1, source_target_pairs={{0,8},{2,10},{4,12},{6,14},{8,0},{10,2},{12,4},{14,6},{1,9},{3,11}... | collective-permute-start | bytes 2801672 | tf_op jit(solution)/shard_map/ppermute | solution.py:544
  9.0 0.0 copy-done.5
  9.0 0.0 copy-done.4
  9.0 0.0 copy-done.1
  9.0 0.0 copy-done
  9.0 2.2 %dispatch.5 = (bf16[64,7296]{1,0:T(8,128)(2,1)S(1)}, bf16[64,7296]{1,0:T(8,128)(2,1)S(1)}) custom-call(s32[2,128]{1,0:T(2,128)S(1)} %bitcast.27, f32[2,128]{1,0:T(2,128)S(1)} %bitcast.30, bf16[128,3584]{1,0:T(8,128)(2,1)S(1)} %bitcast.12, bf16[128,3584]{1,0:T(8,128)(2,1)S(1)} %bitcast.15), custom_call_target="tpu_custom_call" | custom-call | flops 293601280 | bytes 3702784 | tf_op jit(solution)/shard_map/dispatch/pallas_call | solution.py:150
  11.3 1.7 %collective-permute-start.3 = (bf16[64,7296]{1,0:T(8,128)(2,1)S(1)}, bf16[64,7296]{1,0:T(8,128)(2,1)S(1)}, u32[]{:S(2)}, u32[]{:S(2)}) collective-permute-start(bf16[64,7296]{1,0:T(8,128)(2,1)S(1)} %get-tuple-element.39), channel_id=1, source_target_pairs={{0,4},{2,6},{4,0},{6,2},{8,12},{10,14},{12,8},{14,10},{1,5},{3,7},... | collective-permute-start | bytes 2801672 | tf_op jit(solution)/shard_map/ppermute | solution.py:544
  12.9 0.0 collective-permute-done.7.refs_3_.refs_4_
  12.9 1.5 %collective-permute-start = (bf16[128,3584]{1,0:T(8,128)(2,1)S(1)}, bf16[128,3584]{1,0:T(8,128)(2,1)S(1)}, u32[]{:S(2)}, u32[]{:S(2)}) collective-permute-start(bf16[128,3584]{1,0:T(8,128)(2,1)S(1)} %bitcast.16), channel_id=1, source_target_pairs={{0,16},{16,0},{1,17},{17,1},{2,18},{18,2},{3,19},{19,3},{4,20},{20... | collective-permute-start | bytes 2752520 | tf_op jit(solution)/shard_map/ppermute | solution.py:544
  14.4 0.0 collective-permute-done.8.refs_9_.refs_10_
  14.4 0.0 copy-done.3
  14.4 0.5 collective-permute-start.9
  14.9 1.5 %dispatch.3 = (bf16[64,6528]{1,0:T(8,128)(2,1)S(1)}, bf16[64,768]{1,0:T(8,128)(2,1)S(1)}) custom-call(s32[2,128]{1,0:T(2,128)S(1)} %bitcast.28, f32[2,128]{1,0:T(2,128)S(1)} %bitcast.31, bf16[128,3584]{1,0:T(8,128)(2,1)S(1)} %bitcast.13, bf16[128,3584]{1,0:T(8,128)(2,1)S(1)} %bitcast.17), custom_call_target="tpu_custom_call" | custom-call | flops 146800640 | bytes 2768896 | tf_op jit(solution)/shard_map/dispatch/pallas_call | solution.py:150
  16.4 18.0 %collective-permute-done.start_ref = bf16[128,3584]{1,0:T(8,128)(2,1)S(1)} collective-permute-done((bf16[128,3584]{1,0:T(8,128)(2,1)S(1)}, bf16[128,3584]{1,0:T(8,128)(2,1)S(1)}, u32[]{:S(2)}, u32[]{:S(2)}) %collective-permute-start) | collective-permute-done | bytes 917536 | tf_op jit(solution)/shard_map/ppermute | solution.py:544
  34.4 10.2 %collective-permute-done.1.refs_4_.refs_2_.refs_5_ = bf16[1792,512]{1,0:T(8,128)(2,1)S(1)} collective-permute-done((bf16[1792,512]{1,0:T(8,128)(2,1)}, bf16[1792,512]{1,0:T(8,128)(2,1)S(1)}, u32[]{:S(2)}, u32[]{:S(2)}) %collective-permute-start.1) | collective-permute-done | bytes 1835040 | tf_op jit(solution)/shard_map/ppermute | solution.py:544
  44.6 4.1 %collective-permute-start.10 = (bf16[64,6528]{1,0:T(8,128)(2,1)S(1)}, bf16[64,6528]{1,0:T(8,128)(2,1)S(1)}, u32[]{:S(2)}, u32[]{:S(2)}) collective-permute-start(bf16[64,6528]{1,0:T(8,128)(2,1)S(1)} %get-tuple-element.45), channel_id=1, source_target_pairs={{0,12},{2,14},{4,8},{6,10},{8,4},{10,6},{12,0},{14,2},{1,13},{3,15... | collective-permute-start | bytes 2506760 | tf_op jit(solution)/shard_map/ppermute | solution.py:544
  48.7 20.4 %collective-permute-done.2.refs_1_ = bf16[64,7296]{1,0:T(8,128)(2,1)S(1)} collective-permute-done((bf16[64,7296]{1,0:T(8,128)(2,1)}, bf16[64,7296]{1,0:T(8,128)(2,1)S(1)}, u32[]{:S(2)}, u32[]{:S(2)}) %collective-permute-start.2) | collective-permute-done | bytes 933920 | tf_op jit(solution)/shard_map/ppermute | solution.py:544
  69.1 1.2 collective-permute-done.3.refs_0_
  70.3 0.0 copy-start.2
  70.3 0.1 fusion
  70.4 0.1 collective-permute-start.5
  70.4 0.5 collective-permute-start.4
  71.0 0.1 collective-permute-start.6
  71.1 3.1 %collective-permute-done.6.refs_7_.refs_5_.refs_8_ = bf16[512,512]{1,0:T(8,128)(2,1)S(1)} collective-permute-done((bf16[512,512]{1,0:T(8,128)(2,1)S(1)}, bf16[512,512]{1,0:T(8,128)(2,1)S(1)}, u32[]{:S(2)}, u32[]{:S(2)}) %collective-permute-start.6) | collective-permute-done | bytes 524320 | tf_op jit(solution)/shard_map/ppermute | solution.py:544
  74.2 0.0 collective-permute-done.5.refs_6_.refs_4_.refs_7_
  74.2 0.0 collective-permute-done.4.refs_5_.refs_3_.refs_6_
  74.2 0.0 copy-done.2
  74.2 5.6 %expert_early.1 = (f32[144,512]{1,0:T(8,128)S(1)}, f32[144,3584]{1,0:T(8,128)S(1)}) custom-call(bf16[64,7296]{1,0:T(8,128)(2,1)S(1)} %collective-permute-done.3.refs_0_, bf16[64,7296]{1,0:T(8,128)(2,1)S(1)} %collective-permute-done.2.refs_1_, bf16[1792,512]{1,0:T(8,128)(2,1)S(1)} %bitcast.20, bf16[1792,512]{1,0:T(8,128)(2,1)} %collective-permute-done.7.refs_3_.refs_4_, ...), custom_call_target="tpu_custom_call" | custom-call | tf_op jit(solution)/shard_map/expert_early/pallas_call | solution.py:437
  79.8 0.0 collective-permute-done.10.refs_1_
  79.8 3.5 %collective-permute-done.9.refs_6_.refs_11_ = bf16[1792,512]{1,0:T(8,128)(2,1)S(1)} collective-permute-done((bf16[1792,512]{1,0:T(8,128)(2,1)S(1)}, bf16[1792,512]{1,0:T(8,128)(2,1)S(1)}, u32[]{:S(2)}, u32[]{:S(2)}) %collective-permute-start.9) | collective-permute-done | bytes 1835040 | tf_op jit(solution)/shard_map/ppermute | solution.py:544
  83.4 0.0 collective-permute-start.11
  83.4 3.8 %collective-permute-start.12 = (bf16[64,768]{1,0:T(8,128)(2,1)S(1)}, bf16[64,768]{1,0:T(8,128)(2,1)S(1)}, u32[]{:S(2)}, u32[]{:S(2)}) collective-permute-start(bf16[64,768]{1,0:T(8,128)(2,1)S(1)} %get-tuple-element.57), channel_id=1, source_target_pairs={{0,12},{2,14},{4,8},{6,10},{8,4},{10,6},{12,0},{14,2},{1,13},{3,15... | collective-permute-start | bytes 294920 | tf_op jit(solution)/shard_map/ppermute | solution.py:544
  87.2 0.0 collective-permute-done.11.refs_7_.refs_12_
  87.2 2.3 %expert_late.1 = (bf16[32,7296]{1,0:T(8,128)(2,1)S(1)}, bf16[32,7296]{1,0:T(8,128)(2,1)S(1)}) custom-call(bf16[64,7296]{1,0:T(8,128)(2,1)S(1)} %collective-permute-done.3.refs_0_, bf16[64,7296]{1,0:T(8,128)(2,1)S(1)} %collective-permute-done.2.refs_1_, bf16[1792,512]{1,0:T(8,128)(2,1)S(1)} %collective-permute-done.1.refs_4_.refs_2_.refs_5_, ...), custom_call_target="tpu_custom_call" | custom-call | flops 1056964608 | bytes 11468800 | tf_op jit(solution)/shard_map/expert_late/pallas_call | solution.py:391
  89.5 1.2 collective-permute-done.12.refs_2_
  90.7 3.7 %collective-permute-start.13 = (bf16[32,7296]{1,0:T(8,128)(2,1)S(1)}, bf16[32,7296]{1,0:T(8,128)(2,1)S(1)}, u32[]{:S(2)}, u32[]{:S(2)}) collective-permute-start(bf16[32,7296]{1,0:T(8,128)(2,1)S(1)} %get-tuple-element.58), channel_id=1, source_target_pairs={{0,20},{2,22},{4,16},{6,18},{8,28},{10,30},{12,24},{14,26},{16,4},... | collective-permute-start | bytes 1400840 | tf_op jit(solution)/shard_map/ppermute | solution.py:552
  94.4 1.9 %collective-permute-start.14 = (bf16[32,7296]{1,0:T(8,128)(2,1)S(1)}, bf16[32,7296]{1,0:T(8,128)(2,1)S(1)}, u32[]{:S(2)}, u32[]{:S(2)}) collective-permute-start(bf16[32,7296]{1,0:T(8,128)(2,1)S(1)} %get-tuple-element.59), channel_id=1, source_target_pairs={{0,24},{2,26},{4,28},{6,30},{8,16},{10,18},{12,20},{14,22},{16,8},... | collective-permute-start | bytes 1400840 | tf_op jit(solution)/shard_map/ppermute | solution.py:552
  96.3 7.5 %expert_whole.1 = (bf16[32,7296]{1,0:T(8,128)(2,1)S(1)}, bf16[32,7296]{1,0:T(8,128)(2,1)S(1)}) custom-call(bf16[64,7296]{1,0:T(8,128)(2,1)S(1)} %get-tuple-element.60.refs_0_, bf16[64,6528]{1,0:T(8,128)(2,1)S(1)} %collective-permute-done.10.refs_1_, bf16[64,768]{1,0:T(8,128)(2,1)S(1)} %collective-permute-done.12.refs_2_, bf16[1792,512]{1,0:T(8,128)(2,1)S(1)} %bitcast.21, ...), custom_call_target="tpu_custom_call" | custom-call | flops 3170893824 | bytes 17776640 | tf_op jit(solution)/shard_map/expert_whole/pallas_call | solution.py:437
  103.9 1.0 collective-permute-start.15
  104.9 2.0 %collective-permute-start.16 = (bf16[32,7296]{1,0:T(8,128)(2,1)S(1)}, bf16[32,7296]{1,0:T(8,128)(2,1)S(1)}, u32[]{:S(2)}, u32[]{:S(2)}) collective-permute-start(bf16[32,7296]{1,0:T(8,128)(2,1)S(1)} %get-tuple-element.64), channel_id=1, source_target_pairs={{0,28},{2,30},{4,24},{6,26},{8,20},{10,22},{12,16},{14,18},{16,12}... | collective-permute-start | bytes 1400840 | tf_op jit(solution)/shard_map/ppermute | solution.py:552
  106.9 8.5 %collective-permute-done.13.refs_0_ = bf16[32,7296]{1,0:T(8,128)(2,1)S(1)} collective-permute-done((bf16[32,7296]{1,0:T(8,128)(2,1)S(1)}, bf16[32,7296]{1,0:T(8,128)(2,1)S(1)}, u32[]{:S(2)}, u32[]{:S(2)}) %collective-permute-start.13) | collective-permute-done | bytes 466976 | tf_op jit(solution)/shard_map/ppermute | solution.py:552
  115.3 13.4 %collective-permute-done.14.refs_1_ = bf16[32,7296]{1,0:T(8,128)(2,1)S(1)} collective-permute-done((bf16[32,7296]{1,0:T(8,128)(2,1)S(1)}, bf16[32,7296]{1,0:T(8,128)(2,1)S(1)}, u32[]{:S(2)}, u32[]{:S(2)}) %collective-permute-start.14) | collective-permute-done | bytes 466976 | tf_op jit(solution)/shard_map/ppermute | solution.py:552
  128.8 1.6 %settle.1.start_ref = f32[128,3584]{1,0:T(8,128)S(1)} custom-call(bf16[128,3584]{1,0:T(8,128)(2,1)S(1)} %collective-permute-done.start_ref, bf16[32,7296]{1,0:T(8,128)(2,1)S(1)} %collective-permute-done.13.refs_0_, bf16[32,7296]{1,0:T(8,128)(2,1)S(1)} %collective-permute-done.14.refs_1_), custom_call_target="tpu_custom_call" | custom-call | flops 132120576 | bytes 3784704 | tf_op jit(solution)/shard_map/settle/pallas_call | solution.py:518
  130.3 5.0 %collective-permute-done.15.refs_0_ = bf16[32,7296]{1,0:T(8,128)(2,1)S(1)} collective-permute-done((bf16[32,7296]{1,0:T(8,128)(2,1)S(1)}, bf16[32,7296]{1,0:T(8,128)(2,1)S(1)}, u32[]{:S(2)}, u32[]{:S(2)}) %collective-permute-start.15) | collective-permute-done | bytes 466976 | tf_op jit(solution)/shard_map/ppermute | solution.py:552
  135.4 0.0 collective-permute-done.16.refs_1_
  135.4 1.7 %finish.1 = bf16[128,3584]{1,0:T(8,128)(2,1)} custom-call(f32[128,3584]{1,0:T(8,128)S(1)} %settle.1.start_ref, bf16[32,7296]{1,0:T(8,128)(2,1)S(1)} %collective-permute-done.15.refs_0_, bf16[32,7296]{1,0:T(8,128)(2,1)S(1)} %collective-permute-done.16.refs_1_), custom_call_target="tpu_custom_call" | custom-call | flops 132120576 | bytes 3784704 | tf_op jit(solution)/shard_map/finish/pallas_call | solution.py:518
  (1 shorter events, 0.0 us)
Async XLA Ops:
  0.0 9.0 %copy-start.5 = (f32[1,128,2]{1,2,0:T(2,128)S(1)}, f32[1,128,2]{1,2,0:T(2,128)}, u32[]{:S(2)}) copy-start(f32[1,128,2]{1,2,0:T(2,128)} %param.9) | copy-start | bytes 3076
  0.0 9.0 %copy-start.4 = (s32[1,128,2]{1,2,0:T(2,128)S(1)}, s32[1,128,2]{1,2,0:T(2,128)}, u32[]{:S(2)}) copy-start(s32[1,128,2]{1,2,0:T(2,128)} %param.8) | copy-start | bytes 3076
  0.0 9.0 %copy-start.1 = (bf16[1,128,3584]{2,1,0:T(8,128)(2,1)S(1)}, bf16[1,128,3584]{2,1,0:T(8,128)(2,1)}, u32[]{:S(2)}) copy-start(bf16[1,128,3584]{2,1,0:T(8,128)(2,1)} %param.7) | copy-start | bytes 2752516
  0.0 9.0 %copy-start = (bf16[1,128,3584]{2,1,0:T(8,128)(2,1)S(1)}, bf16[1,128,3584]{2,1,0:T(8,128)(2,1)}, u32[]{:S(2)}) copy-start(bf16[1,128,3584]{2,1,0:T(8,128)(2,1)} %param.6) | copy-start | bytes 2752516
  0.0 12.9 %collective-permute-start.7 = (bf16[1792,512]{1,0:T(8,128)(2,1)}, bf16[1792,512]{1,0:T(8,128)(2,1)}, u32[]{:S(2)}, u32[]{:S(2)}) collective-permute-start(bf16[1792,512]{1,0:T(8,128)(2,1)} %bitcast.18), channel_id=1, source_target_pairs={{0,2},{2,0},{4,6},{6,4},{8,10},{10,8},{12,14},{14,12},{1,3},{3,1},... | collective-permute-start | bytes 5505032 | tf_op jit(solution)/shard_map/ppermute | solution.py:544
  0.5 13.9 %collective-permute-start.8 = (bf16[1792,512]{1,0:T(8,128)(2,1)}, bf16[1792,512]{1,0:T(8,128)(2,1)}, u32[]{:S(2)}, u32[]{:S(2)}) collective-permute-start(bf16[1792,512]{1,0:T(8,128)(2,1)} %bitcast.22), channel_id=1, source_target_pairs={{0,2},{2,0},{4,6},{6,4},{8,10},{10,8},{12,14},{14,12},{1,3},{3,1},... | collective-permute-start | bytes 5505032 | tf_op jit(solution)/shard_map/ppermute | solution.py:544
  0.6 44.0 %collective-permute-start.1 = (bf16[1792,512]{1,0:T(8,128)(2,1)}, bf16[1792,512]{1,0:T(8,128)(2,1)S(1)}, u32[]{:S(2)}, u32[]{:S(2)}) collective-permute-start(bf16[1792,512]{1,0:T(8,128)(2,1)} %bitcast.19), channel_id=1, source_target_pairs={{0,1},{1,0},{2,3},{3,2},{4,5},{5,4},{6,7},{7,6},{8,9},{9,8},{10,11... | collective-permute-start | bytes 5505032 | tf_op jit(solution)/shard_map/ppermute | solution.py:544
  3.6 10.9 %copy-start.3 = (bf16[1,1,1792,512]{3,2,1,0:T(8,128)(2,1)S(1)}, bf16[1,1,1792,512]{3,2,1,0:T(8,128)(2,1)}, u32[]{:S(2)}) copy-start(bf16[1,1,1792,512]{3,2,1,0:T(8,128)(2,1)} %param.11) | copy-start | bytes 5505028
  6.4 62.7 %collective-permute-start.2 = (bf16[64,7296]{1,0:T(8,128)(2,1)}, bf16[64,7296]{1,0:T(8,128)(2,1)S(1)}, u32[]{:S(2)}, u32[]{:S(2)}) collective-permute-start(bf16[64,7296]{1,0:T(8,128)(2,1)} %dispatch.4), channel_id=1, source_target_pairs={{0,8},{2,10},{4,12},{6,14},{8,0},{10,2},{12,4},{14,6},{1,9},{3,11}... | collective-permute-start | bytes 2801672 | tf_op jit(solution)/shard_map/ppermute | solution.py:544
  11.3 59.0 %collective-permute-start.3 = (bf16[64,7296]{1,0:T(8,128)(2,1)S(1)}, bf16[64,7296]{1,0:T(8,128)(2,1)S(1)}, u32[]{:S(2)}, u32[]{:S(2)}) collective-permute-start(bf16[64,7296]{1,0:T(8,128)(2,1)S(1)} %get-tuple-element.39), channel_id=1, source_target_pairs={{0,4},{2,6},{4,0},{6,2},{8,12},{10,14},{12,8},{14,10},{1,5},{3,7},... | collective-permute-start | bytes 2801672 | tf_op jit(solution)/shard_map/ppermute | solution.py:544
  12.9 21.5 %collective-permute-start = (bf16[128,3584]{1,0:T(8,128)(2,1)S(1)}, bf16[128,3584]{1,0:T(8,128)(2,1)S(1)}, u32[]{:S(2)}, u32[]{:S(2)}) collective-permute-start(bf16[128,3584]{1,0:T(8,128)(2,1)S(1)} %bitcast.16), channel_id=1, source_target_pairs={{0,16},{16,0},{1,17},{17,1},{2,18},{18,2},{3,19},{19,3},{4,20},{20... | collective-permute-start | bytes 2752520 | tf_op jit(solution)/shard_map/ppermute | solution.py:544
  14.4 68.9 %collective-permute-start.9 = (bf16[1792,512]{1,0:T(8,128)(2,1)S(1)}, bf16[1792,512]{1,0:T(8,128)(2,1)S(1)}, u32[]{:S(2)}, u32[]{:S(2)}) collective-permute-start(bf16[1792,512]{1,0:T(8,128)(2,1)S(1)} %bitcast.23), channel_id=1, source_target_pairs={{0,1},{1,0},{2,3},{3,2},{4,5},{5,4},{6,7},{7,6},{8,9},{9,8},{10,11... | collective-permute-start | bytes 5505032 | tf_op jit(solution)/shard_map/ppermute | solution.py:544
  44.6 35.2 %collective-permute-start.10 = (bf16[64,6528]{1,0:T(8,128)(2,1)S(1)}, bf16[64,6528]{1,0:T(8,128)(2,1)S(1)}, u32[]{:S(2)}, u32[]{:S(2)}) collective-permute-start(bf16[64,6528]{1,0:T(8,128)(2,1)S(1)} %get-tuple-element.45), channel_id=1, source_target_pairs={{0,12},{2,14},{4,8},{6,10},{8,4},{10,6},{12,0},{14,2},{1,13},{3,15... | collective-permute-start | bytes 2506760 | tf_op jit(solution)/shard_map/ppermute | solution.py:544
  70.3 4.0 %copy-start.2 = (bf16[1,1,1792,512]{3,2,1,0:T(8,128)(2,1)S(1)}, bf16[1,1,1792,512]{3,2,1,0:T(8,128)(2,1)}, u32[]{:S(2)}) copy-start(bf16[1,1,1792,512]{3,2,1,0:T(8,128)(2,1)} %param.10) | copy-start | bytes 5505028
  70.4 3.9 %collective-permute-start.5 = (bf16[640,512]{1,0:T(8,128)(2,1)S(1)}, bf16[640,512]{1,0:T(8,128)(2,1)S(1)}, u32[]{:S(2)}, u32[]{:S(2)}) collective-permute-start(bf16[640,512]{1,0:T(8,128)(2,1)S(1)} %get-tuple-element.65), channel_id=1, source_target_pairs={{0,2},{2,0},{4,6},{6,4},{8,10},{10,8},{12,14},{14,12},{1,3},{3,1},... | collective-permute-start | bytes 1966088 | tf_op jit(solution)/shard_map/ppermute | solution.py:544
  70.4 3.8 %collective-permute-start.4 = (bf16[640,512]{1,0:T(8,128)(2,1)S(1)}, bf16[640,512]{1,0:T(8,128)(2,1)S(1)}, u32[]{:S(2)}, u32[]{:S(2)}) collective-permute-start(bf16[640,512]{1,0:T(8,128)(2,1)S(1)} %get-tuple-element.66), channel_id=1, source_target_pairs={{0,2},{2,0},{4,6},{6,4},{8,10},{10,8},{12,14},{14,12},{1,3},{3,1},... | collective-permute-start | bytes 1966088 | tf_op jit(solution)/shard_map/ppermute | solution.py:544
  71.0 3.2 %collective-permute-start.6 = (bf16[512,512]{1,0:T(8,128)(2,1)S(1)}, bf16[512,512]{1,0:T(8,128)(2,1)S(1)}, u32[]{:S(2)}, u32[]{:S(2)}) collective-permute-start(bf16[512,512]{1,0:T(8,128)(2,1)S(1)} %slice.11), channel_id=1, source_target_pairs={{0,2},{2,0},{4,6},{6,4},{8,10},{10,8},{12,14},{14,12},{1,3},{3,1},... | collective-permute-start | bytes 1572872 | tf_op jit(solution)/shard_map/ppermute | solution.py:544
  83.4 3.8 %collective-permute-start.11 = (bf16[1792,512]{1,0:T(8,128)(2,1)S(1)}, bf16[1792,512]{1,0:T(8,128)(2,1)S(1)}, u32[]{:S(2)}, u32[]{:S(2)}) collective-permute-start(bf16[1792,512]{1,0:T(8,128)(2,1)S(1)} %collective-permute-done.9.refs_6_.refs_11_), channel_id=1, source_target_pairs={{0,2},{2,0},{4,6},{6,4},{8,10},{10,8},{12,14},{14,12},{1,3},{3,1},... | collective-permute-start | bytes 5505032 | tf_op jit(solution)/shard_map/ppermute | solution.py:544
  83.4 7.4 %collective-permute-start.12 = (bf16[64,768]{1,0:T(8,128)(2,1)S(1)}, bf16[64,768]{1,0:T(8,128)(2,1)S(1)}, u32[]{:S(2)}, u32[]{:S(2)}) collective-permute-start(bf16[64,768]{1,0:T(8,128)(2,1)S(1)} %get-tuple-element.57), channel_id=1, source_target_pairs={{0,12},{2,14},{4,8},{6,10},{8,4},{10,6},{12,0},{14,2},{1,13},{3,15... | collective-permute-start | bytes 294920 | tf_op jit(solution)/shard_map/ppermute | solution.py:544
  90.7 24.6 %collective-permute-start.13 = (bf16[32,7296]{1,0:T(8,128)(2,1)S(1)}, bf16[32,7296]{1,0:T(8,128)(2,1)S(1)}, u32[]{:S(2)}, u32[]{:S(2)}) collective-permute-start(bf16[32,7296]{1,0:T(8,128)(2,1)S(1)} %get-tuple-element.58), channel_id=1, source_target_pairs={{0,20},{2,22},{4,16},{6,18},{8,28},{10,30},{12,24},{14,26},{16,4},... | collective-permute-start | bytes 1400840 | tf_op jit(solution)/shard_map/ppermute | solution.py:552
  94.4 34.3 %collective-permute-start.14 = (bf16[32,7296]{1,0:T(8,128)(2,1)S(1)}, bf16[32,7296]{1,0:T(8,128)(2,1)S(1)}, u32[]{:S(2)}, u32[]{:S(2)}) collective-permute-start(bf16[32,7296]{1,0:T(8,128)(2,1)S(1)} %get-tuple-element.59), channel_id=1, source_target_pairs={{0,24},{2,26},{4,28},{6,30},{8,16},{10,18},{12,20},{14,22},{16,8},... | collective-permute-start | bytes 1400840 | tf_op jit(solution)/shard_map/ppermute | solution.py:552
  103.9 31.5 %collective-permute-start.15 = (bf16[32,7296]{1,0:T(8,128)(2,1)S(1)}, bf16[32,7296]{1,0:T(8,128)(2,1)S(1)}, u32[]{:S(2)}, u32[]{:S(2)}) collective-permute-start(bf16[32,7296]{1,0:T(8,128)(2,1)S(1)} %get-tuple-element.63), channel_id=1, source_target_pairs={{0,16},{2,18},{4,20},{6,22},{8,24},{10,26},{12,28},{14,30},{16,0},... | collective-permute-start | bytes 1400840 | tf_op jit(solution)/shard_map/ppermute | solution.py:552
  104.9 30.5 %collective-permute-start.16 = (bf16[32,7296]{1,0:T(8,128)(2,1)S(1)}, bf16[32,7296]{1,0:T(8,128)(2,1)S(1)}, u32[]{:S(2)}, u32[]{:S(2)}) collective-permute-start(bf16[32,7296]{1,0:T(8,128)(2,1)S(1)} %get-tuple-element.64), channel_id=1, source_target_pairs={{0,28},{2,30},{4,24},{6,26},{8,20},{10,22},{12,16},{14,18},{16,12}... | collective-permute-start | bytes 1400840 | tf_op jit(solution)/shard_map/ppermute | solution.py:552

commit v6 on v5

--- a/solution.py
+++ b/solution.py
@@ -15,7 +15,7 @@
 CHUNK = 512
 PARTS = 1
 LIMIT = 57
-TAIL = 5
+TAIL = 8
 CUTS = 3
 
 
@@ -609,7 +609,8 @@
         msgs = [got[dist] for dist in group]
         if i == 0:
             backs = expert_late(msgs, base, extra, w_columns[1:], v_columns[1:], carried)
-            backs, got = after(backs, got)
+            backs, heads = after(backs, {dist: parts[:1] for dist, parts in got.items()})
+            got = {dist: heads[dist] + parts[1:] for dist, parts in got.items()}
         else:
             backs = expert(msgs, base, extra, w_columns, v_columns)
         returned = [swap_back(back, 2 * dist) for dist, back in zip(group, backs)]

time: 139 us -> 136 us (0.978)
  transfers between devices with their start and end apart: 17 -> 17, of which waited for: 10 -> 9; matrix products, arithmetic and copies ran while one was open for 0% -> 0% of each run, Pallas kernels for 17% -> 17%
where the time goes in v6:
time: 136 us; the launch traced here: 135 us
  waiting for transfers between devices  83.6 us (61%)
  starting transfers between devices  25.9 us (19%)
  Pallas kernels  25.2 us (19%)
    ppermute x13, waiting for transfers between devices, swap(): lax.ppermute(value, axis, [(i, i ^ apart) for i in range(lax.axis_size(ax...  56.4 us
    ppermute x4, waiting for transfers between devices, swap_back(): return lax.ppermute(value, ('section', 'expert'), pairs)  27.2 us
    ppermute x13, starting transfers between devices, swap(): lax.ppermute(value, axis, [(i, i ^ apart) for i in range(lax.axis_size(ax...  18.5 us
    pallas_call x2, Pallas kernels, expert(): pl.pallas_call(functools.partial(expert_kernel, n, base, extra, stage, w_...  13.1 us
    ppermute x4, starting transfers between devices, swap_back(): return lax.ppermute(value, ('section', 'expert'), pairs)  7.36 us
    pallas_call x3, Pallas kernels, dispatch(): pl.pallas_call(functools.partial(dispatch_kernel, dists, base, extra, spl...  6.52 us
    pallas_call x2, Pallas kernels, add_returned(): pl.pallas_call(functools.partial(add_kernel, n, base, extra), out_shape=j...  3.25 us
  transfers between devices with their start and end apart: 17, of which 9 were waited for; matrix products, arithmetic and copies ran while one was open for 0% of the time, Pallas kernels for 17%

profile of v6, /device:TPU:0, one launch (start us, length us, event | category | flops | bytes accessed | tf_op | source)
XLA Modules:
  0.0 135.1 jit_solution(12959664545329700679)
XLA Ops:
  0.0 0.0 copy-start.5
  0.0 0.0 copy-start.4
  0.0 0.0 copy-start.1
  0.0 0.0 copy-start
  0.0 0.5 collective-permute-start.7
  0.5 0.1 collective-permute-start.8
  0.6 2.9 %collective-permute-start.1 = (bf16[1792,512]{1,0:T(8,128)(2,1)}, bf16[1792,512]{1,0:T(8,128)(2,1)S(1)}, u32[]{:S(2)}, u32[]{:S(2)}) collective-permute-start(bf16[1792,512]{1,0:T(8,128)(2,1)} %bitcast.19), channel_id=1, source_target_pairs={{0,1},{1,0},{2,3},{3,2},{4,5},{5,4},{6,7},{7,6},{8,9},{9,8},{10,11... | collective-permute-start | bytes 5505032 | tf_op jit(solution)/shard_map/ppermute | solution.py:544
  3.6 0.0 copy-start.3
  3.6 2.8 %dispatch.4 = bf16[64,7296]{1,0:T(8,128)(2,1)} custom-call(s32[2,128]{1,0:T(2,128)} %bitcast.26, f32[2,128]{1,0:T(2,128)} %bitcast.29, bf16[128,3584]{1,0:T(8,128)(2,1)} %bitcast.11, bf16[128,3584]{1,0:T(8,128)(2,1)} %bitcast.14), custom_call_target="tpu_custom_call" | custom-call | flops 146800640 | bytes 2768896 | tf_op jit(solution)/shard_map/dispatch/pallas_call | solution.py:150
  6.4 2.7 %collective-permute-start.2 = (bf16[64,7296]{1,0:T(8,128)(2,1)}, bf16[64,7296]{1,0:T(8,128)(2,1)S(1)}, u32[]{:S(2)}, u32[]{:S(2)}) collective-permute-start(bf16[64,7296]{1,0:T(8,128)(2,1)} %dispatch.4), channel_id=1, source_target_pairs={{0,8},{2,10},{4,12},{6,14},{8,0},{10,2},{12,4},{14,6},{1,9},{3,11}... | collective-permute-start | bytes 2801672 | tf_op jit(solution)/shard_map/ppermute | solution.py:544
  9.0 0.0 copy-done.5
  9.0 0.0 copy-done.4
  9.0 0.0 copy-done.1
  9.0 0.0 copy-done
  9.0 2.2 %dispatch.5 = (bf16[64,7296]{1,0:T(8,128)(2,1)S(1)}, bf16[64,7296]{1,0:T(8,128)(2,1)S(1)}) custom-call(s32[2,128]{1,0:T(2,128)S(1)} %bitcast.27, f32[2,128]{1,0:T(2,128)S(1)} %bitcast.30, bf16[128,3584]{1,0:T(8,128)(2,1)S(1)} %bitcast.12, bf16[128,3584]{1,0:T(8,128)(2,1)S(1)} %bitcast.15), custom_call_target="tpu_custom_call" | custom-call | flops 293601280 | bytes 3702784 | tf_op jit(solution)/shard_map/dispatch/pallas_call | solution.py:150
  11.3 1.7 %collective-permute-start.3 = (bf16[64,7296]{1,0:T(8,128)(2,1)S(1)}, bf16[64,7296]{1,0:T(8,128)(2,1)S(1)}, u32[]{:S(2)}, u32[]{:S(2)}) collective-permute-start(bf16[64,7296]{1,0:T(8,128)(2,1)S(1)} %get-tuple-element.38), channel_id=1, source_target_pairs={{0,4},{2,6},{4,0},{6,2},{8,12},{10,14},{12,8},{14,10},{1,5},{3,7},... | collective-permute-start | bytes 2801672 | tf_op jit(solution)/shard_map/ppermute | solution.py:544
  12.9 0.0 collective-permute-done.7.refs_3_.refs_4_
  12.9 1.5 %collective-permute-start = (bf16[128,3584]{1,0:T(8,128)(2,1)S(1)}, bf16[128,3584]{1,0:T(8,128)(2,1)S(1)}, u32[]{:S(2)}, u32[]{:S(2)}) collective-permute-start(bf16[128,3584]{1,0:T(8,128)(2,1)S(1)} %bitcast.16), channel_id=1, source_target_pairs={{0,16},{16,0},{1,17},{17,1},{2,18},{18,2},{3,19},{19,3},{4,20},{20... | collective-permute-start | bytes 2752520 | tf_op jit(solution)/shard_map/ppermute | solution.py:544
  14.4 0.0 collective-permute-done.8.refs_9_.refs_10_
  14.4 0.0 copy-done.3
  14.4 0.5 collective-permute-start.9
  14.9 1.5 %dispatch.3 = (bf16[64,6144]{1,0:T(8,128)(2,1)S(1)}, bf16[64,1152]{1,0:T(8,128)(2,1)S(1)}) custom-call(s32[2,128]{1,0:T(2,128)S(1)} %bitcast.28, f32[2,128]{1,0:T(2,128)S(1)} %bitcast.31, bf16[128,3584]{1,0:T(8,128)(2,1)S(1)} %bitcast.13, bf16[128,3584]{1,0:T(8,128)(2,1)S(1)} %bitcast.17), custom_call_target="tpu_custom_call" | custom-call | flops 146800640 | bytes 2768896 | tf_op jit(solution)/shard_map/dispatch/pallas_call | solution.py:150
  16.4 18.0 %collective-permute-done.start_ref = bf16[128,3584]{1,0:T(8,128)(2,1)S(1)} collective-permute-done((bf16[128,3584]{1,0:T(8,128)(2,1)S(1)}, bf16[128,3584]{1,0:T(8,128)(2,1)S(1)}, u32[]{:S(2)}, u32[]{:S(2)}) %collective-permute-start) | collective-permute-done | bytes 917536 | tf_op jit(solution)/shard_map/ppermute | solution.py:544
  34.4 10.2 %collective-permute-done.1.refs_4_.refs_2_.refs_5_ = bf16[1792,512]{1,0:T(8,128)(2,1)S(1)} collective-permute-done((bf16[1792,512]{1,0:T(8,128)(2,1)}, bf16[1792,512]{1,0:T(8,128)(2,1)S(1)}, u32[]{:S(2)}, u32[]{:S(2)}) %collective-permute-start.1) | collective-permute-done | bytes 1835040 | tf_op jit(solution)/shard_map/ppermute | solution.py:544
  44.6 4.1 %collective-permute-start.10 = (bf16[64,6144]{1,0:T(8,128)(2,1)S(1)}, bf16[64,6144]{1,0:T(8,128)(2,1)S(1)}, u32[]{:S(2)}, u32[]{:S(2)}) collective-permute-start(bf16[64,6144]{1,0:T(8,128)(2,1)S(1)} %get-tuple-element.44), channel_id=1, source_target_pairs={{0,12},{2,14},{4,8},{6,10},{8,4},{10,6},{12,0},{14,2},{1,13},{3,15... | collective-permute-start | bytes 2359304 | tf_op jit(solution)/shard_map/ppermute | solution.py:544
  48.7 19.3 %collective-permute-done.2.refs_1_ = bf16[64,7296]{1,0:T(8,128)(2,1)S(1)} collective-permute-done((bf16[64,7296]{1,0:T(8,128)(2,1)}, bf16[64,7296]{1,0:T(8,128)(2,1)S(1)}, u32[]{:S(2)}, u32[]{:S(2)}) %collective-permute-start.2) | collective-permute-done | bytes 933920 | tf_op jit(solution)/shard_map/ppermute | solution.py:544
  68.0 1.2 collective-permute-done.3.refs_0_
  69.2 0.0 copy-start.2
  69.2 0.1 fusion
  69.3 0.1 collective-permute-start.5
  69.4 0.5 collective-permute-start.4
  69.9 0.1 collective-permute-start.6
  70.1 3.1 %collective-permute-done.6.refs_7_.refs_5_.refs_8_ = bf16[512,512]{1,0:T(8,128)(2,1)S(1)} collective-permute-done((bf16[512,512]{1,0:T(8,128)(2,1)S(1)}, bf16[512,512]{1,0:T(8,128)(2,1)S(1)}, u32[]{:S(2)}, u32[]{:S(2)}) %collective-permute-start.6) | collective-permute-done | bytes 524320 | tf_op jit(solution)/shard_map/ppermute | solution.py:544
  73.2 0.0 collective-permute-done.5.refs_6_.refs_4_.refs_7_
  73.2 0.0 collective-permute-done.4.refs_5_.refs_3_.refs_6_
  73.2 0.0 copy-done.2
  73.2 5.6 %expert_early.1 = (f32[144,512]{1,0:T(8,128)S(1)}, f32[144,3584]{1,0:T(8,128)S(1)}) custom-call(bf16[64,7296]{1,0:T(8,128)(2,1)S(1)} %collective-permute-done.3.refs_0_, bf16[64,7296]{1,0:T(8,128)(2,1)S(1)} %collective-permute-done.2.refs_1_, bf16[1792,512]{1,0:T(8,128)(2,1)S(1)} %bitcast.20, bf16[1792,512]{1,0:T(8,128)(2,1)} %collective-permute-done.7.refs_3_.refs_4_, ...), custom_call_target="tpu_custom_call" | custom-call | tf_op jit(solution)/shard_map/expert_early/pallas_call | solution.py:437
  78.7 0.0 collective-permute-done.10.refs_1_
  78.7 4.6 %collective-permute-done.9.refs_6_.refs_11_ = bf16[1792,512]{1,0:T(8,128)(2,1)S(1)} collective-permute-done((bf16[1792,512]{1,0:T(8,128)(2,1)S(1)}, bf16[1792,512]{1,0:T(8,128)(2,1)S(1)}, u32[]{:S(2)}, u32[]{:S(2)}) %collective-permute-start.9) | collective-permute-done | bytes 1835040 | tf_op jit(solution)/shard_map/ppermute | solution.py:544
  83.4 0.0 collective-permute-start.11
  83.4 3.8 %collective-permute-start.14 = (bf16[64,1152]{1,0:T(8,128)(2,1)S(1)}, bf16[64,1152]{1,0:T(8,128)(2,1)S(1)}, u32[]{:S(2)}, u32[]{:S(2)}) collective-permute-start(bf16[64,1152]{1,0:T(8,128)(2,1)S(1)} %get-tuple-element.60), channel_id=1, source_target_pairs={{0,12},{2,14},{4,8},{6,10},{8,4},{10,6},{12,0},{14,2},{1,13},{3,15... | collective-permute-start | bytes 442376 | tf_op jit(solution)/shard_map/ppermute | solution.py:544
  87.2 0.0 collective-permute-done.11.refs_7_.refs_12_
  87.2 2.3 %expert_late.1 = (bf16[32,7296]{1,0:T(8,128)(2,1)S(1)}, bf16[32,7296]{1,0:T(8,128)(2,1)S(1)}) custom-call(bf16[64,7296]{1,0:T(8,128)(2,1)S(1)} %collective-permute-done.3.refs_0_, bf16[64,7296]{1,0:T(8,128)(2,1)S(1)} %collective-permute-done.2.refs_1_, bf16[1792,512]{1,0:T(8,128)(2,1)S(1)} %collective-permute-done.1.refs_4_.refs_2_.refs_5_, ...), custom_call_target="tpu_custom_call" | custom-call | flops 1056964608 | bytes 11468800 | tf_op jit(solution)/shard_map/expert_late/pallas_call | solution.py:391
  89.5 2.7 %collective-permute-start.12 = (bf16[32,7296]{1,0:T(8,128)(2,1)S(1)}, bf16[32,7296]{1,0:T(8,128)(2,1)S(1)}, u32[]{:S(2)}, u32[]{:S(2)}) collective-permute-start(bf16[32,7296]{1,0:T(8,128)(2,1)S(1)} %get-tuple-element.56), channel_id=1, source_target_pairs={{0,20},{2,22},{4,16},{6,18},{8,28},{10,30},{12,24},{14,26},{16,4},... | collective-permute-start | bytes 1400840 | tf_op jit(solution)/shard_map/ppermute | solution.py:552
  92.2 2.6 %collective-permute-start.13 = (bf16[32,7296]{1,0:T(8,128)(2,1)S(1)}, bf16[32,7296]{1,0:T(8,128)(2,1)S(1)}, u32[]{:S(2)}, u32[]{:S(2)}) collective-permute-start(bf16[32,7296]{1,0:T(8,128)(2,1)S(1)} %get-tuple-element.57), channel_id=1, source_target_pairs={{0,24},{2,26},{4,28},{6,30},{8,16},{10,18},{12,20},{14,22},{16,8},... | collective-permute-start | bytes 1400840 | tf_op jit(solution)/shard_map/ppermute | solution.py:552
  94.8 0.0 collective-permute-done.14.refs_2_
  94.8 7.6 %expert_whole.1 = (bf16[32,7296]{1,0:T(8,128)(2,1)S(1)}, bf16[32,7296]{1,0:T(8,128)(2,1)S(1)}) custom-call(bf16[64,7296]{1,0:T(8,128)(2,1)S(1)} %get-tuple-element.58.refs_0_, bf16[64,6144]{1,0:T(8,128)(2,1)S(1)} %collective-permute-done.10.refs_1_, bf16[64,1152]{1,0:T(8,128)(2,1)S(1)} %collective-permute-done.14.refs_2_, bf16[1792,512]{1,0:T(8,128)(2,1)S(1)} %bitcast.21, ...), custom_call_target="tpu_custom_call" | custom-call | flops 3170893824 | bytes 17776640 | tf_op jit(solution)/shard_map/expert_whole/pallas_call | solution.py:437
  102.4 1.6 %collective-permute-start.15 = (bf16[32,7296]{1,0:T(8,128)(2,1)S(1)}, bf16[32,7296]{1,0:T(8,128)(2,1)S(1)}, u32[]{:S(2)}, u32[]{:S(2)}) collective-permute-start(bf16[32,7296]{1,0:T(8,128)(2,1)S(1)} %get-tuple-element.61), channel_id=1, source_target_pairs={{0,16},{2,18},{4,20},{6,22},{8,24},{10,26},{12,28},{14,30},{16,0},... | collective-permute-start | bytes 1400840 | tf_op jit(solution)/shard_map/ppermute | solution.py:552
  103.9 0.5 collective-permute-start.16
  104.4 8.0 %collective-permute-done.12.refs_0_ = bf16[32,7296]{1,0:T(8,128)(2,1)S(1)} collective-permute-done((bf16[32,7296]{1,0:T(8,128)(2,1)S(1)}, bf16[32,7296]{1,0:T(8,128)(2,1)S(1)}, u32[]{:S(2)}, u32[]{:S(2)}) %collective-permute-start.12) | collective-permute-done | bytes 466976 | tf_op jit(solution)/shard_map/ppermute | solution.py:552
  112.4 14.9 %collective-permute-done.13.refs_1_ = bf16[32,7296]{1,0:T(8,128)(2,1)S(1)} collective-permute-done((bf16[32,7296]{1,0:T(8,128)(2,1)S(1)}, bf16[32,7296]{1,0:T(8,128)(2,1)S(1)}, u32[]{:S(2)}, u32[]{:S(2)}) %collective-permute-start.13) | collective-permute-done | bytes 466976 | tf_op jit(solution)/shard_map/ppermute | solution.py:552
  127.3 1.6 %settle.1.start_ref = f32[128,3584]{1,0:T(8,128)S(1)} custom-call(bf16[128,3584]{1,0:T(8,128)(2,1)S(1)} %collective-permute-done.start_ref, bf16[32,7296]{1,0:T(8,128)(2,1)S(1)} %collective-permute-done.12.refs_0_, bf16[32,7296]{1,0:T(8,128)(2,1)S(1)} %collective-permute-done.13.refs_1_), custom_call_target="tpu_custom_call" | custom-call | flops 132120576 | bytes 3784704 | tf_op jit(solution)/shard_map/settle/pallas_call | solution.py:518
  128.9 4.3 %collective-permute-done.15.refs_0_ = bf16[32,7296]{1,0:T(8,128)(2,1)S(1)} collective-permute-done((bf16[32,7296]{1,0:T(8,128)(2,1)S(1)}, bf16[32,7296]{1,0:T(8,128)(2,1)S(1)}, u32[]{:S(2)}, u32[]{:S(2)}) %collective-permute-start.15) | collective-permute-done | bytes 466976 | tf_op jit(solution)/shard_map/ppermute | solution.py:552
  133.2 0.0 collective-permute-done.16.refs_1_
  133.3 1.7 %finish.1 = bf16[128,3584]{1,0:T(8,128)(2,1)} custom-call(f32[128,3584]{1,0:T(8,128)S(1)} %settle.1.start_ref, bf16[32,7296]{1,0:T(8,128)(2,1)S(1)} %collective-permute-done.15.refs_0_, bf16[32,7296]{1,0:T(8,128)(2,1)S(1)} %collective-permute-done.16.refs_1_), custom_call_target="tpu_custom_call" | custom-call | flops 132120576 | bytes 3784704 | tf_op jit(solution)/shard_map/finish/pallas_call | solution.py:518
  (1 shorter events, 0.0 us)
Async XLA Ops:
  0.0 9.0 %copy-start.5 = (f32[1,128,2]{1,2,0:T(2,128)S(1)}, f32[1,128,2]{1,2,0:T(2,128)}, u32[]{:S(2)}) copy-start(f32[1,128,2]{1,2,0:T(2,128)} %param.9) | copy-start | bytes 3076
  0.0 9.0 %copy-start.4 = (s32[1,128,2]{1,2,0:T(2,128)S(1)}, s32[1,128,2]{1,2,0:T(2,128)}, u32[]{:S(2)}) copy-start(s32[1,128,2]{1,2,0:T(2,128)} %param.8) | copy-start | bytes 3076
  0.0 9.0 %copy-start.1 = (bf16[1,128,3584]{2,1,0:T(8,128)(2,1)S(1)}, bf16[1,128,3584]{2,1,0:T(8,128)(2,1)}, u32[]{:S(2)}) copy-start(bf16[1,128,3584]{2,1,0:T(8,128)(2,1)} %param.7) | copy-start | bytes 2752516
  0.0 9.0 %copy-start = (bf16[1,128,3584]{2,1,0:T(8,128)(2,1)S(1)}, bf16[1,128,3584]{2,1,0:T(8,128)(2,1)}, u32[]{:S(2)}) copy-start(bf16[1,128,3584]{2,1,0:T(8,128)(2,1)} %param.6) | copy-start | bytes 2752516
  0.0 12.9 %collective-permute-start.7 = (bf16[1792,512]{1,0:T(8,128)(2,1)}, bf16[1792,512]{1,0:T(8,128)(2,1)}, u32[]{:S(2)}, u32[]{:S(2)}) collective-permute-start(bf16[1792,512]{1,0:T(8,128)(2,1)} %bitcast.18), channel_id=1, source_target_pairs={{0,2},{2,0},{4,6},{6,4},{8,10},{10,8},{12,14},{14,12},{1,3},{3,1},... | collective-permute-start | bytes 5505032 | tf_op jit(solution)/shard_map/ppermute | solution.py:544
  0.5 13.9 %collective-permute-start.8 = (bf16[1792,512]{1,0:T(8,128)(2,1)}, bf16[1792,512]{1,0:T(8,128)(2,1)}, u32[]{:S(2)}, u32[]{:S(2)}) collective-permute-start(bf16[1792,512]{1,0:T(8,128)(2,1)} %bitcast.22), channel_id=1, source_target_pairs={{0,2},{2,0},{4,6},{6,4},{8,10},{10,8},{12,14},{14,12},{1,3},{3,1},... | collective-permute-start | bytes 5505032 | tf_op jit(solution)/shard_map/ppermute | solution.py:544
  0.6 44.0 %collective-permute-start.1 = (bf16[1792,512]{1,0:T(8,128)(2,1)}, bf16[1792,512]{1,0:T(8,128)(2,1)S(1)}, u32[]{:S(2)}, u32[]{:S(2)}) collective-permute-start(bf16[1792,512]{1,0:T(8,128)(2,1)} %bitcast.19), channel_id=1, source_target_pairs={{0,1},{1,0},{2,3},{3,2},{4,5},{5,4},{6,7},{7,6},{8,9},{9,8},{10,11... | collective-permute-start | bytes 5505032 | tf_op jit(solution)/shard_map/ppermute | solution.py:544
  3.6 10.9 %copy-start.3 = (bf16[1,1,1792,512]{3,2,1,0:T(8,128)(2,1)S(1)}, bf16[1,1,1792,512]{3,2,1,0:T(8,128)(2,1)}, u32[]{:S(2)}) copy-start(bf16[1,1,1792,512]{3,2,1,0:T(8,128)(2,1)} %param.11) | copy-start | bytes 5505028
  6.4 61.7 %collective-permute-start.2 = (bf16[64,7296]{1,0:T(8,128)(2,1)}, bf16[64,7296]{1,0:T(8,128)(2,1)S(1)}, u32[]{:S(2)}, u32[]{:S(2)}) collective-permute-start(bf16[64,7296]{1,0:T(8,128)(2,1)} %dispatch.4), channel_id=1, source_target_pairs={{0,8},{2,10},{4,12},{6,14},{8,0},{10,2},{12,4},{14,6},{1,9},{3,11}... | collective-permute-start | bytes 2801672 | tf_op jit(solution)/shard_map/ppermute | solution.py:544
  11.3 57.9 %collective-permute-start.3 = (bf16[64,7296]{1,0:T(8,128)(2,1)S(1)}, bf16[64,7296]{1,0:T(8,128)(2,1)S(1)}, u32[]{:S(2)}, u32[]{:S(2)}) collective-permute-start(bf16[64,7296]{1,0:T(8,128)(2,1)S(1)} %get-tuple-element.38), channel_id=1, source_target_pairs={{0,4},{2,6},{4,0},{6,2},{8,12},{10,14},{12,8},{14,10},{1,5},{3,7},... | collective-permute-start | bytes 2801672 | tf_op jit(solution)/shard_map/ppermute | solution.py:544
  12.9 21.5 %collective-permute-start = (bf16[128,3584]{1,0:T(8,128)(2,1)S(1)}, bf16[128,3584]{1,0:T(8,128)(2,1)S(1)}, u32[]{:S(2)}, u32[]{:S(2)}) collective-permute-start(bf16[128,3584]{1,0:T(8,128)(2,1)S(1)} %bitcast.16), channel_id=1, source_target_pairs={{0,16},{16,0},{1,17},{17,1},{2,18},{18,2},{3,19},{19,3},{4,20},{20... | collective-permute-start | bytes 2752520 | tf_op jit(solution)/shard_map/ppermute | solution.py:544
  14.4 68.9 %collective-permute-start.9 = (bf16[1792,512]{1,0:T(8,128)(2,1)S(1)}, bf16[1792,512]{1,0:T(8,128)(2,1)S(1)}, u32[]{:S(2)}, u32[]{:S(2)}) collective-permute-start(bf16[1792,512]{1,0:T(8,128)(2,1)S(1)} %bitcast.23), channel_id=1, source_target_pairs={{0,1},{1,0},{2,3},{3,2},{4,5},{5,4},{6,7},{7,6},{8,9},{9,8},{10,11... | collective-permute-start | bytes 5505032 | tf_op jit(solution)/shard_map/ppermute | solution.py:544
  44.6 34.2 %collective-permute-start.10 = (bf16[64,6144]{1,0:T(8,128)(2,1)S(1)}, bf16[64,6144]{1,0:T(8,128)(2,1)S(1)}, u32[]{:S(2)}, u32[]{:S(2)}) collective-permute-start(bf16[64,6144]{1,0:T(8,128)(2,1)S(1)} %get-tuple-element.44), channel_id=1, source_target_pairs={{0,12},{2,14},{4,8},{6,10},{8,4},{10,6},{12,0},{14,2},{1,13},{3,15... | collective-permute-start | bytes 2359304 | tf_op jit(solution)/shard_map/ppermute | solution.py:544
  69.2 4.0 %copy-start.2 = (bf16[1,1,1792,512]{3,2,1,0:T(8,128)(2,1)S(1)}, bf16[1,1,1792,512]{3,2,1,0:T(8,128)(2,1)}, u32[]{:S(2)}) copy-start(bf16[1,1,1792,512]{3,2,1,0:T(8,128)(2,1)} %param.10) | copy-start | bytes 5505028
  69.3 3.9 %collective-permute-start.5 = (bf16[640,512]{1,0:T(8,128)(2,1)S(1)}, bf16[640,512]{1,0:T(8,128)(2,1)S(1)}, u32[]{:S(2)}, u32[]{:S(2)}) collective-permute-start(bf16[640,512]{1,0:T(8,128)(2,1)S(1)} %get-tuple-element.63), channel_id=1, source_target_pairs={{0,2},{2,0},{4,6},{6,4},{8,10},{10,8},{12,14},{14,12},{1,3},{3,1},... | collective-permute-start | bytes 1966088 | tf_op jit(solution)/shard_map/ppermute | solution.py:544
  69.4 3.8 %collective-permute-start.4 = (bf16[640,512]{1,0:T(8,128)(2,1)S(1)}, bf16[640,512]{1,0:T(8,128)(2,1)S(1)}, u32[]{:S(2)}, u32[]{:S(2)}) collective-permute-start(bf16[640,512]{1,0:T(8,128)(2,1)S(1)} %get-tuple-element.64), channel_id=1, source_target_pairs={{0,2},{2,0},{4,6},{6,4},{8,10},{10,8},{12,14},{14,12},{1,3},{3,1},... | collective-permute-start | bytes 1966088 | tf_op jit(solution)/shard_map/ppermute | solution.py:544
  69.9 3.2 %collective-permute-start.6 = (bf16[512,512]{1,0:T(8,128)(2,1)S(1)}, bf16[512,512]{1,0:T(8,128)(2,1)S(1)}, u32[]{:S(2)}, u32[]{:S(2)}) collective-permute-start(bf16[512,512]{1,0:T(8,128)(2,1)S(1)} %slice.11), channel_id=1, source_target_pairs={{0,2},{2,0},{4,6},{6,4},{8,10},{10,8},{12,14},{14,12},{1,3},{3,1},... | collective-permute-start | bytes 1572872 | tf_op jit(solution)/shard_map/ppermute | solution.py:544
  83.4 3.8 %collective-permute-start.11 = (bf16[1792,512]{1,0:T(8,128)(2,1)S(1)}, bf16[1792,512]{1,0:T(8,128)(2,1)S(1)}, u32[]{:S(2)}, u32[]{:S(2)}) collective-permute-start(bf16[1792,512]{1,0:T(8,128)(2,1)S(1)} %collective-permute-done.9.refs_6_.refs_11_), channel_id=1, source_target_pairs={{0,2},{2,0},{4,6},{6,4},{8,10},{10,8},{12,14},{14,12},{1,3},{3,1},... | collective-permute-start | bytes 5505032 | tf_op jit(solution)/shard_map/ppermute | solution.py:544
  83.4 11.4 %collective-permute-start.14 = (bf16[64,1152]{1,0:T(8,128)(2,1)S(1)}, bf16[64,1152]{1,0:T(8,128)(2,1)S(1)}, u32[]{:S(2)}, u32[]{:S(2)}) collective-permute-start(bf16[64,1152]{1,0:T(8,128)(2,1)S(1)} %get-tuple-element.60), channel_id=1, source_target_pairs={{0,12},{2,14},{4,8},{6,10},{8,4},{10,6},{12,0},{14,2},{1,13},{3,15... | collective-permute-start | bytes 442376 | tf_op jit(solution)/shard_map/ppermute | solution.py:544
  89.5 22.9 %collective-permute-start.12 = (bf16[32,7296]{1,0:T(8,128)(2,1)S(1)}, bf16[32,7296]{1,0:T(8,128)(2,1)S(1)}, u32[]{:S(2)}, u32[]{:S(2)}) collective-permute-start(bf16[32,7296]{1,0:T(8,128)(2,1)S(1)} %get-tuple-element.56), channel_id=1, source_target_pairs={{0,20},{2,22},{4,16},{6,18},{8,28},{10,30},{12,24},{14,26},{16,4},... | collective-permute-start | bytes 1400840 | tf_op jit(solution)/shard_map/ppermute | solution.py:552
  92.2 35.1 %collective-permute-start.13 = (bf16[32,7296]{1,0:T(8,128)(2,1)S(1)}, bf16[32,7296]{1,0:T(8,128)(2,1)S(1)}, u32[]{:S(2)}, u32[]{:S(2)}) collective-permute-start(bf16[32,7296]{1,0:T(8,128)(2,1)S(1)} %get-tuple-element.57), channel_id=1, source_target_pairs={{0,24},{2,26},{4,28},{6,30},{8,16},{10,18},{12,20},{14,22},{16,8},... | collective-permute-start | bytes 1400840 | tf_op jit(solution)/shard_map/ppermute | solution.py:552
  102.4 30.9 %collective-permute-start.15 = (bf16[32,7296]{1,0:T(8,128)(2,1)S(1)}, bf16[32,7296]{1,0:T(8,128)(2,1)S(1)}, u32[]{:S(2)}, u32[]{:S(2)}) collective-permute-start(bf16[32,7296]{1,0:T(8,128)(2,1)S(1)} %get-tuple-element.61), channel_id=1, source_target_pairs={{0,16},{2,18},{4,20},{6,22},{8,24},{10,26},{12,28},{14,30},{16,0},... | collective-permute-start | bytes 1400840 | tf_op jit(solution)/shard_map/ppermute | solution.py:552
  103.9 29.3 %collective-permute-start.16 = (bf16[32,7296]{1,0:T(8,128)(2,1)S(1)}, bf16[32,7296]{1,0:T(8,128)(2,1)S(1)}, u32[]{:S(2)}, u32[]{:S(2)}) collective-permute-start(bf16[32,7296]{1,0:T(8,128)(2,1)S(1)} %get-tuple-element.62), channel_id=1, source_target_pairs={{0,28},{2,30},{4,24},{6,26},{8,20},{10,22},{12,16},{14,18},{16,12}... | collective-permute-start | bytes 1400840 | tf_op jit(solution)/shard_map/ppermute | solution.py:552

commit v7 on v6

--- a/solution.py
+++ b/solution.py
@@ -240,36 +240,30 @@
         refs = refs[length:]
     w_pieces, refs = refs[: len(w_layout)], refs[len(w_layout) :]
     v_pieces, refs = refs[: len(v_layout)], refs[len(v_layout) :]
-    if stage == "late":
-        slope, partial, refs = refs[0], refs[1], refs[2:]
+    if stage == "early":
+        slope_late, partial_out, refs = refs[0], refs[1], refs[2:]
+    else:
         outs, refs = refs[:n], refs[n:]
-    elif stage == "early":
-        slope_late, partial_out, slope, refs = refs[0], refs[1], refs[2], refs[3:]
-    else:
-        outs, slope, refs = refs[:n], refs[n], refs[n + 1 :]
-    w, v, x, g, act, ext, row32, ext32, sem_x, sem_g, sem_e, sem_w, sem_v = refs
+    g, ext32, slope, w, v, x, act, ext, row32, sem_x, sem_g, sem_e, sem_w, sem_v = refs
     width = w.shape[0]
     half_ff = w_layout[0][3]
     pieces = width // LANES
     full = n * base
-    x_in = []
-    if stage != "late":
-        x_in = begin_rows(msgs, x, ext, 0, sem_x, sem_e)
+    x_in = begin_rows(msgs, x, ext, 0, sem_x, sem_e)
     w_in = begin_weights(w_pieces, w_layout, w, sem_w)
-    g_in = begin_rows(msgs, g, ext if stage == "late" else None, width, sem_g, sem_e)
+    g_in = begin_rows(msgs, g, None, width, sem_g, sem_e)
     v_in = begin_weights(v_pieces, v_layout, v, sem_v)
-    if stage != "late":
-        finish(x_in)
-        if extra:
-            put_extra(x, row32, ext, n, base, 0)
-        for block in sorted(w_in):
-            finish(w_in[block])
-            for at in range(block * half_ff, (block + 1) * half_ff, TILE):
-                value = silu_slope(jnp.dot(x[...], w[:, at : at + TILE], preferred_element_type=F32))
-                if stage == "early" and block > 0:
-                    slope_late[:, at - half_ff : at - half_ff + TILE] = value
-                else:
-                    slope[:, at : at + TILE] = value
+    finish(x_in)
+    if extra:
+        put_extra(x, row32, ext, n, base, 0)
+    for block in sorted(w_in):
+        finish(w_in[block])
+        for at in range(block * half_ff, (block + 1) * half_ff, TILE):
+            value = silu_slope(jnp.dot(x[...], w[:, at : at + TILE], preferred_element_type=F32))
+            if stage == "early" and block > 0:
+                slope_late[:, at - half_ff : at - half_ff + TILE] = value
+            else:
+                slope[:, at : at + TILE] = value
     finish(g_in)
     if extra:
         put_extra(g, row32, ext, n, base, pieces)
@@ -278,16 +272,12 @@
         for at in range(block * half_ff, (block + 1) * half_ff, TILE):
             hid = jnp.dot(g[...], v[:, at : at + TILE], preferred_element_type=F32)
             act[:, at : at + TILE] = (hid * slope[:, at : at + TILE]).astype(BF16)
-    if stage == "late":
-        for block in sorted(w_in):
-            finish(w_in[block])
-    if stage != "early":
-        ext32[...] = jnp.zeros_like(ext32)
-        at, column = place_of(2 * pieces * extra, base)
-        to, to_column = place_of(pieces * extra, ext32.shape[1])
-        for i in range(n):
-            holders = ext[i].astype(F32)[at : at + 1, column : column + LANES]
-            ext32[i, to : to + 1, to_column : to_column + LANES] = holders
+    ext32[...] = jnp.zeros_like(ext32)
+    at, column = place_of(2 * pieces * extra, base)
+    to, to_column = place_of(pieces * extra, ext32.shape[1])
+    for i in range(n):
+        holders = ext[i].astype(F32)[at : at + 1, column : column + LANES]
+        ext32[i, to : to + 1, to_column : to_column + LANES] = holders
     hidden = act.shape[1]
     for at in range(0, width, TILE):
         cols = slice(at, at + TILE)
@@ -297,50 +287,71 @@
         if stage == "early":
             partial_out[:, cols] = back
             continue
-        if stage == "late":
-            back = back + partial[:, cols]
         put_back(outs, ext32, back, at, TILE, n, base, extra, width)
     if stage != "early":
         for i in range(n):
             outs[i][:, sides_of(base) * width :] = ext32[i].astype(BF16)
 
 
+def middle_kernel(*refs):
+    g, v_blocks, out = refs[0], refs[1:-1], refs[-1]
+    half, block_ff = v_blocks[0].shape
+
+    def work(here):
+        for block, ref in enumerate(v_blocks):
+            for at in range(0, block_ff, TILE):
+                out[:, block * block_ff + at : block * block_ff + at + TILE] = jnp.dot(
+                    g[:, here * half : (here + 1) * half],
+                    ref[:, at : at + TILE],
+                    preferred_element_type=F32,
+                )
+
+    core = lax.axis_index("expert") % 2
+    for here in range(2):
+        pl.when(core == here)(functools.partial(work, here))
+
+
+def expert_middle(g, v_blocks):
+    rows, (half, block_ff) = g.shape[0], v_blocks[0].shape
+    vmem = pl.BlockSpec(memory_space=pltpu.VMEM)
+    return pl.pallas_call(
+        middle_kernel,
+        out_shape=jax.ShapeDtypeStruct((rows, len(v_blocks) * block_ff), F32),
+        in_specs=[vmem] * (1 + len(v_blocks)),
+        out_specs=vmem,
+        compiler_params=pltpu.CompilerParams(vmem_limit_bytes=24 * MIB),
+        cost_estimate=pl.CostEstimate(
+            flops=2 * rows * half * block_ff * len(v_blocks),
+            bytes_accessed=2 * half * block_ff * len(v_blocks),
+            transcendentals=0,
+        ),
+        name="expert_middle",
+    )(g, *v_blocks)
+
+
 def late_kernel(n, base, extra, blocks, w_layout, v_layout, *refs):
-    msgs, refs = refs[:n], refs[n:]
     w_pieces, refs = refs[: len(w_layout)], refs[len(w_layout) :]
     v_pieces, refs = refs[: len(v_layout)], refs[len(v_layout) :]
-    slope, partial, refs = refs[0], refs[1], refs[2:]
-    outs, (g, act, ext, row32, ext32, sem_g, sem_e) = refs[:n], refs[n:]
+    slope, partial, g, folded, half_hid, refs = refs[0], refs[1], refs[2], refs[3], refs[4], refs[5:]
+    outs, (act, ext32) = refs[:n], refs[n:]
     width = g.shape[1]
     half, block_ff = width // 2, v_layout[0][3]
-    pieces = width // LANES
-    full = n * base
     core = lax.axis_index("expert") % 2
-    copies = begin_rows([(msg,) for msg in msgs], g, ext, width, sem_g, sem_e)
-    finish(copies)
-    if extra:
-        put_extra(g, row32, ext, n, base, pieces)
-    ext32[...] = jnp.zeros_like(ext32)
-    at, column = place_of(2 * pieces * extra, base)
-    to, to_column = place_of(pieces * extra, ext32.shape[1])
-    for i in range(n):
-        holders = ext[i].astype(F32)[at : at + 1, column : column + LANES]
-        ext32[i, to : to + 1, to_column : to_column + LANES] = holders
+    ext32[...] = folded[...]
 
     def work(here):
         for block in range(blocks):
             for at in range(0, block_ff, TILE):
-                hid = None
+                cols = slice(block * block_ff + at, block * block_ff + at + TILE)
+                hid = half_hid[:, cols]
                 for ref, (of, other, row, _) in zip(v_pieces, v_layout):
                     if of == block:
                         first = (1 - here if other else here) * half + row
-                        term = jnp.dot(
+                        hid = hid + jnp.dot(
                             g[:, first : first + ref.shape[0]],
                             ref[:, at : at + TILE],
                             preferred_element_type=F32,
                         )
-                        hid = term if hid is None else hid + term
-                cols = slice(block * block_ff + at, block * block_ff + at + TILE)
                 act[:, cols] = (hid * slope[:, cols]).astype(BF16)
         places = {}
         for ref, (of, other, row, _) in zip(w_pieces, w_layout):
@@ -378,30 +389,20 @@
     return arrays, layout, row
 
 
-def expert_late(msgs, base, extra, w_columns, v_columns, carried):
-    n = len(msgs)
-    msgs = [message for (message,) in msgs]
+def expert_late(base, extra, w_columns, v_columns, carried):
     w_pieces, w_layout, half = flat(w_columns)
-    v_pieces, v_layout, _ = flat(v_columns)
+    carried = list(carried) + [expert_middle(carried[2], [own[0] for own, _ in v_columns])]
+    v_pieces, v_layout, _ = flat([[[], other] for _, other in v_columns])
     width, ff = 2 * half, len(w_columns) * w_layout[0][3]
-    rows = n * base + -(-n * extra // 16) * 16
-    ext = fold_columns(2 * width // LANES * extra, base)
-    back_rows, back_cols = back_shape(base, width, extra)
-    anywhere, vmem = pl.BlockSpec(memory_space=pl.ANY), pl.BlockSpec(memory_space=pltpu.VMEM)
+    rows, folded = carried[0].shape[0], carried[3].shape
+    vmem = pl.BlockSpec(memory_space=pltpu.VMEM)
+    back = jax.ShapeDtypeStruct(back_shape(base, width, extra), BF16)
     return pl.pallas_call(
-        functools.partial(late_kernel, n, base, extra, len(w_columns), w_layout, v_layout),
-        out_shape=[jax.ShapeDtypeStruct((back_rows, back_cols), BF16) for _ in msgs],
-        in_specs=[anywhere] * n + [vmem] * (len(w_pieces) + len(v_pieces) + len(carried)),
-        out_specs=[vmem] * n,
-        scratch_shapes=[
-            pltpu.VMEM((rows, width), BF16),
-            pltpu.VMEM((rows, ff), BF16),
-            pltpu.VMEM((n, base, ext), BF16),
-            pltpu.VMEM((max(16, rows - n * base), width), F32),
-            pltpu.VMEM((n, back_rows, back_cols - sides_of(base) * width), F32),
-            pltpu.SemaphoreType.DMA((n, 1)),
-            pltpu.SemaphoreType.DMA((n, 1)),
-        ],
+        functools.partial(late_kernel, folded[0], base, extra, len(w_columns), w_layout, v_layout),
+        out_shape=[back] * folded[0],
+        in_specs=[vmem] * (len(w_pieces) + len(v_pieces) + len(carried)),
+        out_specs=[vmem] * folded[0],
+        scratch_shapes=[pltpu.VMEM((rows, ff), BF16), pltpu.VMEM(folded, F32)],
         compiler_params=pltpu.CompilerParams(vmem_limit_bytes=24 * MIB),
         cost_estimate=pl.CostEstimate(
             flops=4 * rows * width * ff,
@@ -409,12 +410,11 @@
             transcendentals=0,
         ),
         name="expert_late",
-    )(*msgs, *w_pieces, *v_pieces, *carried)
-
-
-def expert(msgs, base, extra, w_columns, v_columns, stage="whole", carried=()):
+    )(*w_pieces, *v_pieces, *carried)
+
+
+def expert(msgs, base, extra, w_columns, v_columns, stage="whole"):
     n = len(msgs)
-
     lengths = [len(parts) for parts in msgs]
     most, parts = max(lengths), [part for message in msgs for part in message]
     w_pieces, w_layout, half = flat(w_columns)
@@ -426,29 +426,25 @@
     back_rows, back_cols = back_shape(base, width, extra)
     anywhere, vmem = pl.BlockSpec(memory_space=pl.ANY), pl.BlockSpec(memory_space=pltpu.VMEM)
     spare = max(16, rows - n * base)
-    own_slope = [] if stage == "late" else [pltpu.VMEM((rows, v_ff), F32)]
+    kept = [((rows, width), BF16), ((n, back_rows, back_cols - sides_of(base) * width), F32)]
     if stage == "early":
-        out_shape = [
-            jax.ShapeDtypeStruct((rows, w_ff - block_ff), F32),
-            jax.ShapeDtypeStruct((rows, width), F32),
-        ]
+        results = [((rows, w_ff - block_ff), F32), ((rows, width), F32)] + kept
     else:
-        out_shape = [jax.ShapeDtypeStruct((back_rows, back_cols), BF16) for _ in msgs]
+        results = [((back_rows, back_cols), BF16)] * n
     return pl.pallas_call(
         functools.partial(expert_kernel, n, base, extra, stage, w_layout, v_layout, lengths),
-        out_shape=out_shape,
-        in_specs=[anywhere] * (len(parts) + len(w_pieces) + len(v_pieces)) + [vmem] * len(carried),
-        out_specs=[vmem] * len(out_shape),
-        scratch_shapes=own_slope
+        out_shape=[jax.ShapeDtypeStruct(*result) for result in results],
+        in_specs=[anywhere] * (len(parts) + len(w_pieces) + len(v_pieces)),
+        out_specs=[vmem] * len(results),
+        scratch_shapes=[pltpu.VMEM(*shape) for shape in (kept if stage != "early" else [])]
         + [
+            pltpu.VMEM((rows, v_ff), F32),
             pltpu.VMEM((width, w_ff), BF16),
             pltpu.VMEM((width, v_ff), BF16),
-            pltpu.VMEM((rows, width), BF16),
             pltpu.VMEM((rows, width), BF16),
             pltpu.VMEM((rows, v_ff), BF16),
             pltpu.VMEM((n, base, ext), BF16),
             pltpu.VMEM((spare, width), F32),
-            pltpu.VMEM((n, back_rows, back_cols - sides_of(base) * width), F32),
             pltpu.SemaphoreType.DMA((n, most)),
             pltpu.SemaphoreType.DMA((n, most)),
             pltpu.SemaphoreType.DMA((n, most)),
@@ -462,7 +458,7 @@
             transcendentals=0 if stage == "early" else rows * w_ff,
         ),
         name="expert_" + stage,
-    )(*parts, *w_pieces, *v_pieces, *carried)
+    )(*parts, *w_pieces, *v_pieces)
 
 
 def add_kernel(n, base, extra, start_ref, *refs):
@@ -608,7 +604,7 @@
     for i, group in enumerate(works):
         msgs = [got[dist] for dist in group]
         if i == 0:
-            backs = expert_late(msgs, base, extra, w_columns[1:], v_columns[1:], carried)
+            backs = expert_late(base, extra, w_columns[1:], v_columns[1:], carried)
             backs, heads = after(backs, {dist: parts[:1] for dist, parts in got.items()})
             got = {dist: heads[dist] + parts[1:] for dist, parts in got.items()}
         else:

time: 136 us -> 136 us (level)
  no operation moved by 1% of the time
where the time goes in v7:
time: 136 us; the launch traced here: 135 us
  waiting for transfers between devices  83.6 us (61%)
  starting transfers between devices  25.9 us (19%)
  Pallas kernels  25.2 us (19%)
    ppermute x13, waiting for transfers between devices, swap(): lax.ppermute(value, axis, [(i, i ^ apart) for i in range(lax.axis_size(ax...  56.3 us
    ppermute x4, waiting for transfers between devices, swap_back(): return lax.ppermute(value, ('section', 'expert'), pairs)  27.3 us
    ppermute x13, starting transfers between devices, swap(): lax.ppermute(value, axis, [(i, i ^ apart) for i in range(lax.axis_size(ax...  18.5 us
    pallas_call x2, Pallas kernels, expert(): pl.pallas_call(functools.partial(expert_kernel, n, base, extra, stage, w_...  13.1 us
    ppermute x4, starting transfers between devices, swap_back(): return lax.ppermute(value, ('section', 'expert'), pairs)  7.35 us
    pallas_call x3, Pallas kernels, dispatch(): pl.pallas_call(functools.partial(dispatch_kernel, dists, base, extra, spl...  6.52 us
    pallas_call x2, Pallas kernels, add_returned(): pl.pallas_call(functools.partial(add_kernel, n, base, extra), out_shape=j...  3.25 us
  transfers between devices with their start and end apart: 17, of which 9 were waited for; matrix products, arithmetic and copies ran while one was open for 0% of the time, Pallas kernels for 17%

profile of v7, /device:TPU:0, one launch (start us, length us, event | category | flops | bytes accessed | tf_op | source)
XLA Modules:
  0.0 135.1 jit_solution(1177062284235264732)
XLA Ops:
  0.0 0.0 copy-start.5
  0.0 0.0 copy-start.4
  0.0 0.0 copy-start.1
  0.0 0.0 copy-start
  0.0 0.5 collective-permute-start.7
  0.5 0.1 collective-permute-start.8
  0.6 2.9 %collective-permute-start.1 = (bf16[1792,512]{1,0:T(8,128)(2,1)}, bf16[1792,512]{1,0:T(8,128)(2,1)S(1)}, u32[]{:S(2)}, u32[]{:S(2)}) collective-permute-start(bf16[1792,512]{1,0:T(8,128)(2,1)} %bitcast.19), channel_id=1, source_target_pairs={{0,1},{1,0},{2,3},{3,2},{4,5},{5,4},{6,7},{7,6},{8,9},{9,8},{10,11... | collective-permute-start | bytes 5505032 | tf_op jit(solution)/shard_map/ppermute | solution.py:540
  3.6 0.0 copy-start.3
  3.6 2.8 %dispatch.4 = bf16[64,7296]{1,0:T(8,128)(2,1)} custom-call(s32[2,128]{1,0:T(2,128)} %bitcast.26, f32[2,128]{1,0:T(2,128)} %bitcast.29, bf16[128,3584]{1,0:T(8,128)(2,1)} %bitcast.11, bf16[128,3584]{1,0:T(8,128)(2,1)} %bitcast.14), custom_call_target="tpu_custom_call" | custom-call | flops 146800640 | bytes 2768896 | tf_op jit(solution)/shard_map/dispatch/pallas_call | solution.py:150
  6.4 2.7 %collective-permute-start.2 = (bf16[64,7296]{1,0:T(8,128)(2,1)}, bf16[64,7296]{1,0:T(8,128)(2,1)S(1)}, u32[]{:S(2)}, u32[]{:S(2)}) collective-permute-start(bf16[64,7296]{1,0:T(8,128)(2,1)} %dispatch.4), channel_id=1, source_target_pairs={{0,8},{2,10},{4,12},{6,14},{8,0},{10,2},{12,4},{14,6},{1,9},{3,11}... | collective-permute-start | bytes 2801672 | tf_op jit(solution)/shard_map/ppermute | solution.py:540
  9.0 0.0 copy-done.5
  9.0 0.0 copy-done.4
  9.0 0.0 copy-done.1
  9.0 0.0 copy-done
  9.0 2.2 %dispatch.5 = (bf16[64,7296]{1,0:T(8,128)(2,1)S(1)}, bf16[64,7296]{1,0:T(8,128)(2,1)S(1)}) custom-call(s32[2,128]{1,0:T(2,128)S(1)} %bitcast.27, f32[2,128]{1,0:T(2,128)S(1)} %bitcast.30, bf16[128,3584]{1,0:T(8,128)(2,1)S(1)} %bitcast.12, bf16[128,3584]{1,0:T(8,128)(2,1)S(1)} %bitcast.15), custom_call_target="tpu_custom_call" | custom-call | flops 293601280 | bytes 3702784 | tf_op jit(solution)/shard_map/dispatch/pallas_call | solution.py:150
  11.3 1.7 %collective-permute-start.3 = (bf16[64,7296]{1,0:T(8,128)(2,1)S(1)}, bf16[64,7296]{1,0:T(8,128)(2,1)S(1)}, u32[]{:S(2)}, u32[]{:S(2)}) collective-permute-start(bf16[64,7296]{1,0:T(8,128)(2,1)S(1)} %get-tuple-element.42), channel_id=1, source_target_pairs={{0,4},{2,6},{4,0},{6,2},{8,12},{10,14},{12,8},{14,10},{1,5},{3,7},... | collective-permute-start | bytes 2801672 | tf_op jit(solution)/shard_map/ppermute | solution.py:540
  12.9 0.0 collective-permute-done.7.refs_3_.refs_4_
  12.9 1.5 %collective-permute-start = (bf16[128,3584]{1,0:T(8,128)(2,1)S(1)}, bf16[128,3584]{1,0:T(8,128)(2,1)S(1)}, u32[]{:S(2)}, u32[]{:S(2)}) collective-permute-start(bf16[128,3584]{1,0:T(8,128)(2,1)S(1)} %bitcast.16), channel_id=1, source_target_pairs={{0,16},{16,0},{1,17},{17,1},{2,18},{18,2},{3,19},{19,3},{4,20},{20... | collective-permute-start | bytes 2752520 | tf_op jit(solution)/shard_map/ppermute | solution.py:540
  14.4 0.0 collective-permute-done.8.refs_9_.refs_10_
  14.4 0.0 copy-done.3
  14.4 0.5 collective-permute-start.9
  14.9 1.5 %dispatch.3 = (bf16[64,6144]{1,0:T(8,128)(2,1)S(1)}, bf16[64,1152]{1,0:T(8,128)(2,1)S(1)}) custom-call(s32[2,128]{1,0:T(2,128)S(1)} %bitcast.28, f32[2,128]{1,0:T(2,128)S(1)} %bitcast.31, bf16[128,3584]{1,0:T(8,128)(2,1)S(1)} %bitcast.13, bf16[128,3584]{1,0:T(8,128)(2,1)S(1)} %bitcast.17), custom_call_target="tpu_custom_call" | custom-call | flops 146800640 | bytes 2768896 | tf_op jit(solution)/shard_map/dispatch/pallas_call | solution.py:150
  16.4 18.0 %collective-permute-done.start_ref = bf16[128,3584]{1,0:T(8,128)(2,1)S(1)} collective-permute-done((bf16[128,3584]{1,0:T(8,128)(2,1)S(1)}, bf16[128,3584]{1,0:T(8,128)(2,1)S(1)}, u32[]{:S(2)}, u32[]{:S(2)}) %collective-permute-start) | collective-permute-done | bytes 917536 | tf_op jit(solution)/shard_map/ppermute | solution.py:540
  34.4 10.2 %collective-permute-done.1.refs_4_.refs_0_.refs_5_ = bf16[1792,512]{1,0:T(8,128)(2,1)S(1)} collective-permute-done((bf16[1792,512]{1,0:T(8,128)(2,1)}, bf16[1792,512]{1,0:T(8,128)(2,1)S(1)}, u32[]{:S(2)}, u32[]{:S(2)}) %collective-permute-start.1) | collective-permute-done | bytes 1835040 | tf_op jit(solution)/shard_map/ppermute | solution.py:540
  44.6 4.1 %collective-permute-start.10 = (bf16[64,6144]{1,0:T(8,128)(2,1)S(1)}, bf16[64,6144]{1,0:T(8,128)(2,1)S(1)}, u32[]{:S(2)}, u32[]{:S(2)}) collective-permute-start(bf16[64,6144]{1,0:T(8,128)(2,1)S(1)} %get-tuple-element.46), channel_id=1, source_target_pairs={{0,12},{2,14},{4,8},{6,10},{8,4},{10,6},{12,0},{14,2},{1,13},{3,15... | collective-permute-start | bytes 2359304 | tf_op jit(solution)/shard_map/ppermute | solution.py:540
  48.7 19.3 %collective-permute-done.2.refs_1_ = bf16[64,7296]{1,0:T(8,128)(2,1)S(1)} collective-permute-done((bf16[64,7296]{1,0:T(8,128)(2,1)}, bf16[64,7296]{1,0:T(8,128)(2,1)S(1)}, u32[]{:S(2)}, u32[]{:S(2)}) %collective-permute-start.2) | collective-permute-done | bytes 933920 | tf_op jit(solution)/shard_map/ppermute | solution.py:540
  68.0 1.2 collective-permute-done.3.refs_0_
  69.2 0.0 copy-start.2
  69.2 0.1 fusion
  69.3 0.1 collective-permute-start.5
  69.4 0.5 collective-permute-start.4
  69.9 0.1 collective-permute-start.6
  70.1 3.1 %collective-permute-done.6.refs_7_.refs_3_.refs_8_ = bf16[512,512]{1,0:T(8,128)(2,1)S(1)} collective-permute-done((bf16[512,512]{1,0:T(8,128)(2,1)S(1)}, bf16[512,512]{1,0:T(8,128)(2,1)S(1)}, u32[]{:S(2)}, u32[]{:S(2)}) %collective-permute-start.6) | collective-permute-done | bytes 524320 | tf_op jit(solution)/shard_map/ppermute | solution.py:540
  73.2 0.0 collective-permute-done.5.refs_6_.refs_2_.refs_7_
  73.2 0.0 collective-permute-done.4.refs_5_.refs_1_.refs_6_
  73.2 0.0 copy-done.2
  73.2 5.6 %expert_early.1 = (f32[144,512]{1,0:T(8,128)S(1)}, f32[144,3584]{1,0:T(8,128)S(1)}, bf16[144,3584]{1,0:T(8,128)(2,1)S(1)}, f32[2,32,128]{2,1,0:T(8,128)S(1)}) custom-call(bf16[64,7296]{1,0:T(8,128)(2,1)S(1)} %collective-permute-done.3.refs_0_, bf16[64,7296]{1,0:T(8,128)(2,1)S(1)} %collective-permute-done.2.refs_1_, bf16[1792,512]{1,0:T(8,128)(2,1)S(1)} %bitcast.20, ...), custom_call_target="tpu_custom_call" | custom-call | tf_op jit(solution)/shard_map/expert_early/pallas_call | solution.py:434
  78.7 0.0 collective-permute-done.10.refs_1_
  78.8 4.6 %collective-permute-done.9.refs_1_.refs_11_ = bf16[1792,512]{1,0:T(8,128)(2,1)S(1)} collective-permute-done((bf16[1792,512]{1,0:T(8,128)(2,1)S(1)}, bf16[1792,512]{1,0:T(8,128)(2,1)S(1)}, u32[]{:S(2)}, u32[]{:S(2)}) %collective-permute-start.9) | collective-permute-done | bytes 1835040 | tf_op jit(solution)/shard_map/ppermute | solution.py:540
  83.4 0.0 collective-permute-start.11
  83.4 3.8 %collective-permute-start.14 = (bf16[64,1152]{1,0:T(8,128)(2,1)S(1)}, bf16[64,1152]{1,0:T(8,128)(2,1)S(1)}, u32[]{:S(2)}, u32[]{:S(2)}) collective-permute-start(bf16[64,1152]{1,0:T(8,128)(2,1)S(1)} %get-tuple-element.68), channel_id=1, source_target_pairs={{0,12},{2,14},{4,8},{6,10},{8,4},{10,6},{12,0},{14,2},{1,13},{3,15... | collective-permute-start | bytes 442376 | tf_op jit(solution)/shard_map/ppermute | solution.py:540
  87.2 0.4 expert_middle.1.refs_9_
  87.6 0.0 collective-permute-done.11.refs_4_.refs_12_
  87.6 1.9 %expert_late.1 = (bf16[32,7296]{1,0:T(8,128)(2,1)S(1)}, bf16[32,7296]{1,0:T(8,128)(2,1)S(1)}) custom-call(bf16[1792,512]{1,0:T(8,128)(2,1)S(1)} %collective-permute-done.1.refs_4_.refs_0_.refs_5_, bf16[640,512]{1,0:T(8,128)(2,1)S(1)} %collective-permute-done.4.refs_5_.refs_1_.refs_6_, bf16[640,512]{1,0:T(8,128)(2,1)S(1)} %collective-permute-done.5.refs_6_.refs_2_.refs_7_, ...), custom_call_target="tpu_custom_call" | custom-call | flops 1056964608 | bytes 11468800 | tf_op jit(solution)/shard_map/expert_late/pallas_call | solution.py:400
  89.5 2.3 %collective-permute-start.12 = (bf16[32,7296]{1,0:T(8,128)(2,1)S(1)}, bf16[32,7296]{1,0:T(8,128)(2,1)S(1)}, u32[]{:S(2)}, u32[]{:S(2)}) collective-permute-start(bf16[32,7296]{1,0:T(8,128)(2,1)S(1)} %get-tuple-element.64), channel_id=1, source_target_pairs={{0,20},{2,22},{4,16},{6,18},{8,28},{10,30},{12,24},{14,26},{16,4},... | collective-permute-start | bytes 1400840 | tf_op jit(solution)/shard_map/ppermute | solution.py:548
  91.8 2.6 %collective-permute-start.13 = (bf16[32,7296]{1,0:T(8,128)(2,1)S(1)}, bf16[32,7296]{1,0:T(8,128)(2,1)S(1)}, u32[]{:S(2)}, u32[]{:S(2)}) collective-permute-start(bf16[32,7296]{1,0:T(8,128)(2,1)S(1)} %get-tuple-element.65), channel_id=1, source_target_pairs={{0,24},{2,26},{4,28},{6,30},{8,16},{10,18},{12,20},{14,22},{16,8},... | collective-permute-start | bytes 1400840 | tf_op jit(solution)/shard_map/ppermute | solution.py:548
  94.3 0.0 collective-permute-done.14.refs_2_
  94.4 7.6 %expert_whole.1 = (bf16[32,7296]{1,0:T(8,128)(2,1)S(1)}, bf16[32,7296]{1,0:T(8,128)(2,1)S(1)}) custom-call(bf16[64,7296]{1,0:T(8,128)(2,1)S(1)} %get-tuple-element.66.refs_0_, bf16[64,6144]{1,0:T(8,128)(2,1)S(1)} %collective-permute-done.10.refs_1_, bf16[64,1152]{1,0:T(8,128)(2,1)S(1)} %collective-permute-done.14.refs_2_, bf16[1792,512]{1,0:T(8,128)(2,1)S(1)} %bitcast.21, ...), custom_call_target="tpu_custom_call" | custom-call | flops 3170893824 | bytes 17776640 | tf_op jit(solution)/shard_map/expert_whole/pallas_call | solution.py:434
  101.9 1.6 %collective-permute-start.15 = (bf16[32,7296]{1,0:T(8,128)(2,1)S(1)}, bf16[32,7296]{1,0:T(8,128)(2,1)S(1)}, u32[]{:S(2)}, u32[]{:S(2)}) collective-permute-start(bf16[32,7296]{1,0:T(8,128)(2,1)S(1)} %get-tuple-element.69), channel_id=1, source_target_pairs={{0,16},{2,18},{4,20},{6,22},{8,24},{10,26},{12,28},{14,30},{16,0},... | collective-permute-start | bytes 1400840 | tf_op jit(solution)/shard_map/ppermute | solution.py:548
  103.5 1.0 collective-permute-start.16
  104.4 8.1 %collective-permute-done.12.refs_0_ = bf16[32,7296]{1,0:T(8,128)(2,1)S(1)} collective-permute-done((bf16[32,7296]{1,0:T(8,128)(2,1)S(1)}, bf16[32,7296]{1,0:T(8,128)(2,1)S(1)}, u32[]{:S(2)}, u32[]{:S(2)}) %collective-permute-start.12) | collective-permute-done | bytes 466976 | tf_op jit(solution)/shard_map/ppermute | solution.py:548
  112.5 14.4 %collective-permute-done.13.refs_1_ = bf16[32,7296]{1,0:T(8,128)(2,1)S(1)} collective-permute-done((bf16[32,7296]{1,0:T(8,128)(2,1)S(1)}, bf16[32,7296]{1,0:T(8,128)(2,1)S(1)}, u32[]{:S(2)}, u32[]{:S(2)}) %collective-permute-start.13) | collective-permute-done | bytes 466976 | tf_op jit(solution)/shard_map/ppermute | solution.py:548
  126.9 1.6 %settle.1.start_ref = f32[128,3584]{1,0:T(8,128)S(1)} custom-call(bf16[128,3584]{1,0:T(8,128)(2,1)S(1)} %collective-permute-done.start_ref, bf16[32,7296]{1,0:T(8,128)(2,1)S(1)} %collective-permute-done.12.refs_0_, bf16[32,7296]{1,0:T(8,128)(2,1)S(1)} %collective-permute-done.13.refs_1_), custom_call_target="tpu_custom_call" | custom-call | flops 132120576 | bytes 3784704 | tf_op jit(solution)/shard_map/settle/pallas_call | solution.py:514
  128.5 4.8 %collective-permute-done.15.refs_0_ = bf16[32,7296]{1,0:T(8,128)(2,1)S(1)} collective-permute-done((bf16[32,7296]{1,0:T(8,128)(2,1)S(1)}, bf16[32,7296]{1,0:T(8,128)(2,1)S(1)}, u32[]{:S(2)}, u32[]{:S(2)}) %collective-permute-start.15) | collective-permute-done | bytes 466976 | tf_op jit(solution)/shard_map/ppermute | solution.py:548
  133.3 0.0 collective-permute-done.16.refs_1_
  133.3 1.7 %finish.1 = bf16[128,3584]{1,0:T(8,128)(2,1)} custom-call(f32[128,3584]{1,0:T(8,128)S(1)} %settle.1.start_ref, bf16[32,7296]{1,0:T(8,128)(2,1)S(1)} %collective-permute-done.15.refs_0_, bf16[32,7296]{1,0:T(8,128)(2,1)S(1)} %collective-permute-done.16.refs_1_), custom_call_target="tpu_custom_call" | custom-call | flops 132120576 | bytes 3784704 | tf_op jit(solution)/shard_map/finish/pallas_call | solution.py:514
  (1 shorter events, 0.0 us)
Async XLA Ops:
  0.0 9.0 %copy-start.5 = (f32[1,128,2]{1,2,0:T(2,128)S(1)}, f32[1,128,2]{1,2,0:T(2,128)}, u32[]{:S(2)}) copy-start(f32[1,128,2]{1,2,0:T(2,128)} %param.9) | copy-start | bytes 3076
  0.0 9.0 %copy-start.4 = (s32[1,128,2]{1,2,0:T(2,128)S(1)}, s32[1,128,2]{1,2,0:T(2,128)}, u32[]{:S(2)}) copy-start(s32[1,128,2]{1,2,0:T(2,128)} %param.8) | copy-start | bytes 3076
  0.0 9.0 %copy-start.1 = (bf16[1,128,3584]{2,1,0:T(8,128)(2,1)S(1)}, bf16[1,128,3584]{2,1,0:T(8,128)(2,1)}, u32[]{:S(2)}) copy-start(bf16[1,128,3584]{2,1,0:T(8,128)(2,1)} %param.7) | copy-start | bytes 2752516
  0.0 9.0 %copy-start = (bf16[1,128,3584]{2,1,0:T(8,128)(2,1)S(1)}, bf16[1,128,3584]{2,1,0:T(8,128)(2,1)}, u32[]{:S(2)}) copy-start(bf16[1,128,3584]{2,1,0:T(8,128)(2,1)} %param.6) | copy-start | bytes 2752516
  0.0 12.9 %collective-permute-start.7 = (bf16[1792,512]{1,0:T(8,128)(2,1)}, bf16[1792,512]{1,0:T(8,128)(2,1)}, u32[]{:S(2)}, u32[]{:S(2)}) collective-permute-start(bf16[1792,512]{1,0:T(8,128)(2,1)} %bitcast.18), channel_id=1, source_target_pairs={{0,2},{2,0},{4,6},{6,4},{8,10},{10,8},{12,14},{14,12},{1,3},{3,1},... | collective-permute-start | bytes 5505032 | tf_op jit(solution)/shard_map/ppermute | solution.py:540
  0.5 13.9 %collective-permute-start.8 = (bf16[1792,512]{1,0:T(8,128)(2,1)}, bf16[1792,512]{1,0:T(8,128)(2,1)}, u32[]{:S(2)}, u32[]{:S(2)}) collective-permute-start(bf16[1792,512]{1,0:T(8,128)(2,1)} %bitcast.22), channel_id=1, source_target_pairs={{0,2},{2,0},{4,6},{6,4},{8,10},{10,8},{12,14},{14,12},{1,3},{3,1},... | collective-permute-start | bytes 5505032 | tf_op jit(solution)/shard_map/ppermute | solution.py:540
  0.6 44.0 %collective-permute-start.1 = (bf16[1792,512]{1,0:T(8,128)(2,1)}, bf16[1792,512]{1,0:T(8,128)(2,1)S(1)}, u32[]{:S(2)}, u32[]{:S(2)}) collective-permute-start(bf16[1792,512]{1,0:T(8,128)(2,1)} %bitcast.19), channel_id=1, source_target_pairs={{0,1},{1,0},{2,3},{3,2},{4,5},{5,4},{6,7},{7,6},{8,9},{9,8},{10,11... | collective-permute-start | bytes 5505032 | tf_op jit(solution)/shard_map/ppermute | solution.py:540
  3.6 10.9 %copy-start.3 = (bf16[1,1,1792,512]{3,2,1,0:T(8,128)(2,1)S(1)}, bf16[1,1,1792,512]{3,2,1,0:T(8,128)(2,1)}, u32[]{:S(2)}) copy-start(bf16[1,1,1792,512]{3,2,1,0:T(8,128)(2,1)} %param.11) | copy-start | bytes 5505028
  6.4 61.7 %collective-permute-start.2 = (bf16[64,7296]{1,0:T(8,128)(2,1)}, bf16[64,7296]{1,0:T(8,128)(2,1)S(1)}, u32[]{:S(2)}, u32[]{:S(2)}) collective-permute-start(bf16[64,7296]{1,0:T(8,128)(2,1)} %dispatch.4), channel_id=1, source_target_pairs={{0,8},{2,10},{4,12},{6,14},{8,0},{10,2},{12,4},{14,6},{1,9},{3,11}... | collective-permute-start | bytes 2801672 | tf_op jit(solution)/shard_map/ppermute | solution.py:540
  11.3 57.9 %collective-permute-start.3 = (bf16[64,7296]{1,0:T(8,128)(2,1)S(1)}, bf16[64,7296]{1,0:T(8,128)(2,1)S(1)}, u32[]{:S(2)}, u32[]{:S(2)}) collective-permute-start(bf16[64,7296]{1,0:T(8,128)(2,1)S(1)} %get-tuple-element.42), channel_id=1, source_target_pairs={{0,4},{2,6},{4,0},{6,2},{8,12},{10,14},{12,8},{14,10},{1,5},{3,7},... | collective-permute-start | bytes 2801672 | tf_op jit(solution)/shard_map/ppermute | solution.py:540
  12.9 21.5 %collective-permute-start = (bf16[128,3584]{1,0:T(8,128)(2,1)S(1)}, bf16[128,3584]{1,0:T(8,128)(2,1)S(1)}, u32[]{:S(2)}, u32[]{:S(2)}) collective-permute-start(bf16[128,3584]{1,0:T(8,128)(2,1)S(1)} %bitcast.16), channel_id=1, source_target_pairs={{0,16},{16,0},{1,17},{17,1},{2,18},{18,2},{3,19},{19,3},{4,20},{20... | collective-permute-start | bytes 2752520 | tf_op jit(solution)/shard_map/ppermute | solution.py:540
  14.4 68.9 %collective-permute-start.9 = (bf16[1792,512]{1,0:T(8,128)(2,1)S(1)}, bf16[1792,512]{1,0:T(8,128)(2,1)S(1)}, u32[]{:S(2)}, u32[]{:S(2)}) collective-permute-start(bf16[1792,512]{1,0:T(8,128)(2,1)S(1)} %bitcast.23), channel_id=1, source_target_pairs={{0,1},{1,0},{2,3},{3,2},{4,5},{5,4},{6,7},{7,6},{8,9},{9,8},{10,11... | collective-permute-start | bytes 5505032 | tf_op jit(solution)/shard_map/ppermute | solution.py:540
  44.6 34.2 %collective-permute-start.10 = (bf16[64,6144]{1,0:T(8,128)(2,1)S(1)}, bf16[64,6144]{1,0:T(8,128)(2,1)S(1)}, u32[]{:S(2)}, u32[]{:S(2)}) collective-permute-start(bf16[64,6144]{1,0:T(8,128)(2,1)S(1)} %get-tuple-element.46), channel_id=1, source_target_pairs={{0,12},{2,14},{4,8},{6,10},{8,4},{10,6},{12,0},{14,2},{1,13},{3,15... | collective-permute-start | bytes 2359304 | tf_op jit(solution)/shard_map/ppermute | solution.py:540
  69.2 4.0 %copy-start.2 = (bf16[1,1,1792,512]{3,2,1,0:T(8,128)(2,1)S(1)}, bf16[1,1,1792,512]{3,2,1,0:T(8,128)(2,1)}, u32[]{:S(2)}) copy-start(bf16[1,1,1792,512]{3,2,1,0:T(8,128)(2,1)} %param.10) | copy-start | bytes 5505028
  69.3 3.9 %collective-permute-start.5 = (bf16[640,512]{1,0:T(8,128)(2,1)S(1)}, bf16[640,512]{1,0:T(8,128)(2,1)S(1)}, u32[]{:S(2)}, u32[]{:S(2)}) collective-permute-start(bf16[640,512]{1,0:T(8,128)(2,1)S(1)} %get-tuple-element.71), channel_id=1, source_target_pairs={{0,2},{2,0},{4,6},{6,4},{8,10},{10,8},{12,14},{14,12},{1,3},{3,1},... | collective-permute-start | bytes 1966088 | tf_op jit(solution)/shard_map/ppermute | solution.py:540
  69.4 3.8 %collective-permute-start.4 = (bf16[640,512]{1,0:T(8,128)(2,1)S(1)}, bf16[640,512]{1,0:T(8,128)(2,1)S(1)}, u32[]{:S(2)}, u32[]{:S(2)}) collective-permute-start(bf16[640,512]{1,0:T(8,128)(2,1)S(1)} %get-tuple-element.72), channel_id=1, source_target_pairs={{0,2},{2,0},{4,6},{6,4},{8,10},{10,8},{12,14},{14,12},{1,3},{3,1},... | collective-permute-start | bytes 1966088 | tf_op jit(solution)/shard_map/ppermute | solution.py:540
  69.9 3.2 %collective-permute-start.6 = (bf16[512,512]{1,0:T(8,128)(2,1)S(1)}, bf16[512,512]{1,0:T(8,128)(2,1)S(1)}, u32[]{:S(2)}, u32[]{:S(2)}) collective-permute-start(bf16[512,512]{1,0:T(8,128)(2,1)S(1)} %slice.11), channel_id=1, source_target_pairs={{0,2},{2,0},{4,6},{6,4},{8,10},{10,8},{12,14},{14,12},{1,3},{3,1},... | collective-permute-start | bytes 1572872 | tf_op jit(solution)/shard_map/ppermute | solution.py:540
  83.4 4.3 %collective-permute-start.11 = (bf16[1792,512]{1,0:T(8,128)(2,1)S(1)}, bf16[1792,512]{1,0:T(8,128)(2,1)S(1)}, u32[]{:S(2)}, u32[]{:S(2)}) collective-permute-start(bf16[1792,512]{1,0:T(8,128)(2,1)S(1)} %collective-permute-done.9.refs_1_.refs_11_), channel_id=1, source_target_pairs={{0,2},{2,0},{4,6},{6,4},{8,10},{10,8},{12,14},{14,12},{1,3},{3,1},... | collective-permute-start | bytes 5505032 | tf_op jit(solution)/shard_map/ppermute | solution.py:540
  83.4 11.0 %collective-permute-start.14 = (bf16[64,1152]{1,0:T(8,128)(2,1)S(1)}, bf16[64,1152]{1,0:T(8,128)(2,1)S(1)}, u32[]{:S(2)}, u32[]{:S(2)}) collective-permute-start(bf16[64,1152]{1,0:T(8,128)(2,1)S(1)} %get-tuple-element.68), channel_id=1, source_target_pairs={{0,12},{2,14},{4,8},{6,10},{8,4},{10,6},{12,0},{14,2},{1,13},{3,15... | collective-permute-start | bytes 442376 | tf_op jit(solution)/shard_map/ppermute | solution.py:540
  89.5 23.0 %collective-permute-start.12 = (bf16[32,7296]{1,0:T(8,128)(2,1)S(1)}, bf16[32,7296]{1,0:T(8,128)(2,1)S(1)}, u32[]{:S(2)}, u32[]{:S(2)}) collective-permute-start(bf16[32,7296]{1,0:T(8,128)(2,1)S(1)} %get-tuple-element.64), channel_id=1, source_target_pairs={{0,20},{2,22},{4,16},{6,18},{8,28},{10,30},{12,24},{14,26},{16,4},... | collective-permute-start | bytes 1400840 | tf_op jit(solution)/shard_map/ppermute | solution.py:548
  91.8 35.1 %collective-permute-start.13 = (bf16[32,7296]{1,0:T(8,128)(2,1)S(1)}, bf16[32,7296]{1,0:T(8,128)(2,1)S(1)}, u32[]{:S(2)}, u32[]{:S(2)}) collective-permute-start(bf16[32,7296]{1,0:T(8,128)(2,1)S(1)} %get-tuple-element.65), channel_id=1, source_target_pairs={{0,24},{2,26},{4,28},{6,30},{8,16},{10,18},{12,20},{14,22},{16,8},... | collective-permute-start | bytes 1400840 | tf_op jit(solution)/shard_map/ppermute | solution.py:548
  101.9 31.4 %collective-permute-start.15 = (bf16[32,7296]{1,0:T(8,128)(2,1)S(1)}, bf16[32,7296]{1,0:T(8,128)(2,1)S(1)}, u32[]{:S(2)}, u32[]{:S(2)}) collective-permute-start(bf16[32,7296]{1,0:T(8,128)(2,1)S(1)} %get-tuple-element.69), channel_id=1, source_target_pairs={{0,16},{2,18},{4,20},{6,22},{8,24},{10,26},{12,28},{14,30},{16,0},... | collective-permute-start | bytes 1400840 | tf_op jit(solution)/shard_map/ppermute | solution.py:548
  103.5 29.8 %collective-permute-start.16 = (bf16[32,7296]{1,0:T(8,128)(2,1)S(1)}, bf16[32,7296]{1,0:T(8,128)(2,1)S(1)}, u32[]{:S(2)}, u32[]{:S(2)}) collective-permute-start(bf16[32,7296]{1,0:T(8,128)(2,1)S(1)} %get-tuple-element.70), channel_id=1, source_target_pairs={{0,28},{2,30},{4,24},{6,26},{8,20},{10,22},{12,16},{14,18},{16,12}... | collective-permute-start | bytes 1400840 | tf_op jit(solution)/shard_map/ppermute | solution.py:548

commit v8 on v7

--- a/solution.py
+++ b/solution.py
@@ -14,6 +14,7 @@
 MIB = 1 << 20
 CHUNK = 512
 PARTS = 1
+PIECES = 2
 LIMIT = 57
 TAIL = 8
 CUTS = 3
@@ -217,7 +218,7 @@
 def put_extra(rows, row32, ext, n, base, first):
     row32[...] = jnp.zeros_like(row32)
     for i in range(n):
-        unfold(row32, i, ext[i].astype(F32), rows.shape[1] // LANES, first, ext.shape[1])
+        unfold(row32, i, ext[i].astype(F32), rows.shape[1] // LANES, first, ext[i].shape[0])
     rows[n * base :, :] = row32[...].astype(BF16)
 
 
@@ -462,21 +463,17 @@
 
 
 def add_kernel(n, base, extra, start_ref, *refs):
-    msgs, (out_hbm, out, rows, ext, row32, places, sem_b, sem_e, sem_o) = refs[:n], refs[n:]
+    msgs, (out_hbm, out, rows, row32, places, sem_b, sem_o) = refs[:n], refs[n:]
     tokens, width = start_ref.shape
     pieces = width // LANES
     part, sides = msgs[0].shape[0], sides_of(base)
-    ext_in = [
-        begin(msg.at[:, pl.ds(sides * width, ext.shape[2])], ext.at[i], sem_e.at[i])
-        for i, msg in enumerate(msgs)
-    ]
     rows_in = []
     for i, msg in enumerate(msgs):
         for side in range(sides):
             src = msg.at[:, pl.ds(side * width, width)]
             dst = rows.at[pl.ds(i * base + side * part, part), :]
             rows_in.append(begin(src, dst, sem_b.at[i, side]))
-    finish(ext_in)
+    ext = [msg[:, sides * width :] for msg in msgs]
     folded = jnp.zeros((tokens, 16), F32)
     at, column = place_of(pieces * extra, part)
     for i in range(n):
@@ -492,9 +489,9 @@
         put_extra(rows, row32, ext, n, base, 0)
     place = places[...]
     finish(rows_in)
-    step = width // 4
+    step = width // PIECES
     sent = []
-    for h in range(4):
+    for h in range(PIECES):
         for at in range(h * step, (h + 1) * step, TILE):
             cols = slice(at, min(at + TILE, (h + 1) * step))
             back = jnp.dot(place, rows[:, cols], preferred_element_type=F32)
@@ -508,23 +505,20 @@
     tokens, width = start.shape
     n = len(msgs)
     slots = n * base + 16 * extra
-    part, cols = msgs[0].shape
     sides = sides_of(base)
     anywhere, vmem = pl.BlockSpec(memory_space=pl.ANY), pl.BlockSpec(memory_space=pltpu.VMEM)
     return pl.pallas_call(
         functools.partial(add_kernel, n, base, extra),
         out_shape=jax.ShapeDtypeStruct((tokens, width), kind),
-        in_specs=[vmem] + [anywhere] * n,
+        in_specs=[vmem] * (1 + n),
         out_specs=anywhere,
         scratch_shapes=[
             pltpu.VMEM((tokens, width), kind),
             pltpu.VMEM((slots, width), BF16),
-            pltpu.VMEM((n, part, cols - sides * width), BF16),
             pltpu.VMEM((16, width), F32),
             pltpu.VMEM((tokens, slots), BF16),
             pltpu.SemaphoreType.DMA((n, sides)),
-            pltpu.SemaphoreType.DMA((n,)),
-            pltpu.SemaphoreType.DMA((4,)),
+            pltpu.SemaphoreType.DMA((PIECES,)),
         ],
         compiler_params=pltpu.CompilerParams(vmem_limit_bytes=24 * MIB),
         cost_estimate=pl.CostEstimate(
@@ -583,7 +577,7 @@
     other_grad = swap(grad, "section", 1)
     v_late, w_other, v_other = after(v_own, w_other, v_other)
     v_far = [swap(v_late, "dp", apart) for apart in others]
-    sent[-1], other_grad, w_far = after(sent[-1], other_grad, w_far)
+    sent[-1], other_grad = after(sent[-1], other_grad)
     got = {}
     for group, msgs in zip(sends, sent):
         for dist, msg in zip(group, msgs):

time: 136 us -> 136 us (level)
  waiting for transfers between devices: 83.6 us -> 87.9 us
  starting transfers between devices: 25.9 us -> 22 us
    ppermute x13, waiting for transfers between devices: 56.3 us -> 60.3 us  [swap(): lax.ppermute(value, axis, [(i, i ^ apart) for i in range(lax.axis_size(ax...]
    ppermute x13, starting transfers between devices: 18.5 us -> 14.6 us  [swap(): lax.ppermute(value, axis, [(i, i ^ apart) for i in range(lax.axis_size(ax...]
  transfers between devices with their start and end apart: 17 -> 17, of which waited for: 9 -> 8; matrix products, arithmetic and copies ran while one was open for 0% -> 0% of each run, Pallas kernels for 17% -> 17%
where the time goes in v8:
time: 136 us; the launch traced here: 135 us
  waiting for transfers between devices  87.9 us (65%)
  Pallas kernels  24.8 us (18%)
  starting transfers between devices  22 us (16%)
    ppermute x13, waiting for transfers between devices, swap(): lax.ppermute(value, axis, [(i, i ^ apart) for i in range(lax.axis_size(ax...  60.3 us
    ppermute x4, waiting for transfers between devices, swap_back(): return lax.ppermute(value, ('section', 'expert'), pairs)  27.7 us
    ppermute x13, starting transfers between devices, swap(): lax.ppermute(value, axis, [(i, i ^ apart) for i in range(lax.axis_size(ax...  14.6 us
    pallas_call x2, Pallas kernels, expert(): pl.pallas_call(functools.partial(expert_kernel, n, base, extra, stage, w_...  13.1 us
    ppermute x4, starting transfers between devices, swap_back(): return lax.ppermute(value, ('section', 'expert'), pairs)  7.35 us
    pallas_call x3, Pallas kernels, dispatch(): pl.pallas_call(functools.partial(dispatch_kernel, dists, base, extra, spl...  6.52 us
    pallas_call x2, Pallas kernels, add_returned(): pl.pallas_call(functools.partial(add_kernel, n, base, extra), out_shape=j...  2.86 us
  transfers between devices with their start and end apart: 17, of which 8 were waited for; matrix products, arithmetic and copies ran while one was open for 0% of the time, Pallas kernels for 17%

profile of v8, /device:TPU:0, one launch (start us, length us, event | category | flops | bytes accessed | tf_op | source)
XLA Modules:
  0.0 135.1 jit_solution(8960842107402680951)
XLA Ops:
  0.0 0.0 copy-start.5
  0.0 0.0 copy-start.4
  0.0 0.0 copy-start.1
  0.0 0.0 copy-start
  0.0 0.5 collective-permute-start.7
  0.5 0.1 collective-permute-start.8
  0.6 2.9 %collective-permute-start.1 = (bf16[1792,512]{1,0:T(8,128)(2,1)}, bf16[1792,512]{1,0:T(8,128)(2,1)S(1)}, u32[]{:S(2)}, u32[]{:S(2)}) collective-permute-start(bf16[1792,512]{1,0:T(8,128)(2,1)} %bitcast.19), channel_id=1, source_target_pairs={{0,1},{1,0},{2,3},{3,2},{4,5},{5,4},{6,7},{7,6},{8,9},{9,8},{10,11... | collective-permute-start | bytes 5505032 | tf_op jit(solution)/shard_map/ppermute | solution.py:534
  3.6 0.0 copy-start.3
  3.6 2.8 %dispatch.4 = bf16[64,7296]{1,0:T(8,128)(2,1)} custom-call(s32[2,128]{1,0:T(2,128)} %bitcast.26, f32[2,128]{1,0:T(2,128)} %bitcast.29, bf16[128,3584]{1,0:T(8,128)(2,1)} %bitcast.11, bf16[128,3584]{1,0:T(8,128)(2,1)} %bitcast.14), custom_call_target="tpu_custom_call" | custom-call | flops 146800640 | bytes 2768896 | tf_op jit(solution)/shard_map/dispatch/pallas_call | solution.py:151
  6.4 2.7 %collective-permute-start.2 = (bf16[64,7296]{1,0:T(8,128)(2,1)}, bf16[64,7296]{1,0:T(8,128)(2,1)S(1)}, u32[]{:S(2)}, u32[]{:S(2)}) collective-permute-start(bf16[64,7296]{1,0:T(8,128)(2,1)} %dispatch.4), channel_id=1, source_target_pairs={{0,8},{2,10},{4,12},{6,14},{8,0},{10,2},{12,4},{14,6},{1,9},{3,11}... | collective-permute-start | bytes 2801672 | tf_op jit(solution)/shard_map/ppermute | solution.py:534
  9.0 0.0 copy-done.5
  9.0 0.0 copy-done.4
  9.0 0.0 copy-done.1
  9.0 0.0 copy-done
  9.0 2.2 %dispatch.5 = (bf16[64,7296]{1,0:T(8,128)(2,1)S(1)}, bf16[64,7296]{1,0:T(8,128)(2,1)S(1)}) custom-call(s32[2,128]{1,0:T(2,128)S(1)} %bitcast.27, f32[2,128]{1,0:T(2,128)S(1)} %bitcast.30, bf16[128,3584]{1,0:T(8,128)(2,1)S(1)} %bitcast.12, bf16[128,3584]{1,0:T(8,128)(2,1)S(1)} %bitcast.15), custom_call_target="tpu_custom_call" | custom-call | flops 293601280 | bytes 3702784 | tf_op jit(solution)/shard_map/dispatch/pallas_call | solution.py:151
  11.3 1.7 %collective-permute-start.3 = (bf16[64,7296]{1,0:T(8,128)(2,1)S(1)}, bf16[64,7296]{1,0:T(8,128)(2,1)S(1)}, u32[]{:S(2)}, u32[]{:S(2)}) collective-permute-start(bf16[64,7296]{1,0:T(8,128)(2,1)S(1)} %get-tuple-element.40), channel_id=1, source_target_pairs={{0,4},{2,6},{4,0},{6,2},{8,12},{10,14},{12,8},{14,10},{1,5},{3,7},... | collective-permute-start | bytes 2801672 | tf_op jit(solution)/shard_map/ppermute | solution.py:534
  12.9 0.0 collective-permute-done.7.refs_3_.refs_4_
  12.9 1.5 %collective-permute-start = (bf16[128,3584]{1,0:T(8,128)(2,1)S(1)}, bf16[128,3584]{1,0:T(8,128)(2,1)S(1)}, u32[]{:S(2)}, u32[]{:S(2)}) collective-permute-start(bf16[128,3584]{1,0:T(8,128)(2,1)S(1)} %bitcast.16), channel_id=1, source_target_pairs={{0,16},{16,0},{1,17},{17,1},{2,18},{18,2},{3,19},{19,3},{4,20},{20... | collective-permute-start | bytes 2752520 | tf_op jit(solution)/shard_map/ppermute | solution.py:534
  14.4 0.0 collective-permute-done.8.refs_9_.refs_10_
  14.4 0.0 copy-done.3
  14.4 0.5 collective-permute-start.9
  14.9 1.5 %dispatch.3 = (bf16[64,6144]{1,0:T(8,128)(2,1)S(1)}, bf16[64,1152]{1,0:T(8,128)(2,1)S(1)}) custom-call(s32[2,128]{1,0:T(2,128)S(1)} %bitcast.28, f32[2,128]{1,0:T(2,128)S(1)} %bitcast.31, bf16[128,3584]{1,0:T(8,128)(2,1)S(1)} %bitcast.13, bf16[128,3584]{1,0:T(8,128)(2,1)S(1)} %bitcast.17), custom_call_target="tpu_custom_call" | custom-call | flops 146800640 | bytes 2768896 | tf_op jit(solution)/shard_map/dispatch/pallas_call | solution.py:151
  16.4 18.0 %collective-permute-done.start_ref = bf16[128,3584]{1,0:T(8,128)(2,1)S(1)} collective-permute-done((bf16[128,3584]{1,0:T(8,128)(2,1)S(1)}, bf16[128,3584]{1,0:T(8,128)(2,1)S(1)}, u32[]{:S(2)}, u32[]{:S(2)}) %collective-permute-start) | collective-permute-done | bytes 917536 | tf_op jit(solution)/shard_map/ppermute | solution.py:534
  34.4 0.2 collective-permute-start.10
  34.6 33.4 %collective-permute-done.2.refs_1_ = bf16[64,7296]{1,0:T(8,128)(2,1)S(1)} collective-permute-done((bf16[64,7296]{1,0:T(8,128)(2,1)}, bf16[64,7296]{1,0:T(8,128)(2,1)S(1)}, u32[]{:S(2)}, u32[]{:S(2)}) %collective-permute-start.2) | collective-permute-done | bytes 933920 | tf_op jit(solution)/shard_map/ppermute | solution.py:534
  68.0 1.2 collective-permute-done.3.refs_0_
  69.2 0.0 collective-permute-done.1.refs_4_.refs_0_.refs_5_
  69.2 0.0 copy-start.2
  69.2 0.1 fusion
  69.3 0.1 collective-permute-start.5
  69.4 0.5 collective-permute-start.4
  69.9 0.1 collective-permute-start.6
  70.1 3.1 %collective-permute-done.6.refs_7_.refs_3_.refs_8_ = bf16[512,512]{1,0:T(8,128)(2,1)S(1)} collective-permute-done((bf16[512,512]{1,0:T(8,128)(2,1)S(1)}, bf16[512,512]{1,0:T(8,128)(2,1)S(1)}, u32[]{:S(2)}, u32[]{:S(2)}) %collective-permute-start.6) | collective-permute-done | bytes 524320 | tf_op jit(solution)/shard_map/ppermute | solution.py:534
  73.2 0.0 collective-permute-done.5.refs_6_.refs_2_.refs_7_
  73.2 0.0 collective-permute-done.4.refs_5_.refs_1_.refs_6_
  73.2 0.0 copy-done.2
  73.2 5.6 %expert_early.1 = (f32[144,512]{1,0:T(8,128)S(1)}, f32[144,3584]{1,0:T(8,128)S(1)}, bf16[144,3584]{1,0:T(8,128)(2,1)S(1)}, f32[2,32,128]{2,1,0:T(8,128)S(1)}) custom-call(bf16[64,7296]{1,0:T(8,128)(2,1)S(1)} %collective-permute-done.3.refs_0_, bf16[64,7296]{1,0:T(8,128)(2,1)S(1)} %collective-permute-done.2.refs_1_, bf16[1792,512]{1,0:T(8,128)(2,1)S(1)} %bitcast.20, ...), custom_call_target="tpu_custom_call" | custom-call | tf_op jit(solution)/shard_map/expert_early/pallas_call | solution.py:435
  78.7 0.0 collective-permute-done.10.refs_1_
  78.8 4.6 %collective-permute-done.9.refs_1_.refs_11_ = bf16[1792,512]{1,0:T(8,128)(2,1)S(1)} collective-permute-done((bf16[1792,512]{1,0:T(8,128)(2,1)S(1)}, bf16[1792,512]{1,0:T(8,128)(2,1)S(1)}, u32[]{:S(2)}, u32[]{:S(2)}) %collective-permute-start.9) | collective-permute-done | bytes 1835040 | tf_op jit(solution)/shard_map/ppermute | solution.py:534
  83.4 0.0 collective-permute-start.11
  83.4 3.8 %collective-permute-start.14 = (bf16[64,1152]{1,0:T(8,128)(2,1)S(1)}, bf16[64,1152]{1,0:T(8,128)(2,1)S(1)}, u32[]{:S(2)}, u32[]{:S(2)}) collective-permute-start(bf16[64,1152]{1,0:T(8,128)(2,1)S(1)} %get-tuple-element.66), channel_id=1, source_target_pairs={{0,12},{2,14},{4,8},{6,10},{8,4},{10,6},{12,0},{14,2},{1,13},{3,15... | collective-permute-start | bytes 442376 | tf_op jit(solution)/shard_map/ppermute | solution.py:534
  87.2 0.4 expert_middle.1.refs_9_
  87.6 0.0 collective-permute-done.11.refs_4_.refs_12_
  87.6 1.9 %expert_late.1 = (bf16[32,7296]{1,0:T(8,128)(2,1)S(1)}, bf16[32,7296]{1,0:T(8,128)(2,1)S(1)}) custom-call(bf16[1792,512]{1,0:T(8,128)(2,1)S(1)} %collective-permute-done.1.refs_4_.refs_0_.refs_5_, bf16[640,512]{1,0:T(8,128)(2,1)S(1)} %collective-permute-done.4.refs_5_.refs_1_.refs_6_, bf16[640,512]{1,0:T(8,128)(2,1)S(1)} %collective-permute-done.5.refs_6_.refs_2_.refs_7_, ...), custom_call_target="tpu_custom_call" | custom-call | flops 1056964608 | bytes 11468800 | tf_op jit(solution)/shard_map/expert_late/pallas_call | solution.py:401
  89.5 2.3 %collective-permute-start.12 = (bf16[32,7296]{1,0:T(8,128)(2,1)S(1)}, bf16[32,7296]{1,0:T(8,128)(2,1)S(1)}, u32[]{:S(2)}, u32[]{:S(2)}) collective-permute-start(bf16[32,7296]{1,0:T(8,128)(2,1)S(1)} %get-tuple-element.62), channel_id=1, source_target_pairs={{0,20},{2,22},{4,16},{6,18},{8,28},{10,30},{12,24},{14,26},{16,4},... | collective-permute-start | bytes 1400840 | tf_op jit(solution)/shard_map/ppermute | solution.py:542
  91.8 2.6 %collective-permute-start.13 = (bf16[32,7296]{1,0:T(8,128)(2,1)S(1)}, bf16[32,7296]{1,0:T(8,128)(2,1)S(1)}, u32[]{:S(2)}, u32[]{:S(2)}) collective-permute-start(bf16[32,7296]{1,0:T(8,128)(2,1)S(1)} %get-tuple-element.63), channel_id=1, source_target_pairs={{0,24},{2,26},{4,28},{6,30},{8,16},{10,18},{12,20},{14,22},{16,8},... | collective-permute-start | bytes 1400840 | tf_op jit(solution)/shard_map/ppermute | solution.py:542
  94.3 0.0 collective-permute-done.14.refs_2_
  94.4 7.6 %expert_whole.1 = (bf16[32,7296]{1,0:T(8,128)(2,1)S(1)}, bf16[32,7296]{1,0:T(8,128)(2,1)S(1)}) custom-call(bf16[64,7296]{1,0:T(8,128)(2,1)S(1)} %get-tuple-element.64.refs_0_, bf16[64,6144]{1,0:T(8,128)(2,1)S(1)} %collective-permute-done.10.refs_1_, bf16[64,1152]{1,0:T(8,128)(2,1)S(1)} %collective-permute-done.14.refs_2_, bf16[1792,512]{1,0:T(8,128)(2,1)S(1)} %bitcast.21, ...), custom_call_target="tpu_custom_call" | custom-call | flops 3170893824 | bytes 17776640 | tf_op jit(solution)/shard_map/expert_whole/pallas_call | solution.py:435
  101.9 1.6 %collective-permute-start.15 = (bf16[32,7296]{1,0:T(8,128)(2,1)S(1)}, bf16[32,7296]{1,0:T(8,128)(2,1)S(1)}, u32[]{:S(2)}, u32[]{:S(2)}) collective-permute-start(bf16[32,7296]{1,0:T(8,128)(2,1)S(1)} %get-tuple-element.67), channel_id=1, source_target_pairs={{0,16},{2,18},{4,20},{6,22},{8,24},{10,26},{12,28},{14,30},{16,0},... | collective-permute-start | bytes 1400840 | tf_op jit(solution)/shard_map/ppermute | solution.py:542
  103.5 1.0 collective-permute-start.16
  104.4 8.1 %collective-permute-done.12.refs_0_ = bf16[32,7296]{1,0:T(8,128)(2,1)S(1)} collective-permute-done((bf16[32,7296]{1,0:T(8,128)(2,1)S(1)}, bf16[32,7296]{1,0:T(8,128)(2,1)S(1)}, u32[]{:S(2)}, u32[]{:S(2)}) %collective-permute-start.12) | collective-permute-done | bytes 466976 | tf_op jit(solution)/shard_map/ppermute | solution.py:542
  112.5 14.4 %collective-permute-done.13.refs_1_ = bf16[32,7296]{1,0:T(8,128)(2,1)S(1)} collective-permute-done((bf16[32,7296]{1,0:T(8,128)(2,1)S(1)}, bf16[32,7296]{1,0:T(8,128)(2,1)S(1)}, u32[]{:S(2)}, u32[]{:S(2)}) %collective-permute-start.13) | collective-permute-done | bytes 466976 | tf_op jit(solution)/shard_map/ppermute | solution.py:542
  126.9 1.2 settle.1.start_ref
  128.1 5.2 %collective-permute-done.15.refs_0_ = bf16[32,7296]{1,0:T(8,128)(2,1)S(1)} collective-permute-done((bf16[32,7296]{1,0:T(8,128)(2,1)S(1)}, bf16[32,7296]{1,0:T(8,128)(2,1)S(1)}, u32[]{:S(2)}, u32[]{:S(2)}) %collective-permute-start.15) | collective-permute-done | bytes 466976 | tf_op jit(solution)/shard_map/ppermute | solution.py:542
  133.3 0.0 collective-permute-done.16.refs_1_
  133.3 1.7 %finish.1 = bf16[128,3584]{1,0:T(8,128)(2,1)} custom-call(f32[128,3584]{1,0:T(8,128)S(1)} %settle.1.start_ref, bf16[32,7296]{1,0:T(8,128)(2,1)S(1)} %collective-permute-done.15.refs_0_, bf16[32,7296]{1,0:T(8,128)(2,1)S(1)} %collective-permute-done.16.refs_1_), custom_call_target="tpu_custom_call" | custom-call | flops 132120576 | bytes 3784704 | tf_op jit(solution)/shard_map/finish/pallas_call | solution.py:510
  (1 shorter events, 0.0 us)
Async XLA Ops:
  0.0 9.0 %copy-start.5 = (f32[1,128,2]{1,2,0:T(2,128)S(1)}, f32[1,128,2]{1,2,0:T(2,128)}, u32[]{:S(2)}) copy-start(f32[1,128,2]{1,2,0:T(2,128)} %param.9) | copy-start | bytes 3076
  0.0 9.0 %copy-start.4 = (s32[1,128,2]{1,2,0:T(2,128)S(1)}, s32[1,128,2]{1,2,0:T(2,128)}, u32[]{:S(2)}) copy-start(s32[1,128,2]{1,2,0:T(2,128)} %param.8) | copy-start | bytes 3076
  0.0 9.0 %copy-start.1 = (bf16[1,128,3584]{2,1,0:T(8,128)(2,1)S(1)}, bf16[1,128,3584]{2,1,0:T(8,128)(2,1)}, u32[]{:S(2)}) copy-start(bf16[1,128,3584]{2,1,0:T(8,128)(2,1)} %param.7) | copy-start | bytes 2752516
  0.0 9.0 %copy-start = (bf16[1,128,3584]{2,1,0:T(8,128)(2,1)S(1)}, bf16[1,128,3584]{2,1,0:T(8,128)(2,1)}, u32[]{:S(2)}) copy-start(bf16[1,128,3584]{2,1,0:T(8,128)(2,1)} %param.6) | copy-start | bytes 2752516
  0.0 12.9 %collective-permute-start.7 = (bf16[1792,512]{1,0:T(8,128)(2,1)}, bf16[1792,512]{1,0:T(8,128)(2,1)}, u32[]{:S(2)}, u32[]{:S(2)}) collective-permute-start(bf16[1792,512]{1,0:T(8,128)(2,1)} %bitcast.18), channel_id=1, source_target_pairs={{0,2},{2,0},{4,6},{6,4},{8,10},{10,8},{12,14},{14,12},{1,3},{3,1},... | collective-permute-start | bytes 5505032 | tf_op jit(solution)/shard_map/ppermute | solution.py:534
  0.5 13.9 %collective-permute-start.8 = (bf16[1792,512]{1,0:T(8,128)(2,1)}, bf16[1792,512]{1,0:T(8,128)(2,1)}, u32[]{:S(2)}, u32[]{:S(2)}) collective-permute-start(bf16[1792,512]{1,0:T(8,128)(2,1)} %bitcast.22), channel_id=1, source_target_pairs={{0,2},{2,0},{4,6},{6,4},{8,10},{10,8},{12,14},{14,12},{1,3},{3,1},... | collective-permute-start | bytes 5505032 | tf_op jit(solution)/shard_map/ppermute | solution.py:534
  0.6 68.6 %collective-permute-start.1 = (bf16[1792,512]{1,0:T(8,128)(2,1)}, bf16[1792,512]{1,0:T(8,128)(2,1)S(1)}, u32[]{:S(2)}, u32[]{:S(2)}) collective-permute-start(bf16[1792,512]{1,0:T(8,128)(2,1)} %bitcast.19), channel_id=1, source_target_pairs={{0,1},{1,0},{2,3},{3,2},{4,5},{5,4},{6,7},{7,6},{8,9},{9,8},{10,11... | collective-permute-start | bytes 5505032 | tf_op jit(solution)/shard_map/ppermute | solution.py:534
  3.6 10.9 %copy-start.3 = (bf16[1,1,1792,512]{3,2,1,0:T(8,128)(2,1)S(1)}, bf16[1,1,1792,512]{3,2,1,0:T(8,128)(2,1)}, u32[]{:S(2)}) copy-start(bf16[1,1,1792,512]{3,2,1,0:T(8,128)(2,1)} %param.11) | copy-start | bytes 5505028
  6.4 61.7 %collective-permute-start.2 = (bf16[64,7296]{1,0:T(8,128)(2,1)}, bf16[64,7296]{1,0:T(8,128)(2,1)S(1)}, u32[]{:S(2)}, u32[]{:S(2)}) collective-permute-start(bf16[64,7296]{1,0:T(8,128)(2,1)} %dispatch.4), channel_id=1, source_target_pairs={{0,8},{2,10},{4,12},{6,14},{8,0},{10,2},{12,4},{14,6},{1,9},{3,11}... | collective-permute-start | bytes 2801672 | tf_op jit(solution)/shard_map/ppermute | solution.py:534
  11.3 57.9 %collective-permute-start.3 = (bf16[64,7296]{1,0:T(8,128)(2,1)S(1)}, bf16[64,7296]{1,0:T(8,128)(2,1)S(1)}, u32[]{:S(2)}, u32[]{:S(2)}) collective-permute-start(bf16[64,7296]{1,0:T(8,128)(2,1)S(1)} %get-tuple-element.40), channel_id=1, source_target_pairs={{0,4},{2,6},{4,0},{6,2},{8,12},{10,14},{12,8},{14,10},{1,5},{3,7},... | collective-permute-start | bytes 2801672 | tf_op jit(solution)/shard_map/ppermute | solution.py:534
  12.9 21.5 %collective-permute-start = (bf16[128,3584]{1,0:T(8,128)(2,1)S(1)}, bf16[128,3584]{1,0:T(8,128)(2,1)S(1)}, u32[]{:S(2)}, u32[]{:S(2)}) collective-permute-start(bf16[128,3584]{1,0:T(8,128)(2,1)S(1)} %bitcast.16), channel_id=1, source_target_pairs={{0,16},{16,0},{1,17},{17,1},{2,18},{18,2},{3,19},{19,3},{4,20},{20... | collective-permute-start | bytes 2752520 | tf_op jit(solution)/shard_map/ppermute | solution.py:534
  14.4 68.9 %collective-permute-start.9 = (bf16[1792,512]{1,0:T(8,128)(2,1)S(1)}, bf16[1792,512]{1,0:T(8,128)(2,1)S(1)}, u32[]{:S(2)}, u32[]{:S(2)}) collective-permute-start(bf16[1792,512]{1,0:T(8,128)(2,1)S(1)} %bitcast.23), channel_id=1, source_target_pairs={{0,1},{1,0},{2,3},{3,2},{4,5},{5,4},{6,7},{7,6},{8,9},{9,8},{10,11... | collective-permute-start | bytes 5505032 | tf_op jit(solution)/shard_map/ppermute | solution.py:534
  34.4 44.3 %collective-permute-start.10 = (bf16[64,6144]{1,0:T(8,128)(2,1)S(1)}, bf16[64,6144]{1,0:T(8,128)(2,1)S(1)}, u32[]{:S(2)}, u32[]{:S(2)}) collective-permute-start(bf16[64,6144]{1,0:T(8,128)(2,1)S(1)} %get-tuple-element.44), channel_id=1, source_target_pairs={{0,12},{2,14},{4,8},{6,10},{8,4},{10,6},{12,0},{14,2},{1,13},{3,15... | collective-permute-start | bytes 2359304 | tf_op jit(solution)/shard_map/ppermute | solution.py:534
  69.2 4.0 %copy-start.2 = (bf16[1,1,1792,512]{3,2,1,0:T(8,128)(2,1)S(1)}, bf16[1,1,1792,512]{3,2,1,0:T(8,128)(2,1)}, u32[]{:S(2)}) copy-start(bf16[1,1,1792,512]{3,2,1,0:T(8,128)(2,1)} %param.10) | copy-start | bytes 5505028
  69.3 3.9 %collective-permute-start.5 = (bf16[640,512]{1,0:T(8,128)(2,1)S(1)}, bf16[640,512]{1,0:T(8,128)(2,1)S(1)}, u32[]{:S(2)}, u32[]{:S(2)}) collective-permute-start(bf16[640,512]{1,0:T(8,128)(2,1)S(1)} %get-tuple-element.69), channel_id=1, source_target_pairs={{0,2},{2,0},{4,6},{6,4},{8,10},{10,8},{12,14},{14,12},{1,3},{3,1},... | collective-permute-start | bytes 1966088 | tf_op jit(solution)/shard_map/ppermute | solution.py:534
  69.4 3.8 %collective-permute-start.4 = (bf16[640,512]{1,0:T(8,128)(2,1)S(1)}, bf16[640,512]{1,0:T(8,128)(2,1)S(1)}, u32[]{:S(2)}, u32[]{:S(2)}) collective-permute-start(bf16[640,512]{1,0:T(8,128)(2,1)S(1)} %get-tuple-element.70), channel_id=1, source_target_pairs={{0,2},{2,0},{4,6},{6,4},{8,10},{10,8},{12,14},{14,12},{1,3},{3,1},... | collective-permute-start | bytes 1966088 | tf_op jit(solution)/shard_map/ppermute | solution.py:534
  69.9 3.2 %collective-permute-start.6 = (bf16[512,512]{1,0:T(8,128)(2,1)S(1)}, bf16[512,512]{1,0:T(8,128)(2,1)S(1)}, u32[]{:S(2)}, u32[]{:S(2)}) collective-permute-start(bf16[512,512]{1,0:T(8,128)(2,1)S(1)} %slice.11), channel_id=1, source_target_pairs={{0,2},{2,0},{4,6},{6,4},{8,10},{10,8},{12,14},{14,12},{1,3},{3,1},... | collective-permute-start | bytes 1572872 | tf_op jit(solution)/shard_map/ppermute | solution.py:534
  83.4 4.3 %collective-permute-start.11 = (bf16[1792,512]{1,0:T(8,128)(2,1)S(1)}, bf16[1792,512]{1,0:T(8,128)(2,1)S(1)}, u32[]{:S(2)}, u32[]{:S(2)}) collective-permute-start(bf16[1792,512]{1,0:T(8,128)(2,1)S(1)} %collective-permute-done.9.refs_1_.refs_11_), channel_id=1, source_target_pairs={{0,2},{2,0},{4,6},{6,4},{8,10},{10,8},{12,14},{14,12},{1,3},{3,1},... | collective-permute-start | bytes 5505032 | tf_op jit(solution)/shard_map/ppermute | solution.py:534
  83.4 11.0 %collective-permute-start.14 = (bf16[64,1152]{1,0:T(8,128)(2,1)S(1)}, bf16[64,1152]{1,0:T(8,128)(2,1)S(1)}, u32[]{:S(2)}, u32[]{:S(2)}) collective-permute-start(bf16[64,1152]{1,0:T(8,128)(2,1)S(1)} %get-tuple-element.66), channel_id=1, source_target_pairs={{0,12},{2,14},{4,8},{6,10},{8,4},{10,6},{12,0},{14,2},{1,13},{3,15... | collective-permute-start | bytes 442376 | tf_op jit(solution)/shard_map/ppermute | solution.py:534
  89.5 23.0 %collective-permute-start.12 = (bf16[32,7296]{1,0:T(8,128)(2,1)S(1)}, bf16[32,7296]{1,0:T(8,128)(2,1)S(1)}, u32[]{:S(2)}, u32[]{:S(2)}) collective-permute-start(bf16[32,7296]{1,0:T(8,128)(2,1)S(1)} %get-tuple-element.62), channel_id=1, source_target_pairs={{0,20},{2,22},{4,16},{6,18},{8,28},{10,30},{12,24},{14,26},{16,4},... | collective-permute-start | bytes 1400840 | tf_op jit(solution)/shard_map/ppermute | solution.py:542
  91.8 35.1 %collective-permute-start.13 = (bf16[32,7296]{1,0:T(8,128)(2,1)S(1)}, bf16[32,7296]{1,0:T(8,128)(2,1)S(1)}, u32[]{:S(2)}, u32[]{:S(2)}) collective-permute-start(bf16[32,7296]{1,0:T(8,128)(2,1)S(1)} %get-tuple-element.63), channel_id=1, source_target_pairs={{0,24},{2,26},{4,28},{6,30},{8,16},{10,18},{12,20},{14,22},{16,8},... | collective-permute-start | bytes 1400840 | tf_op jit(solution)/shard_map/ppermute | solution.py:542
  101.9 31.4 %collective-permute-start.15 = (bf16[32,7296]{1,0:T(8,128)(2,1)S(1)}, bf16[32,7296]{1,0:T(8,128)(2,1)S(1)}, u32[]{:S(2)}, u32[]{:S(2)}) collective-permute-start(bf16[32,7296]{1,0:T(8,128)(2,1)S(1)} %get-tuple-element.67), channel_id=1, source_target_pairs={{0,16},{2,18},{4,20},{6,22},{8,24},{10,26},{12,28},{14,30},{16,0},... | collective-permute-start | bytes 1400840 | tf_op jit(solution)/shard_map/ppermute | solution.py:542
  103.5 29.8 %collective-permute-start.16 = (bf16[32,7296]{1,0:T(8,128)(2,1)S(1)}, bf16[32,7296]{1,0:T(8,128)(2,1)S(1)}, u32[]{:S(2)}, u32[]{:S(2)}) collective-permute-start(bf16[32,7296]{1,0:T(8,128)(2,1)S(1)} %get-tuple-element.68), channel_id=1, source_target_pairs={{0,28},{2,30},{4,24},{6,26},{8,20},{10,22},{12,16},{14,18},{16,12}... | collective-permute-start | bytes 1400840 | tf_op jit(solution)/shard_map/ppermute | solution.py:542
